TPU v7x, 32 devices: a whole 2x2x4 slice. The times are simulated.
32 devices in a mesh: fsdp: 32 (over z, y, x, core).
Axes of the slice: x: 2, y: 2, z: 4, core: 2. Of those that a mesh axis runs over, the one named last changes fastest.
Arguments:
- activations: bfloat16 [4096, 768], P('fsdp'), may hold values from -6 to 6
- query_weight: bfloat16 [2, 768, 768], P(None, 'fsdp'), may hold values from -0.21875 to 0.21875
- query_bias: bfloat16 [2, 768], P(None, 'fsdp'), may hold values from -4 to 4
- key_weight: bfloat16 [2, 768, 768], P(None, 'fsdp'), may hold values from -0.21875 to 0.21875
- value_weight: bfloat16 [2, 768, 768], P(None, 'fsdp'), may hold values from -0.21875 to 0.21875
- value_bias: bfloat16 [2, 768], P(None, 'fsdp'), may hold values from -0.4375 to 0.4375
- output_weight: bfloat16 [2, 768, 768], P(None, 'fsdp'), may hold values from -3.5 to 3.5
- output_bias: bfloat16 [2, 768], P(None, 'fsdp'), may hold values from -4 to 4
- first_gain: bfloat16 [2, 768], P(None, 'fsdp'), may hold values from 0.5 to 1.5
- first_shift: bfloat16 [2, 768], P(None, 'fsdp'), may hold values from -4 to 4
- inner_weight: bfloat16 [2, 768, 3072], P(None, 'fsdp'), may hold values from -0.21875 to 0.21875
- inner_bias: bfloat16 [2, 3072], P(None, 'fsdp'), may hold values from -4 to 4
- outer_weight: bfloat16 [2, 3072, 768], P(None, 'fsdp'), may hold values from -0.109375 to 0.109375
- outer_bias: bfloat16 [2, 768], P(None, 'fsdp'), may hold values from -4 to 4
- second_gain: bfloat16 [2, 768], P(None, 'fsdp'), may hold values from 0.5 to 1.5
- second_shift: bfloat16 [2, 768], P(None, 'fsdp'), may hold values from -4 to 4
- cotangent: bfloat16 [4096, 768], P('fsdp'), may hold values from -6 to 6
- parents: int32 [13], replicated, may hold values from 0 to 12, as said below
- segments: int32 [4096], P('fsdp'), may hold values from 0 to 12, as said below
Outputs:
- result: bfloat16 [4096, 768], P('fsdp')
- input_grad: bfloat16 [4096, 768], P('fsdp')
- query_weight_grad: float32 [2, 768, 768], P(None, 'fsdp')
- query_bias_grad: float32 [2, 768], P(None, 'fsdp')
- key_weight_grad: float32 [2, 768, 768], P(None, 'fsdp')
- value_weight_grad: float32 [2, 768, 768], P(None, 'fsdp')
- value_bias_grad: float32 [2, 768], P(None, 'fsdp')
- output_weight_grad: float32 [2, 768, 768], P(None, 'fsdp')
- output_bias_grad: float32 [2, 768], P(None, 'fsdp')
- first_gain_grad: float32 [2, 768], P(None, 'fsdp')
- first_shift_grad: float32 [2, 768], P(None, 'fsdp')
- inner_weight_grad: float32 [2, 768, 3072], P(None, 'fsdp')
- inner_bias_grad: float32 [2, 3072], P(None, 'fsdp')
- outer_weight_grad: float32 [2, 3072, 768], P(None, 'fsdp')
- outer_bias_grad: float32 [2, 768], P(None, 'fsdp')
- second_gain_grad: float32 [2, 768], P(None, 'fsdp')
- second_shift_grad: float32 [2, 768], P(None, 'fsdp')
Inputs may be any that keep to these rules, and one draw needn't show every extreme that they name: `parents`: every tree is one trunk, four branches whose parent is the trunk, and eight leaves, two with each branch as parent; a trunk is its own parent. Segment numbers are spread over the trees in a drawn order. `segments`: tree t fills tokens t * 4096 to (t + 1) * 4096 - 1: its trunk's 1024 tokens first, then its twelve branches and leaves, 256 tokens each, in an order drawn per tree.
All inputs are finite; a program needn't handle non-finite values.
Results may differ from a plain program's by a relative error of at most 0.023.
Values may be sent and summed in bfloat16 or wider, within the bound.
A program may use at most 256 MiB of HBM per device.

v0:
```python
import jax
import jax.numpy as jnp
from jax import lax
from jax.sharding import PartitionSpec as P

HEADS = 12
HEAD_DIM = 64
LAYERS = 2
TREE_LEN = 4096


EPSILON = 1e-06
MASKED = -1000000000.0


def partner_2(shard, axis, stride):
    return lax.ppermute(shard, axis, [(i, i ^ 1 << stride) for i in range(lax.axis_size(axis))])


def as_sent(shard):
    return jax.tree.map(lambda a: a.astype(jnp.bfloat16) if a.dtype == jnp.float32 else a, shard)


def product(a, b):
    return jnp.dot(a, b, preferred_element_type=jnp.float32)


def product_tn(a, b):
    return lax.dot_general(a, b, (((0,), (0,)), ((), ())), preferred_element_type=jnp.float32)


def product_nt(a, b):
    return lax.dot_general(a, b, (((1,), (1,)), ((), ())), preferred_element_type=jnp.float32)


def exact_gelu(u):
    return jax.nn.gelu(u, approximate=False)


def layer_norm(z, gain_vec, shift_vec):
    centre = z - jnp.mean(z, axis=-1, keepdims=True)
    scaled = centre * lax.rsqrt(jnp.mean(centre * centre, axis=-1, keepdims=True) + EPSILON)
    return scaled * gain_vec.astype(jnp.float32) + shift_vec.astype(jnp.float32)


def norm_backward(z, gain_vec, upstream):
    centre = z - jnp.mean(z, axis=-1, keepdims=True)
    invert = lax.rsqrt(jnp.mean(centre * centre, axis=-1, keepdims=True) + EPSILON)
    scaled = centre * invert
    weighted = upstream * gain_vec.astype(jnp.float32)
    inner = invert * (
        weighted
        - jnp.mean(weighted, axis=-1, keepdims=True)
        - scaled * jnp.mean(weighted * scaled, axis=-1, keepdims=True)
    )
    return (inner, jnp.sum(upstream * scaled, axis=0), jnp.sum(upstream, axis=0))


def lookup_rows(ids, parents):
    table = jnp.arange(parents.shape[0], dtype=jnp.int32)
    return jnp.sum(jnp.where(ids[:, None] == table[None, :], parents[None, :], 0), axis=1)


def join_heads(stacked):
    return stacked.transpose(1, 0, 2).reshape(stacked.shape[1], -1)


def gather_group(key_rows, value_rows, labels, position, bit_count):
    for b in range(bit_count):
        partner = partner_2((key_rows, value_rows, labels), "fsdp", b)
        upper_side = position >> b & 1 == 1
        key_rows = jnp.where(
            upper_side,
            jnp.concatenate([partner[0], key_rows]),
            jnp.concatenate([key_rows, partner[0]]),
        )
        value_rows = jnp.where(
            upper_side,
            jnp.concatenate([partner[1], value_rows]),
            jnp.concatenate([value_rows, partner[1]]),
        )
        labels = jnp.where(
            upper_side, jnp.concatenate([partner[2], labels]), jnp.concatenate([labels, partner[2]])
        )
    return (key_rows, value_rows, labels)


def sum_group(key_grad, value_grad, position, bit_count):
    for b in reversed(range(bit_count)):
        halfway = key_grad.shape[0] // 2
        upper_side = position >> b & 1 == 1
        outgoing = (
            jnp.where(upper_side, key_grad[:halfway], key_grad[halfway:]),
            jnp.where(upper_side, value_grad[:halfway], value_grad[halfway:]),
        )
        partner = partner_2((as_sent(outgoing[0]), as_sent(outgoing[1])), "fsdp", b)
        key_grad = jnp.where(upper_side, key_grad[halfway:], key_grad[:halfway]) + partner[0]
        value_grad = jnp.where(upper_side, value_grad[halfway:], value_grad[:halfway]) + partner[1]
    return (key_grad, value_grad)


def attend_forward(queries, key_rows, value_rows, allowed):
    factor = HEAD_DIM ** (-0.5)

    def one_head(j):
        start = j * HEAD_DIM
        q = lax.dynamic_slice_in_dim(queries, start, HEAD_DIM, 1)
        k = lax.dynamic_slice_in_dim(key_rows, start, HEAD_DIM, 1)
        v = lax.dynamic_slice_in_dim(value_rows, start, HEAD_DIM, 1)
        s = jnp.where(allowed, product_nt(q, k) * factor, MASKED)
        maxima = jnp.max(s, axis=1, keepdims=True)
        e = jnp.exp(s - maxima)
        totals = jnp.sum(e, axis=1, keepdims=True)
        p = (e / totals).astype(jnp.bfloat16)
        return (product(p, v), (maxima + jnp.log(totals))[:, 0])

    stacked, log_total = lax.map(one_head, jnp.arange(HEADS))
    return (join_heads(stacked), log_total)


def attend_backward(queries, key_rows, value_rows, allowed, log_total, grad_context):
    factor = HEAD_DIM ** (-0.5)

    def one_head(j):
        start = j * HEAD_DIM
        q = lax.dynamic_slice_in_dim(queries, start, HEAD_DIM, 1)
        k = lax.dynamic_slice_in_dim(key_rows, start, HEAD_DIM, 1)
        v = lax.dynamic_slice_in_dim(value_rows, start, HEAD_DIM, 1)
        g = lax.dynamic_slice_in_dim(grad_context, start, HEAD_DIM, 1)
        s = jnp.where(allowed, product_nt(q, k) * factor, MASKED)
        p = jnp.where(allowed, jnp.exp(s - log_total[j][:, None]), 0.0)
        grad_p = product_nt(g, v)
        grad_v = product_tn(p.astype(jnp.bfloat16), g)
        grad_s = (p * (grad_p - jnp.sum(p * grad_p, axis=1, keepdims=True))).astype(jnp.bfloat16)
        grad_q = product(grad_s, k) * factor
        grad_k = product_tn(grad_s, q) * factor
        return (grad_q, grad_k, grad_v)

    grad_q, grad_k, grad_v = lax.map(one_head, jnp.arange(HEADS))
    return (join_heads(grad_q), join_heads(grad_k), join_heads(grad_v))


def layer_forward(state, full, segments, parent_one, parent_two, position, bit_count):
    (
        q_weight,
        q_bias,
        k_weight,
        v_weight,
        v_bias,
        o_weight,
        o_bias,
        gain_one,
        shift_one,
        up_weight,
        up_bias,
        down_weight,
        down_bias,
        gain_two,
        shift_two,
    ) = full
    inputs = state.astype(jnp.bfloat16)
    queries = (product(inputs, q_weight) + q_bias).astype(jnp.bfloat16)
    key_local = product(inputs, k_weight).astype(jnp.bfloat16)
    value_local = (product(inputs, v_weight) + v_bias).astype(jnp.bfloat16)
    key_rows, value_rows, labels = gather_group(
        key_local, value_local, segments, position, bit_count
    )
    allowed = (
        (labels[None, :] == segments[:, None])
        | (labels[None, :] == parent_one[:, None])
        | (labels[None, :] == parent_two[:, None])
    )
    context_wide, log_total = attend_forward(queries, key_rows, value_rows, allowed)
    context = context_wide.astype(jnp.bfloat16)
    first_sum = state + product(context, o_weight) + o_bias
    hidden = layer_norm(first_sum, gain_one, shift_one)
    hidden_low = hidden.astype(jnp.bfloat16)
    pre_act = product(hidden_low, up_weight) + up_bias
    gelu_out = exact_gelu(pre_act).astype(jnp.bfloat16)
    second_sum = hidden + product(gelu_out, down_weight) + down_bias
    record = (
        inputs,
        queries,
        key_rows,
        value_rows,
        allowed,
        log_total,
        context,
        first_sum,
        hidden_low,
        pre_act,
        gelu_out,
        second_sum,
    )
    return (record, layer_norm(second_sum, gain_two, shift_two))


def layer_backward(upstream, full, record, position, bit_count):
    (
        q_weight,
        q_bias,
        k_weight,
        v_weight,
        v_bias,
        o_weight,
        o_bias,
        gain_one,
        shift_one,
        up_weight,
        up_bias,
        down_weight,
        down_bias,
        gain_two,
        shift_two,
    ) = full
    (
        inputs,
        queries,
        key_rows,
        value_rows,
        allowed,
        log_total,
        context,
        first_sum,
        hidden_low,
        pre_act,
        gelu_out,
        second_sum,
    ) = record
    grad_z2, grad_gain_two, grad_shift_two = norm_backward(second_sum, gain_two, upstream)
    grad_f = grad_z2.astype(jnp.bfloat16)
    grad_down_bias = jnp.sum(grad_f.astype(jnp.float32), axis=0)
    grad_down = product_tn(gelu_out, grad_f)
    grad_gelu = product_nt(grad_f, down_weight)
    unused_value, gelu_back = jax.vjp(exact_gelu, pre_act)
    grad_u = gelu_back(grad_gelu)[0].astype(jnp.bfloat16)
    grad_up_bias = jnp.sum(grad_u.astype(jnp.float32), axis=0)
    grad_up = product_tn(hidden_low, grad_u)
    grad_h = grad_z2 + product_nt(grad_u, up_weight)
    grad_z1, grad_gain_one, grad_shift_one = norm_backward(first_sum, gain_one, grad_h)
    grad_a = grad_z1.astype(jnp.bfloat16)
    grad_o_bias = jnp.sum(grad_a.astype(jnp.float32), axis=0)
    grad_o = product_tn(context, grad_a)
    grad_context = product_nt(grad_a, o_weight).astype(jnp.bfloat16)
    grad_q, key_grad, value_grad = attend_backward(
        queries, key_rows, value_rows, allowed, log_total, grad_context
    )
    key_grad, value_grad = sum_group(key_grad, value_grad, position, bit_count)
    q_low = grad_q.astype(jnp.bfloat16)
    k_low = key_grad.astype(jnp.bfloat16)
    v_low = value_grad.astype(jnp.bfloat16)
    grad_x = (
        grad_z1
        + product_nt(q_low, q_weight)
        + product_nt(k_low, k_weight)
        + product_nt(v_low, v_weight)
    )
    terms = (
        product_tn(inputs, q_low),
        jnp.sum(q_low.astype(jnp.float32), axis=0),
        product_tn(inputs, k_low),
        product_tn(inputs, v_low),
        jnp.sum(v_low.astype(jnp.float32), axis=0),
        grad_o,
        grad_o_bias,
        grad_gain_one,
        grad_shift_one,
        grad_up,
        grad_up_bias,
        grad_down,
        grad_down_bias,
        grad_gain_two,
        grad_shift_two,
    )
    return (grad_x, terms)


def stack_layers(groups, n):
    return jnp.stack([g[n] for g in groups])


def body(
    activations,
    query_weight,
    query_bias,
    key_weight,
    value_weight,
    value_bias,
    output_weight,
    output_bias,
    first_gain,
    first_shift,
    inner_weight,
    inner_bias,
    outer_weight,
    outer_bias,
    second_gain,
    second_shift,
    cotangent,
    parents,
    segments,
):
    position = lax.axis_index("fsdp")
    bit_count = (TREE_LEN // activations.shape[0]).bit_length() - 1
    parent_one = lookup_rows(segments, parents)
    parent_two = lookup_rows(parent_one, parents)
    state = activations.astype(jnp.float32)
    saved = []
    kept_weights = []
    for i in range(LAYERS):
        full = (
            lax.all_gather(query_weight[i], "fsdp", axis=0, tiled=True),
            lax.all_gather(query_bias[i], "fsdp", axis=0, tiled=True),
            lax.all_gather(key_weight[i], "fsdp", axis=0, tiled=True),
            lax.all_gather(value_weight[i], "fsdp", axis=0, tiled=True),
            lax.all_gather(value_bias[i], "fsdp", axis=0, tiled=True),
            lax.all_gather(output_weight[i], "fsdp", axis=0, tiled=True),
            lax.all_gather(output_bias[i], "fsdp", axis=0, tiled=True),
            lax.all_gather(first_gain[i], "fsdp", axis=0, tiled=True),
            lax.all_gather(first_shift[i], "fsdp", axis=0, tiled=True),
            lax.all_gather(inner_weight[i], "fsdp", axis=0, tiled=True),
            lax.all_gather(inner_bias[i], "fsdp", axis=0, tiled=True),
            lax.all_gather(outer_weight[i], "fsdp", axis=0, tiled=True),
            lax.all_gather(outer_bias[i], "fsdp", axis=0, tiled=True),
            lax.all_gather(second_gain[i], "fsdp", axis=0, tiled=True),
            lax.all_gather(second_shift[i], "fsdp", axis=0, tiled=True),
        )
        kept_weights.append(full)
        record, state = layer_forward(
            state, full, segments, parent_one, parent_two, position, bit_count
        )
        saved.append(record)
    outcome = state.astype(jnp.bfloat16)
    upstream = cotangent.astype(jnp.float32)
    layer_grads = [None] * LAYERS
    for i in reversed(range(LAYERS)):
        full = (
            lax.all_gather(query_weight[i], "fsdp", axis=0, tiled=True),
            lax.all_gather(query_bias[i], "fsdp", axis=0, tiled=True),
            lax.all_gather(key_weight[i], "fsdp", axis=0, tiled=True),
            lax.all_gather(value_weight[i], "fsdp", axis=0, tiled=True),
            lax.all_gather(value_bias[i], "fsdp", axis=0, tiled=True),
            lax.all_gather(output_weight[i], "fsdp", axis=0, tiled=True),
            lax.all_gather(output_bias[i], "fsdp", axis=0, tiled=True),
            lax.all_gather(first_gain[i], "fsdp", axis=0, tiled=True),
            lax.all_gather(first_shift[i], "fsdp", axis=0, tiled=True),
            lax.all_gather(inner_weight[i], "fsdp", axis=0, tiled=True),
            lax.all_gather(inner_bias[i], "fsdp", axis=0, tiled=True),
            lax.all_gather(outer_weight[i], "fsdp", axis=0, tiled=True),
            lax.all_gather(outer_bias[i], "fsdp", axis=0, tiled=True),
            lax.all_gather(second_gain[i], "fsdp", axis=0, tiled=True),
            lax.all_gather(second_shift[i], "fsdp", axis=0, tiled=True),
        )
        upstream, terms = layer_backward(upstream, full, saved[i], position, bit_count)
        layer_grads[i] = (
            lax.psum_scatter(terms[0], "fsdp", scatter_dimension=0, tiled=True),
            lax.psum_scatter(terms[1], "fsdp", scatter_dimension=0, tiled=True),
            lax.psum_scatter(terms[2], "fsdp", scatter_dimension=0, tiled=True),
            lax.psum_scatter(terms[3], "fsdp", scatter_dimension=0, tiled=True),
            lax.psum_scatter(terms[4], "fsdp", scatter_dimension=0, tiled=True),
            lax.psum_scatter(terms[5], "fsdp", scatter_dimension=0, tiled=True),
            lax.psum_scatter(terms[6], "fsdp", scatter_dimension=0, tiled=True),
            lax.psum_scatter(terms[7], "fsdp", scatter_dimension=0, tiled=True),
            lax.psum_scatter(terms[8], "fsdp", scatter_dimension=0, tiled=True),
            lax.psum_scatter(terms[9], "fsdp", scatter_dimension=0, tiled=True),
            lax.psum_scatter(terms[10], "fsdp", scatter_dimension=0, tiled=True),
            lax.psum_scatter(terms[11], "fsdp", scatter_dimension=0, tiled=True),
            lax.psum_scatter(terms[12], "fsdp", scatter_dimension=0, tiled=True),
            lax.psum_scatter(terms[13], "fsdp", scatter_dimension=0, tiled=True),
            lax.psum_scatter(terms[14], "fsdp", scatter_dimension=0, tiled=True),
        )
    shares = tuple((stack_layers(layer_grads, n) for n in range(15)))
    return (outcome, upstream.astype(jnp.bfloat16)) + tuple(shares)


def solution(mesh):
    placed = (
        P("fsdp", None),
        P(None, "fsdp", None),
        P(None, "fsdp"),
        P(None, "fsdp", None),
        P(None, "fsdp", None),
        P(None, "fsdp"),
        P(None, "fsdp", None),
        P(None, "fsdp"),
        P(None, "fsdp"),
        P(None, "fsdp"),
        P(None, "fsdp", None),
        P(None, "fsdp"),
        P(None, "fsdp", None),
        P(None, "fsdp"),
        P(None, "fsdp"),
        P(None, "fsdp"),
        P("fsdp", None),
        P(),
        P("fsdp"),
    )
    return jax.shard_map(
        body,
        mesh=mesh,
        in_specs=placed,
        out_specs=(
            P("fsdp", None),
            P("fsdp", None),
            P(None, "fsdp", None),
            P(None, "fsdp"),
            P(None, "fsdp", None),
            P(None, "fsdp", None),
            P(None, "fsdp"),
            P(None, "fsdp", None),
            P(None, "fsdp"),
            P(None, "fsdp"),
            P(None, "fsdp"),
            P(None, "fsdp", None),
            P(None, "fsdp"),
            P(None, "fsdp", None),
            P(None, "fsdp"),
            P(None, "fsdp"),
            P(None, "fsdp"),
        ),
        check_vma=False,
    )
```

profile of v0, /device:TPU:9, one launch (start us, length us, event | category | flops | bytes accessed | tf_op | source)
XLA Modules:
  0.0 3482.4 jit_solution(1874557696325852305)
XLA Ops:
  18.7 47.7 %all-gather.45.cloned.1.call-done = bf16[1,768,768]{2,1,0:T(8,128)(2,1)} async-done(((bf16[1,24,768]{2,1,0:T(8,128)(2,1)}), bf16[1,768,768]{2,1,0:T(8,128)(2,1)}) %all-gather.45.cloned.1.call-update) | async-done | bytes 1179664 | tf_op jit(solution)/shard_map/all_gather | solution.py:314
  74.5 40.6 %all-reduce.37 = (bf16[3072]{0:T(1024)(128)(2,1)}, bf16[3072]{0:T(1024)(128)(2,1)S(1)}, bf16[768]{0:T(1024)(128)(2,1)S(1)}, bf16[768]{0:T(1024)(128)(2,1)S(1)}, ...) all-reduce(bf16[3072]{0:T(1024)(128)(2,1)S(1)} %dynamic-update-slic, ...), channel_id=27, replica_groups=mesh['fsdp'=32] {'fsdp'}, use_global_device_ids=true, to_apply=%add.14 | all-reduce | flops 18432 | bytes 73728
  127.1 9.2 collective-permute-done.11
  147.3 13.9 collective-permute-done.12
  165.9 19.0 collective-permute-done.3
  190.5 57.7 %collective-permute-done.13 = bf16[1024,768]{1,0:T(8,128)(2,1)} collective-permute-done((bf16[1024,768]{1,0:T(8,128)(2,1)}, bf16[1024,768]{1,0:T(8,128)(2,1)}, u32[]{:S(2)}, u32[]{:S(2)}) %collective-permute-start.13) | collective-permute-done | bytes 1572896 | tf_op jit(solution)/shard_map/ppermute | solution.py:17
  264.5 89.8 %collective-permute-done.8 = s32[1024]{0:T(1024)S(1)} collective-permute-done((s32[1024]{0:T(1024)S(1)}, s32[1024]{0:T(1024)S(1)}, u32[]{:S(2)}, u32[]{:S(2)}) %collective-permute-start.8) | collective-permute-done | bytes 4128 | tf_op jit(solution)/shard_map/ppermute | solution.py:17
  357.5 100.5 %collective-permute-done.9 = s32[2048]{0:T(1024)S(1)} collective-permute-done((s32[2048]{0:T(1024)S(1)}, s32[2048]{0:T(1024)S(1)}, u32[]{:S(2)}, u32[]{:S(2)}) %collective-permute-start.9) | collective-permute-done | bytes 8224 | tf_op jit(solution)/shard_map/ppermute | solution.py:17
  460.2 7.6 maximum_select_fusion
  467.8 8.7 maximum_select_fusion.1
  476.7 77.2 %while.56 = (s32[]{:T(128)}, bf16[12,128,64]{1,2,0:T(8,128)(2,1)S(1)}, f32[12,128]{1,0:T(8,128)S(1)}, s32[12]{0:T(128)S(1)}, bf16[128,768]{1,0:T(8,128)(2,1)S(1)...) while((s32[]{:T(128)}, ...), condition=%wide.region_5.6_spmd.clone, body=%wide.region_2.5_spmd.clone.sunk | while | flops 141033344 | bytes 8478427 | solution.py:117
  556.6 8.4 multiply_convert_fusion.3
  565.0 50.5 %all-gather.53.cloned.1.call-done = bf16[1,3072,768]{2,1,0:T(8,128)(2,1)} async-done(((bf16[1,96,768]{2,1,0:T(8,128)(2,1)}), bf16[1,3072,768]{2,1,0:T(8,128)(2,1)}) %all-gather.53.cloned.1.call-update) | async-done | bytes 4718608 | tf_op jit(solution)/shard_map/all_gather | solution.py:323
  619.6 51.0 %all-gather.57.cloned.1.call-done = bf16[1,768,768]{2,1,0:T(8,128)(2,1)} async-done(((bf16[1,24,768]{2,1,0:T(8,128)(2,1)}), bf16[1,768,768]{2,1,0:T(8,128)(2,1)}) %all-gather.57.cloned.1.call-update) | async-done | bytes 1179664 | tf_op jit(solution)/shard_map/all_gather | solution.py:314
  675.0 51.4 %all-gather.59.cloned.1.call-done = bf16[1,768,768]{2,1,0:T(8,128)(2,1)} async-done(((bf16[1,24,768]{2,1,0:T(8,128)(2,1)}), bf16[1,768,768]{2,1,0:T(8,128)(2,1)}) %all-gather.59.cloned.1.call-update) | async-done | bytes 1179664 | tf_op jit(solution)/shard_map/all_gather | solution.py:315
  731.3 9.0 collective-permute-done.21
  749.9 15.4 collective-permute-done.22
  767.2 20.5 collective-permute-done.18
  792.0 59.5 %collective-permute-done.23 = bf16[1024,768]{1,0:T(8,128)(2,1)S(1)} collective-permute-done((bf16[1024,768]{1,0:T(8,128)(2,1)S(1)}, bf16[1024,768]{1,0:T(8,128)(2,1)S(1)}, u32[]{:S(2)}, u32[]{:S(2)}) %collective-permute-start.23) | collective-permute-done | bytes 1572896 | tf_op jit(solution)/shard_map/ppermute | solution.py:17
  858.6 133.8 %collective-permute-done.19 = bf16[2048,768]{1,0:T(8,128)(2,1)} collective-permute-done((bf16[2048,768]{1,0:T(8,128)(2,1)}, bf16[2048,768]{1,0:T(8,128)(2,1)}, u32[]{:S(2)}, u32[]{:S(2)}) %collective-permute-start.19) | collective-permute-done | bytes 3145760 | tf_op jit(solution)/shard_map/ppermute | solution.py:17
  992.4 8.9 maximum_select_fusion.2
  1001.4 58.5 %collective-permute-done.24 = bf16[2048,768]{1,0:T(8,128)(2,1)} collective-permute-done((bf16[2048,768]{1,0:T(8,128)(2,1)}, bf16[2048,768]{1,0:T(8,128)(2,1)}, u32[]{:S(2)}, u32[]{:S(2)}) %collective-permute-start.24) | collective-permute-done | bytes 3145760 | tf_op jit(solution)/shard_map/ppermute | solution.py:17
  1059.8 8.6 maximum_select_fusion.3
  1068.6 76.7 %while.57 = (s32[]{:T(128)}, bf16[12,128,64]{1,2,0:T(8,128)(2,1)S(1)}, f32[12,128]{1,0:T(8,128)S(1)}, s32[12]{0:T(128)S(1)}, bf16[128,768]{1,0:T(8,128)(2,1)S(1)...) while((s32[]{:T(128)}, ...), condition=%wide.region_13.14_spmd.clone, body=%wide.region_10.13_spmd.clone.sunk | while | flops 141033344 | bytes 8478427 | solution.py:117
  1151.4 8.5 multiply_convert_fusion.2
  1159.9 57.3 %all-gather.65.cloned.1.call-done = bf16[1,3072,768]{2,1,0:T(8,128)(2,1)} async-done(((bf16[1,96,768]{2,1,0:T(8,128)(2,1)}), bf16[1,3072,768]{2,1,0:T(8,128)(2,1)}) %all-gather.65.cloned.1.call-update) | async-done | bytes 4718608 | tf_op jit(solution)/shard_map/all_gather | solution.py:323
  1241.9 172.7 %while.58 = (s32[]{:T(128)}, bf16[12,128,64]{1,2,0:T(8,128)(2,1)S(1)}, f32[12,4096,64]{1,2,0:T(8,128)}, f32[12,4096,64]{1,2,0:T(8,128)}, s32[12]{0:T(128)S(1)}, ...) while((s32[]{:T(128)}, ...), condition=%wide.region_24.25_spmd.clone, body=%wide.region_22.24_spmd.clone.sunk | while | flops 343678848 | bytes 21158188 | solution.py:139
  1441.2 183.1 %collective-permute-done.30 = bf16[2048,768]{0,1:T(8,128)(2,1)} collective-permute-done((bf16[2048,768]{0,1:T(8,128)(2,1)}, bf16[2048,768]{0,1:T(8,128)(2,1)}, u32[]{:S(2)}, u32[]{:S(2)}) %collective-permute-start.30) | collective-permute-done | bytes 3145760 | tf_op jit(solution)/shard_map/ppermute | solution.py:17
  1633.1 58.8 %collective-permute-done.25 = bf16[2048,768]{0,1:T(8,128)(2,1)} collective-permute-done((bf16[2048,768]{0,1:T(8,128)(2,1)}, bf16[2048,768]{0,1:T(8,128)(2,1)}, u32[]{:S(2)}, u32[]{:S(2)}) %collective-permute-start.25) | collective-permute-done | bytes 3145760 | tf_op jit(solution)/shard_map/ppermute | solution.py:17
  1702.8 23.5 collective-permute-done.31
  1732.0 34.2 collective-permute-done.26
  1774.9 16.8 collective-permute-done.27
  1794.8 7.4 collective-permute-done.28
  1837.4 172.9 %while.59 = (s32[]{:T(128)}, bf16[12,128,64]{1,2,0:T(8,128)(2,1)S(1)}, f32[12,4096,64]{1,2,0:T(8,128)}, f32[12,4096,64]{1,2,0:T(8,128)}, s32[12]{0:T(128)S(1)}, ...) while((s32[]{:T(128)}, ...), condition=%wide.region_31.32_spmd.clone, body=%wide.region_29.31_spmd.clone.sunk | while | flops 343678848 | bytes 21158188 | solution.py:139
  2035.3 194.7 %collective-permute-done.40 = bf16[2048,768]{0,1:T(8,128)(2,1)} collective-permute-done((bf16[2048,768]{0,1:T(8,128)(2,1)}, bf16[2048,768]{0,1:T(8,128)(2,1)}, u32[]{:S(2)}, u32[]{:S(2)}) %collective-permute-start.40) | collective-permute-done | bytes 3145760 | tf_op jit(solution)/shard_map/ppermute | solution.py:17
  2247.7 88.6 %collective-permute-done.41 = bf16[1024,768]{0,1:T(8,128)(2,1)} collective-permute-done((bf16[1024,768]{0,1:T(8,128)(2,1)}, bf16[1024,768]{0,1:T(8,128)(2,1)}, u32[]{:S(2)}, u32[]{:S(2)}) %collective-permute-start.41) | collective-permute-done | bytes 1572896 | tf_op jit(solution)/shard_map/ppermute | solution.py:17
  2351.0 8.6 collective-permute-done.42
  2372.0 13.5 collective-permute-done.36
  2398.2 19.0 collective-permute-done.37
  2418.7 7.6 collective-permute-done.38
  2466.6 77.0 %reduce-scatter.25.cloned.1.call-done = f32[24,768]{1,0:T(8,128)} async-done(((f32[768,768]{1,0:T(8,128)}), f32[24,768]{1,0:T(8,128)}) %reduce-scatter.25.cloned.1.call-update) | async-done | bytes 73744 | tf_op jit(solution)/shard_map/reduce_scatter | solution.py:361
  2548.6 152.0 %all-reduce.40.cloned.1.call-done = (f32[768]{0:T(1024)}, f32[768]{0:T(1024)}, f32[768]{0:T(1024)}, f32[768]{0:T(1024)}, f32[768]{0:T(1024)}, /*index=5*/f32[768...) async-done(((f32[768]{0:T(1024)}, f32[768]{0:T(1024)}, ...) | async-done | bytes 73744
  2719.2 86.4 %reduce-scatter.45.cloned.1.call-done = f32[24,768]{1,0:T(8,128)} async-done(((f32[768,768]{1,0:T(8,128)}), f32[24,768]{1,0:T(8,128)}) %reduce-scatter.45.cloned.1.call-update) | async-done | bytes 73744
  2806.8 103.0 %reduce-scatter.41.cloned.1.call-done = f32[24,768]{1,0:T(8,128)} async-done(((f32[768,768]{1,0:T(8,128)}), f32[24,768]{1,0:T(8,128)}) %reduce-scatter.41.cloned.1.call-update) | async-done | bytes 73744
  2912.4 137.7 %reduce-scatter.31.cloned.1.call-done = f32[24,3072]{1,0:T(8,128)} async-done(((f32[768,3072]{1,0:T(8,128)}), f32[24,3072]{1,0:T(8,128)}) %reduce-scatter.31.cloned.1.call-update) | async-done | bytes 294928 | tf_op jit(solution)/shard_map/reduce_scatter | solution.py:365
  3050.1 141.5 %reduce-scatter.29.cloned.1.call-done = f32[24,3072]{1,0:T(8,128)} async-done(((f32[768,3072]{1,0:T(8,128)}), f32[24,3072]{1,0:T(8,128)}) %reduce-scatter.29.cloned.1.call-update) | async-done | bytes 294928 | tf_op jit(solution)/shard_map/reduce_scatter | solution.py:365
  3193.5 138.5 %reduce-scatter.35.cloned.1.call-done = f32[96,768]{1,0:T(8,128)} async-done(((f32[3072,768]{1,0:T(8,128)}), f32[96,768]{1,0:T(8,128)}) %reduce-scatter.35.cloned.1.call-update) | async-done | bytes 294928 | tf_op jit(solution)/shard_map/reduce_scatter | solution.py:367
  3332.0 141.5 %reduce-scatter.33.cloned.1.call-done = f32[96,768]{1,0:T(8,128)} async-done(((f32[3072,768]{1,0:T(8,128)}), f32[96,768]{1,0:T(8,128)}) %reduce-scatter.33.cloned.1.call-update) | async-done | bytes 294928 | tf_op jit(solution)/shard_map/reduce_scatter | solution.py:367
  (1001 shorter events, 816.9 us)
Async XLA Ops:
  7.3 59.0 %all-gather.45.cloned.1.call-start = ((), (), s32[]{:S(2)}) async-start(), calls=%async_computation.19 | async-start | bytes 1216512 | tf_op jit(solution)/shard_map/all_gather | solution.py:314
  8.9 113.5 %all-gather.47.cloned.1.call-start = ((), (), s32[]{:S(2)}) async-start(), calls=%async_computation.20 | async-start | bytes 1216512 | tf_op jit(solution)/shard_map/all_gather | solution.py:315
  10.4 448.2 %all-gather.43.cloned.1.call-start = ((), (), s32[]{:S(2)}) async-start(), calls=%async_computation.18 | async-start | bytes 1216512 | tf_op jit(solution)/shard_map/all_gather | solution.py:312
  11.9 542.1 %all-gather.49.cloned.1.call-start = ((), (), s32[]{:S(2)}) async-start(), calls=%async_computation.21 | async-start | bytes 1216512 | tf_op jit(solution)/shard_map/all_gather | solution.py:317
  13.4 543.2 %all-gather.51.cloned.1.call-start = ((), (), s32[]{:S(2)}) async-start(), calls=%async_computation.22 | async-start | bytes 4866048 | tf_op jit(solution)/shard_map/all_gather | solution.py:321
  15.1 600.4 %all-gather.53.cloned.1.call-start = ((), (), s32[]{:S(2)}) async-start(), calls=%async_computation.23 | async-start | bytes 4866048 | tf_op jit(solution)/shard_map/all_gather | solution.py:323
  16.9 653.6 %all-gather.57.cloned.1.call-start = ((), (), s32[]{:S(2)}) async-start(), calls=%async_computation.25 | async-start | bytes 1216512 | tf_op jit(solution)/shard_map/all_gather | solution.py:314
  17.7 708.8 %all-gather.59.cloned.1.call-start = ((), (), s32[]{:S(2)}) async-start(), calls=%async_computation.26 | async-start | bytes 1216512 | tf_op jit(solution)/shard_map/all_gather | solution.py:315
  18.4 838.6 %all-gather.55.cloned.1.call-start = ((), (), s32[]{:S(2)}) async-start(), calls=%async_computation.24 | async-start | bytes 1216512 | tf_op jit(solution)/shard_map/all_gather | solution.py:312
  69.5 54.8 %collective-permute-start.1 = (bf16[256,768]{1,0:T(8,128)(2,1)S(1)}, bf16[256,768]{1,0:T(8,128)(2,1)S(1)}, u32[]{:S(2)}, u32[]{:S(2)}) collective-permute-start(bf16[256,768]{1,0:T(8,128)(2,1)S(1)} %maximum_select_fusion.16), channel_id=1, source_target_pairs={{0,2},{1,3},{2,0},{3,1},{4,6},{5,7},{6,4},{7,5},{8,10},{9,11},{10,... | collective-permute-start | bytes 1179656 | tf_op jit(solution)/shard_map/ppermute | solution.py:17
  127.1 1018.3 %all-gather.61.cloned.1.call-start = ((), (), s32[]{:S(2)}) async-start(), calls=%async_computation.27 | async-start | bytes 1216512 | tf_op jit(solution)/shard_map/all_gather | solution.py:317
  136.7 24.6 collective-permute-start.12
  145.8 39.0 %collective-permute-start.3 = (bf16[1024,768]{1,0:T(8,128)(2,1)S(1)}, bf16[1024,768]{1,0:T(8,128)(2,1)}, u32[]{:S(2)}, u32[]{:S(2)}) collective-permute-start(bf16[1024,768]{1,0:T(8,128)(2,1)S(1)} %maximum_select_fusion.8), channel_id=1, source_target_pairs={{0,8},{1,9},{2,10},{3,11},{4,12},{5,13},{6,14},{7,15},{8,0},{9,1},... | collective-permute-start | bytes 4718600 | tf_op jit(solution)/shard_map/ppermute | solution.py:17
  164.4 83.7 %collective-permute-start.13 = (bf16[1024,768]{1,0:T(8,128)(2,1)}, bf16[1024,768]{1,0:T(8,128)(2,1)}, u32[]{:S(2)}, u32[]{:S(2)}) collective-permute-start(bf16[1024,768]{1,0:T(8,128)(2,1)} %maximum_select_fusion.9), channel_id=1, source_target_pairs={{0,8},{1,9},{2,10},{3,11},{4,12},{5,13},{6,14},{7,15},{8,0},{9,1},... | collective-permute-start | bytes 4718600 | tf_op jit(solution)/shard_map/ppermute | solution.py:17
  188.0 272.2 %collective-permute-start.4 = (bf16[2048,768]{1,0:T(8,128)(2,1)S(1)}, bf16[2048,768]{1,0:T(8,128)(2,1)}, u32[]{:S(2)}, u32[]{:S(2)}) collective-permute-start(bf16[2048,768]{1,0:T(8,128)(2,1)S(1)} %maximum_select_fusion.4), channel_id=1, source_target_pairs={{0,16},{1,17},{2,18},{3,19},{4,20},{5,21},{6,22},{7,23},{8,24},{9,... | collective-permute-start | bytes 9437192 | tf_op jit(solution)/shard_map/ppermute | solution.py:17
  190.4 961.0 %all-gather.63.cloned.1.call-start = ((), (), s32[]{:S(2)}) async-start(), calls=%async_computation.28 | async-start | bytes 4866048 | tf_op jit(solution)/shard_map/all_gather | solution.py:321
  252.5 215.3 %collective-permute-start.14 = (bf16[2048,768]{1,0:T(8,128)(2,1)}, bf16[2048,768]{1,0:T(8,128)(2,1)}, u32[]{:S(2)}, u32[]{:S(2)}) collective-permute-start(bf16[2048,768]{1,0:T(8,128)(2,1)} %maximum_select_fusion.5), channel_id=1, source_target_pairs={{0,16},{1,17},{2,18},{3,19},{4,20},{5,21},{6,22},{7,23},{8,24},{9,... | collective-permute-start | bytes 9437192 | tf_op jit(solution)/shard_map/ppermute | solution.py:17
  262.9 954.4 %all-gather.65.cloned.1.call-start = ((), (), s32[]{:S(2)}) async-start(), calls=%async_computation.29 | async-start | bytes 4866048 | tf_op jit(solution)/shard_map/all_gather | solution.py:323
  264.4 89.9 %collective-permute-start.8 = (s32[1024]{0:T(1024)S(1)}, s32[1024]{0:T(1024)S(1)}, u32[]{:S(2)}, u32[]{:S(2)}) collective-permute-start(s32[1024]{0:T(1024)S(1)} %add_select_fusion.2), channel_id=1, source_target_pairs={{0,8},{1,9},{2,10},{3,11},{4,12},{5,13},{6,14},{7,15},{8,0},{9,1},... | collective-permute-start | bytes 12296 | tf_op jit(solution)/shard_map/ppermute | solution.py:17
  354.3 103.7 %collective-permute-start.9 = (s32[2048]{0:T(1024)S(1)}, s32[2048]{0:T(1024)S(1)}, u32[]{:S(2)}, u32[]{:S(2)}) collective-permute-start(s32[2048]{0:T(1024)S(1)} %add_select_fusion.1), channel_id=1, source_target_pairs={{0,16},{1,17},{2,18},{3,19},{4,20},{5,21},{6,22},{7,23},{8,24},{9,... | collective-permute-start | bytes 24584 | tf_op jit(solution)/shard_map/ppermute | solution.py:17
  673.7 54.6 %collective-permute-start.16 = (bf16[256,768]{1,0:T(8,128)(2,1)S(1)}, bf16[256,768]{1,0:T(8,128)(2,1)S(1)}, u32[]{:S(2)}, u32[]{:S(2)}) collective-permute-start(bf16[256,768]{1,0:T(8,128)(2,1)S(1)} %maximum_select_fusion.18), channel_id=1, source_target_pairs={{0,2},{1,3},{2,0},{3,1},{4,6},{5,7},{6,4},{7,5},{8,10},{9,11},{10,... | collective-permute-start | bytes 1179656 | tf_op jit(solution)/shard_map/ppermute | solution.py:17
  740.6 24.8 collective-permute-start.22
  748.7 39.0 %collective-permute-start.18 = (bf16[1024,768]{1,0:T(8,128)(2,1)S(1)}, bf16[1024,768]{1,0:T(8,128)(2,1)S(1)}, u32[]{:S(2)}, u32[]{:S(2)}) collective-permute-start(bf16[1024,768]{1,0:T(8,128)(2,1)S(1)} %maximum_select_fusion.10), channel_id=1, source_target_pairs={{0,8},{1,9},{2,10},{3,11},{4,12},{5,13},{6,14},{7,15},{8,0},{9,1},... | collective-permute-start | bytes 4718600 | tf_op jit(solution)/shard_map/ppermute | solution.py:17
  766.0 85.5 %collective-permute-start.23 = (bf16[1024,768]{1,0:T(8,128)(2,1)S(1)}, bf16[1024,768]{1,0:T(8,128)(2,1)S(1)}, u32[]{:S(2)}, u32[]{:S(2)}) collective-permute-start(bf16[1024,768]{1,0:T(8,128)(2,1)S(1)} %maximum_select_fusion.11), channel_id=1, source_target_pairs={{0,8},{1,9},{2,10},{3,11},{4,12},{5,13},{6,14},{7,15},{8,0},{9,1},... | collective-permute-start | bytes 4718600 | tf_op jit(solution)/shard_map/ppermute | solution.py:17
  789.9 202.5 %collective-permute-start.19 = (bf16[2048,768]{1,0:T(8,128)(2,1)}, bf16[2048,768]{1,0:T(8,128)(2,1)}, u32[]{:S(2)}, u32[]{:S(2)}) collective-permute-start(bf16[2048,768]{1,0:T(8,128)(2,1)} %maximum_select_fusion.6), channel_id=1, source_target_pairs={{0,16},{1,17},{2,18},{3,19},{4,20},{5,21},{6,22},{7,23},{8,24},{9,... | collective-permute-start | bytes 9437192 | tf_op jit(solution)/shard_map/ppermute | solution.py:17
  853.6 206.2 %collective-permute-start.24 = (bf16[2048,768]{1,0:T(8,128)(2,1)}, bf16[2048,768]{1,0:T(8,128)(2,1)}, u32[]{:S(2)}, u32[]{:S(2)}) collective-permute-start(bf16[2048,768]{1,0:T(8,128)(2,1)} %maximum_select_fusion.7), channel_id=1, source_target_pairs={{0,16},{1,17},{2,18},{3,19},{4,20},{5,21},{6,22},{7,23},{8,24},{9,... | collective-permute-start | bytes 9437192 | tf_op jit(solution)/shard_map/ppermute | solution.py:17
  856.3 1602.1 %reduce-scatter.39.cloned.1.call-start = ((), (), s32[]{:S(2)}) async-start(), calls=%async_computation.31 | async-start | bytes 2433024
  1421.5 202.9 %collective-permute-start.30 = (bf16[2048,768]{0,1:T(8,128)(2,1)}, bf16[2048,768]{0,1:T(8,128)(2,1)}, u32[]{:S(2)}, u32[]{:S(2)}) collective-permute-start(bf16[2048,768]{0,1:T(8,128)(2,1)} %bitcast.41), channel_id=1, source_target_pairs={{0,16},{1,17},{2,18},{3,19},{4,20},{5,21},{6,22},{7,23},{8,24},{9,... | collective-permute-start | bytes 9437192 | tf_op jit(solution)/shard_map/ppermute | solution.py:17
  1429.0 262.9 %collective-permute-start.25 = (bf16[2048,768]{0,1:T(8,128)(2,1)}, bf16[2048,768]{0,1:T(8,128)(2,1)}, u32[]{:S(2)}, u32[]{:S(2)}) collective-permute-start(bf16[2048,768]{0,1:T(8,128)(2,1)} %bitcast.38), channel_id=1, source_target_pairs={{0,16},{1,17},{2,18},{3,19},{4,20},{5,21},{6,22},{7,23},{8,24},{9,... | collective-permute-start | bytes 9437192 | tf_op jit(solution)/shard_map/ppermute | solution.py:17
  1630.6 95.7 %collective-permute-start.31 = (bf16[1024,768]{0,1:T(8,128)(2,1)}, bf16[1024,768]{0,1:T(8,128)(2,1)}, u32[]{:S(2)}, u32[]{:S(2)}) collective-permute-start(bf16[1024,768]{0,1:T(8,128)(2,1)} %select_convert_fusion.6), channel_id=1, source_target_pairs={{0,8},{1,9},{2,10},{3,11},{4,12},{5,13},{6,14},{7,15},{8,0},{9,1},... | collective-permute-start | bytes 4718600 | tf_op jit(solution)/shard_map/ppermute | solution.py:17
  1698.0 68.3 %collective-permute-start.26 = (bf16[1024,768]{0,1:T(8,128)(2,1)S(1)}, bf16[1024,768]{0,1:T(8,128)(2,1)}, u32[]{:S(2)}, u32[]{:S(2)}) collective-permute-start(bf16[1024,768]{0,1:T(8,128)(2,1)S(1)} %select_convert_fusion.7), channel_id=1, source_target_pairs={{0,8},{1,9},{2,10},{3,11},{4,12},{5,13},{6,14},{7,15},{8,0},{9,1},... | collective-permute-start | bytes 4718600 | tf_op jit(solution)/shard_map/ppermute | solution.py:17
  1702.4 758.5 %reduce-scatter.47.cloned.1.call-start = ((), (), s32[]{:S(2)}) async-start(), calls=%async_computation.35 | async-start | bytes 2433024
  1730.8 42.4 %collective-permute-start.32 = (bf16[512,768]{0,1:T(8,128)(2,1)S(1)}, bf16[512,768]{0,1:T(8,128)(2,1)S(1)}, u32[]{:S(2)}, u32[]{:S(2)}) collective-permute-start(bf16[512,768]{0,1:T(8,128)(2,1)S(1)} %select_convert_fusion.10), channel_id=1, source_target_pairs={{0,4},{1,5},{2,6},{3,7},{4,0},{5,1},{6,2},{7,3},{8,12},{9,13},{10,... | collective-permute-start | bytes 2359304 | tf_op jit(solution)/shard_map/ppermute | solution.py:17
  1807.5 655.4 %reduce-scatter.43.cloned.1.call-start = ((), (), s32[]{:S(2)}) async-start(), calls=%async_computation.33 | async-start | bytes 2433024
  1822.7 642.1 %reduce-scatter.37.cloned.1.call-start = ((), (), s32[]{:S(2)}) async-start(), calls=%async_computation.30 | async-start | bytes 2433024
  2012.8 453.9 %reduce-scatter.27.cloned.1.call-start = ((), (), s32[]{:S(2)}) async-start(), calls=%async_computation.13 | async-start | bytes 2433024 | tf_op jit(solution)/shard_map/reduce_scatter | solution.py:361
  2019.6 210.4 %collective-permute-start.40 = (bf16[2048,768]{0,1:T(8,128)(2,1)}, bf16[2048,768]{0,1:T(8,128)(2,1)}, u32[]{:S(2)}, u32[]{:S(2)}) collective-permute-start(bf16[2048,768]{0,1:T(8,128)(2,1)} %bitcast.49), channel_id=1, source_target_pairs={{0,16},{1,17},{2,18},{3,19},{4,20},{5,21},{6,22},{7,23},{8,24},{9,... | collective-permute-start | bytes 9437192 | tf_op jit(solution)/shard_map/ppermute | solution.py:17
  2023.0 520.5 %reduce-scatter.25.cloned.1.call-start = ((), (), s32[]{:S(2)}) async-start(), calls=%async_computation.12 | async-start | bytes 2433024 | tf_op jit(solution)/shard_map/reduce_scatter | solution.py:361
  2028.4 312.9 %collective-permute-start.35 = (bf16[2048,768]{0,1:T(8,128)(2,1)S(1)}, bf16[2048,768]{0,1:T(8,128)(2,1)}, u32[]{:S(2)}, u32[]{:S(2)}) collective-permute-start(bf16[2048,768]{0,1:T(8,128)(2,1)S(1)} %bitcast.384), channel_id=1, source_target_pairs={{0,16},{1,17},{2,18},{3,19},{4,20},{5,21},{6,22},{7,23},{8,24},{9,... | collective-permute-start | bytes 9437192 | tf_op jit(solution)/shard_map/ppermute | solution.py:17
  2237.5 98.8 %collective-permute-start.41 = (bf16[1024,768]{0,1:T(8,128)(2,1)}, bf16[1024,768]{0,1:T(8,128)(2,1)}, u32[]{:S(2)}, u32[]{:S(2)}) collective-permute-start(bf16[1024,768]{0,1:T(8,128)(2,1)} %select_convert_fusion.4), channel_id=1, source_target_pairs={{0,8},{1,9},{2,10},{3,11},{4,12},{5,13},{6,14},{7,15},{8,0},{9,1},... | collective-permute-start | bytes 4718600 | tf_op jit(solution)/shard_map/ppermute | solution.py:17
  2241.5 459.0 %all-reduce.40.cloned.1.call-start = ((), (), s32[]{:S(2)}) async-start(), calls=%async_computation.36 | async-start | bytes 180224
  2348.8 36.6 %collective-permute-start.36 = (bf16[1024,768]{0,1:T(8,128)(2,1)}, bf16[1024,768]{0,1:T(8,128)(2,1)}, u32[]{:S(2)}, u32[]{:S(2)}) collective-permute-start(bf16[1024,768]{0,1:T(8,128)(2,1)} %select_convert_fusion.5), channel_id=1, source_target_pairs={{0,8},{1,9},{2,10},{3,11},{4,12},{5,13},{6,14},{7,15},{8,0},{9,1},... | collective-permute-start | bytes 4718600 | tf_op jit(solution)/shard_map/ppermute | solution.py:17
  2391.0 414.6 %reduce-scatter.45.cloned.1.call-start = ((), (), s32[]{:S(2)}) async-start(), calls=%async_computation.34 | async-start | bytes 2433024
  2397.0 512.8 %reduce-scatter.41.cloned.1.call-start = ((), (), s32[]{:S(2)}) async-start(), calls=%async_computation.32 | async-start | bytes 2433024
  2433.2 616.9 %reduce-scatter.31.cloned.1.call-start = ((), (), s32[]{:S(2)}) async-start(), calls=%async_computation.15 | async-start | bytes 9732096 | tf_op jit(solution)/shard_map/reduce_scatter | solution.py:365
  2439.6 752.0 %reduce-scatter.29.cloned.1.call-start = ((), (), s32[]{:S(2)}) async-start(), calls=%async_computation.14 | async-start | bytes 9732096 | tf_op jit(solution)/shard_map/reduce_scatter | solution.py:365
  2445.8 886.2 %reduce-scatter.35.cloned.1.call-start = ((), (), s32[]{:S(2)}) async-start(), calls=%async_computation.17 | async-start | bytes 9732096 | tf_op jit(solution)/shard_map/reduce_scatter | solution.py:367
  2452.1 1021.4 %reduce-scatter.33.cloned.1.call-start = ((), (), s32[]{:S(2)}) async-start(), calls=%async_computation.16 | async-start | bytes 9732096 | tf_op jit(solution)/shard_map/reduce_scatter | solution.py:367
  (158 other events, 5923.3 us)
Sparse Core Ops, SparseCore 0:
  11.6 54.6 all-gather.44
  69.2 53.1 all-gather.46
  125.9 54.2 all-gather.42
  182.9 299.5 all-gather.48
  485.8 63.8 all-gather.50
  553.0 62.4 all-gather.52
  619.0 51.4 all-gather.56
  673.5 52.9 all-gather.58
  729.9 54.1 all-gather.54
  786.9 297.0 all-gather.60
  1087.4 63.9 all-gather.62
  1154.7 62.5 all-gather.64
  1702.5 96.9 reduce-scatter.38
  1807.6 96.5 reduce-scatter.46
  1909.3 98.0 reduce-scatter.42
  2013.4 321.1 reduce-scatter.36
  2339.7 99.8 reduce-scatter.26
  2445.7 97.8 reduce-scatter.24
  2550.0 150.5 all-reduce.39
  2705.7 99.8 reduce-scatter.44
  2811.8 98.0 reduce-scatter.40
  2915.7 134.3 reduce-scatter.30
  3057.0 134.5 reduce-scatter.28
  3197.4 134.5 reduce-scatter.34
  3338.9 134.5 reduce-scatter.32
where the time goes:
time: 3500 us; the launch traced here: 3480 us
  waiting for transfers between devices  2520 us (72%)
  matrix products  447 us (13%)
  other arithmetic  188 us (5%)
  local copies, waits for them, and re-layouts  130 us (4%)
  loops' own time  79.4 us (2%)
  starting transfers between devices  64.8 us (2%)
  blocking collectives  40.6 us (1%)
    ppermute x45, waiting for transfers between devices, partner_2(): lax.ppermute(shard, axis, [(i, i ^ 1 << stride) for i in range(lax.axis_s...  1270 us
    unnamed x32, waiting for transfers between devices  343 us
    reduce_scatter x2, waiting for transfers between devices, body(): lax.psum_scatter(terms[11], 'fsdp', scatter_dimension=0, tiled=True)  280 us
    reduce_scatter x2, waiting for transfers between devices, body(): lax.psum_scatter(terms[9], 'fsdp', scatter_dimension=0, tiled=True)  279 us
    dot_general x84, matrix products, product_nt(): lax.dot_general(a, b, (((1,), (1,)), ((), ())), preferred_element_type=jn...  180 us
    dot_general x60, matrix products, product(): return jnp.dot(a, b, preferred_element_type=jnp.float32)  146 us
    dot_general x57, matrix products, product_tn(): lax.dot_general(a, b, (((0,), (0,)), ((), ())), preferred_element_type=jn...  114 us
    all_gather x2, waiting for transfers between devices, body(): lax.all_gather(outer_weight[i], 'fsdp', axis=0, tiled=True)  108 us
  transfers between devices with their start and end apart: 70, of which 48 were waited for; matrix products, arithmetic and copies ran while one was open for 16% of the time, Pallas kernels for 0%

commit v1 on v0

--- a/solution.py
+++ b/solution.py
@@ -1,6 +1,8 @@
 import jax
 import jax.numpy as jnp
 from jax import lax
+from jax.experimental import pallas as pl
+from jax.experimental.pallas import tpu as pltpu
 from jax.sharding import PartitionSpec as P
 
 HEADS = 12
@@ -373,6 +375,777 @@
     return (outcome, upstream.astype(jnp.bfloat16)) + tuple(shares)
 
 
+MESH = pl.DeviceIdType.MESH
+BF = jnp.bfloat16
+F32 = jnp.float32
+WIDE = 768
+SLICE = 384
+PACKED = 640
+ROWS = 128
+NKEYS = 1536
+
+
+class Pool:
+    def __init__(self, ref):
+        self.ref = ref
+        self.used = 0
+
+    def take(self):
+        self.used += 1
+        return self.ref.at[self.used - 1]
+
+    def block(self, n):
+        first = self.used
+        self.used += n
+        return lambda i: self.ref.at[first + i]
+
+
+class Place:
+    def __init__(self):
+        me = lax.axis_index("fsdp")
+        p = lax.rem(me, 32)
+        self.base = me - p
+        self.z = p // 8
+        self.f = lax.rem(p // 2, 4)
+        self.c = lax.rem(p, 2)
+
+    def at(self, z, f, c):
+        return self.base + 8 * z + 2 * f + c
+
+    def f_at(self, k):
+        return lax.rem(self.f + k + 4, 4)
+
+    def z_at(self, k):
+        return lax.rem(self.z + k + 4, 4)
+
+    def plane(self, k):
+        return self.at(self.z, self.f_at(k), self.c)
+
+    def column(self, k):
+        return self.at(self.z_at(k), self.f, self.c)
+
+    def sibling(self):
+        return self.at(self.z, self.f, 1 - self.c)
+
+
+def greet(place):
+    barrier = pltpu.get_barrier_semaphore()
+    for dev in [place.plane(k) for k in (1, 2, 3)] + [place.column(k) for k in (1, 2, 3)] + [place.sibling()]:
+        pl.semaphore_signal(barrier, inc=1, device_id=(dev,), device_id_type=MESH)
+    pl.semaphore_wait(barrier, 7)
+
+
+def remote(src, dst, sems, device):
+    return pltpu.make_async_remote_copy(
+        src_ref=src, dst_ref=dst, send_sem=sems[0], recv_sem=sems[1], device_id=(device,), device_id_type=MESH
+    )
+
+
+def norm_rows(z, gain, shift):
+    centre = z - jnp.mean(z, axis=-1, keepdims=True)
+    inv = lax.rsqrt(jnp.mean(centre * centre, axis=-1, keepdims=True) + EPSILON)
+    return centre * inv * gain + shift
+
+
+def norm_rows_back(z, gain, upstream):
+    centre = z - jnp.mean(z, axis=-1, keepdims=True)
+    inv = lax.rsqrt(jnp.mean(centre * centre, axis=-1, keepdims=True) + EPSILON)
+    scaled = centre * inv
+    weighted = upstream * gain
+    inner = inv * (
+        weighted
+        - jnp.mean(weighted, axis=-1, keepdims=True)
+        - scaled * jnp.mean(weighted * scaled, axis=-1, keepdims=True)
+    )
+    return inner, jnp.sum(upstream * scaled, axis=0, keepdims=True), jnp.sum(upstream, axis=0, keepdims=True)
+
+
+def weights_kernel(
+    col, rows_out, rows_o, small, colg, outg, og, smallg, send_sems, recv_sems, local_sems
+):
+    place = Place()
+    z, f, c = place.z, place.f, place.c
+    sends, recvs, locs = Pool(send_sems), Pool(recv_sems), Pool(local_sems)
+
+    def pair():
+        return sends.take(), recvs.take()
+
+    mine = [
+        pltpu.make_async_copy(col.at[f], colg.at[z, c, f], locs.take()),
+        pltpu.make_async_copy(small, smallg.at[z, c, f], locs.take()),
+        pltpu.make_async_copy(rows_out, outg.at[z, c], locs.take()),
+    ]
+    o_copy = pltpu.make_async_copy(rows_o, og.at[c, f], locs.take())
+    for m in mine:
+        m.start()
+
+    @pl.when(f == z)
+    def _():
+        o_copy.start()
+
+    greet(place)
+    flying = []
+    first = []
+    for k in (1, 2, 3):
+        a = remote(col.at[place.f_at(k)], colg.at[z, c, f], pair(), place.plane(k))
+        b = remote(small, smallg.at[z, c, f], pair(), place.plane(k))
+        a.start()
+        b.start()
+        first += [a, b]
+        flying += [a, b]
+    o_send, o_recv = sends.take(), recvs.block(4)
+    o_index = lax.rem(z - f + 4, 4)
+    o_first = remote(rows_o, og.at[c, f], (o_send, o_recv(o_index)), place.at(z, z, c))
+
+    @pl.when(f != z)
+    def _():
+        o_first.start()
+
+    out_moves = []
+    for k in (1, 2, 3):
+        a = remote(rows_out, outg.at[z, c], pair(), place.column(k))
+        a.start()
+        out_moves.append(a)
+    flying += out_moves
+    for m in mine:
+        m.wait()
+    for a in first:
+        a.wait_recv()
+    moves = []
+    for k in (1, 2, 3):
+        a = remote(colg.at[z, c], colg.at[z, c], pair(), place.column(k))
+        b = remote(smallg.at[z, c], smallg.at[z, c], pair(), place.column(k))
+        a.start()
+        b.start()
+        moves.append((a, b))
+        flying += [a, b]
+    o_sends, o_arrive = sends.block(4), recvs.take()
+    o_moves = [
+        remote(og.at[c], og.at[c], (o_sends(k), o_arrive), place.column(k)) for k in (1, 2, 3)
+    ]
+
+    @pl.when(f == z)
+    def _():
+        o_copy.wait()
+        for k in (1, 2, 3):
+            remote(rows_o, og.at[c, f], (o_send, o_recv(k)), place.at(z, z, c)).wait_recv()
+        for m in o_moves:
+            m.start()
+
+    side = []
+
+    def hand_over(zz):
+        for ref in (colg, outg, smallg):
+            a = remote(ref.at[zz, c], ref.at[zz, c], pair(), place.sibling())
+            a.start()
+            side.append(a)
+
+    hand_over(z)
+    for k in (1, 2, 3):
+        moves[k - 1][0].wait_recv()
+        moves[k - 1][1].wait_recv()
+        out_moves[k - 1].wait_recv()
+        hand_over(place.z_at(-k))
+
+    @pl.when(f != z)
+    def _():
+        o_moves[0].wait_recv()
+
+    a = remote(og.at[c], og.at[c], pair(), place.sibling())
+    a.start()
+    side.append(a)
+    for a in side:
+        a.wait_recv()
+    for a in flying + side:
+        a.wait_send()
+
+    @pl.when(f != z)
+    def _():
+        o_first.wait_send()
+
+    @pl.when(f == z)
+    def _():
+        for m in o_moves:
+            m.wait_send()
+
+
+def pick_parents(kp, kv, route, zz, cc):
+    def one(b, carry):
+        total = kp[b, cc]
+        for ft in range(4):
+            total = total + kv[zz, cc, ft * ROWS : (ft + 1) * ROWS, :] * route[b, 4 * zz + ft].astype(BF)
+        kp[b, cc] = total
+        return carry
+
+    lax.fori_loop(0, 4, one, 0)
+
+
+def all_keys(kv, kp, z, b, lanes):
+    rows = pl.ds(pl.multiple_of(b * ROWS, ROWS), ROWS)
+    return jnp.concatenate(
+        [
+            kv[0, 0, :, lanes], kv[0, 1, :, lanes], kv[z, 0, rows, lanes], kv[z, 1, rows, lanes],
+            kp[b, 0, :, lanes], kp[b, 1, :, lanes],
+        ],
+        axis=0,
+    )
+
+
+def forward_kernel(
+    x_ref, wqkv, wo, win, wout, vec, route, pen,
+    xn_ref, xb_o, qp_o, kv_o, kp_o, p_o, ctx_o, z1_o, hb_o, gp_o, gl_o, z2_o,
+    xb, qp, kv, kp, p, ctx, hb, gp, gl, z1, z2, own, rs1_s, rs1_r, rs2_s, rs2_r,
+    send_sems, recv_sems, local_sems,
+):
+    place = Place()
+    z, f, c = place.z, place.f, place.c
+    sends, recvs, locs = Pool(send_sems), Pool(recv_sems), Pool(local_sems)
+    flying, saving = [], []
+
+    def launch(src, dst, device):
+        a = remote(src, dst, (sends.take(), recvs.take()), device)
+        a.start()
+        flying.append(a)
+        return a
+
+    def save(src, dst):
+        a = pltpu.make_async_copy(src, dst, locs.take())
+        a.start()
+        saving.append(a)
+
+    xb[f] = x_ref[...].astype(BF)
+    greet(place)
+    came = [None] + [launch(xb.at[f], xb.at[f], place.plane(k)) for k in (1, 2, 3)]
+    lane = lax.broadcasted_iota(jnp.int32, (ROWS, 128), 1)
+    for k in range(4):
+        g = place.f_at(-k)
+        if k:
+            came[k].wait_recv()
+        qkv = product(xb[g], wqkv[...]) + vec[0:1, :PACKED]
+        rows = pl.ds(pl.multiple_of(g * ROWS, ROWS), ROWS)
+        kv[z, c, rows, :] = qkv[:, 256:].astype(BF)
+        scaled = qkv[:, :256] * (HEAD_DIM ** (-0.5))
+        front = scaled[:, :128]
+        qp[rows, 0:128] = jnp.where(lane < 64, front, 0.0).astype(BF)
+        qp[rows, 128:256] = jnp.where(lane < 64, pltpu.roll(front, 64, 1), 0.0).astype(BF)
+        qp[rows, 256:384] = scaled[:, 128:].astype(BF)
+    move = [launch(kv.at[z, c], kv.at[z, c], place.column(k)) for k in (1, 2, 3)]
+    side = [launch(kv.at[z, c], kv.at[z, c], place.sibling())]
+    save(xb, xb_o)
+    save(qp, qp_o)
+    kp[...] = jnp.zeros_like(kp)
+    pick_parents(kp, kv, route, z, c)
+    for k in (1, 2, 3):
+        move[k - 1].wait_recv()
+        there = place.z_at(-k)
+        side.append(launch(kv.at[there, c], kv.at[there, c], place.sibling()))
+        pick_parents(kp, kv, route, there, c)
+    for k in range(4):
+        side[k].wait_recv()
+        pick_parents(kp, kv, route, place.z_at(-k), 1 - c)
+    save(kp, kp_o)
+    save(kv, kv_o)
+
+    def attend(i, carry):
+        h, b = i // 4, lax.rem(i, 4)
+        lanes = pl.ds(pl.multiple_of(h * 128, 128), 128)
+        rows = pl.ds(pl.multiple_of(b * ROWS, ROWS), ROWS)
+        keys = all_keys(kv, kp, z, b, lanes)
+        s = product_nt(qp[rows, lanes], keys)
+        s = jnp.concatenate(
+            [s[:, :1024], s[:, 1024:1280] + pen[4 + b], s[:, 1280:] + pen[b]], axis=1
+        )
+        e = jnp.exp(s - jnp.max(s, axis=1, keepdims=True))
+        pb = (e / jnp.sum(e, axis=1, keepdims=True)).astype(BF)
+        p[h, b] = pb
+        ctx[rows, lanes] = product(pb, keys).astype(BF)
+        return carry
+
+    lax.fori_loop(0, 12, attend, 0)
+    save(p, p_o)
+    save(ctx, ctx_o)
+    back = [None]
+    for k in (1, 2, 3, 0):
+        g = place.f_at(-k)
+        rows = pl.ds(pl.multiple_of(g * ROWS, ROWS), ROWS)
+        part = product(ctx[rows, :], wo[...])
+        if k:
+            rs1_s[k - 1] = part.astype(BF)
+            back.append(launch(rs1_s.at[k - 1], rs1_r.at[k - 1], place.plane(-k)))
+        else:
+            own[...] = part
+    for k in (1, 2, 3):
+        back[k].wait_recv()
+    total = own[...] + rs1_r[0].astype(F32) + rs1_r[1].astype(F32) + rs1_r[2].astype(F32)
+    zz = x_ref[...] + total + vec[1:2, :]
+    z1[...] = zz
+    save(z1, z1_o)
+    hidden = norm_rows(zz, vec[2:3, :], vec[3:4, :])
+    hb[f] = hidden.astype(BF)
+    came = [None] + [launch(hb.at[f], hb.at[f], place.plane(k)) for k in (1, 2, 3)]
+    back = [None]
+    for k in range(4):
+        g = place.f_at(-k)
+        if k:
+            came[k].wait_recv()
+        u = product(hb[g], win[...]) + vec[4:5, :]
+        cdf = 0.5 * (1.0 + lax.erf(u * (0.5 ** 0.5)))
+        gp[g] = cdf + u * jnp.exp(-0.5 * u * u) * 0.3989422804014327
+        low = (u * cdf).astype(BF)
+        gl[g] = low
+        part = product(low, wout[...])
+        if k:
+            rs2_s[k - 1] = part.astype(BF)
+            back.append(launch(rs2_s.at[k - 1], rs2_r.at[k - 1], place.plane(-k)))
+        else:
+            own[...] = part
+    save(hb, hb_o)
+    save(gp, gp_o)
+    save(gl, gl_o)
+    for k in (1, 2, 3):
+        back[k].wait_recv()
+    total = own[...] + rs2_r[0].astype(F32) + rs2_r[1].astype(F32) + rs2_r[2].astype(F32)
+    zz = norm_rows(z1[...], vec[2:3, :], vec[3:4, :]) + total + vec[5:6, :]
+    z2[...] = zz
+    save(z2, z2_o)
+    xn_ref[...] = norm_rows(zz, vec[6:7, :], vec[7:8, :])
+    for a in saving:
+        a.wait()
+    for a in flying:
+        a.wait_send()
+
+
+def backward_kernel(
+    dy_ref, wqkv, wo, win, wout, vec, route, xb, qp, kv, kp, p, ctx, z1, hb, gp, gl, z2,
+    dx_ref, dqkv_o, din_o, dout_o, do_o, dvec_o,
+    df, du, da, dctx, dqf, dqkv, dz, dz1, dkt, dself, dpar, tgt, tgt_r, summed, summed_r,
+    own, rs1_s, rs1_r, rs2_s, rs2_r, send_sems, recv_sems,
+):
+    place = Place()
+    z, f, c = place.z, place.f, place.c
+    sends, recvs = Pool(send_sems), Pool(recv_sems)
+    flying = []
+
+    def launch(src, dst, device):
+        a = remote(src, dst, (sends.take(), recvs.take()), device)
+        a.start()
+        flying.append(a)
+        return a
+
+    def whole(ref):
+        return ref[...].reshape(4 * ROWS, ref.shape[-1])
+
+    grad, dgain, dshift = norm_rows_back(z2[...], vec[6:7, :], dy_ref[...])
+    dvec_o[6:7, :] = dgain
+    dvec_o[7:8, :] = dshift
+    dz[...] = grad
+    low = grad.astype(BF)
+    df[f] = low
+    dvec_o[5:6, :] = jnp.sum(low.astype(F32), axis=0, keepdims=True)
+    greet(place)
+    came = [None] + [launch(df.at[f], df.at[f], place.plane(k)) for k in (1, 2, 3)]
+    back = [None]
+    bias = jnp.zeros((1, WIDE), F32)
+    for k in range(4):
+        g = place.f_at(-k)
+        if k:
+            came[k].wait_recv()
+        low = (product_nt(df[g], wout[...]) * gp[g]).astype(BF)
+        du[g] = low
+        bias = bias + jnp.sum(low.astype(F32), axis=0, keepdims=True)
+        part = product_nt(low, win[...])
+        if k:
+            rs1_s[k - 1] = part.astype(BF)
+            back.append(launch(rs1_s.at[k - 1], rs1_r.at[k - 1], place.plane(-k)))
+        else:
+            own[...] = part
+    dvec_o[4:5, :] = bias
+
+    def ffn_grads(i, carry):
+        lanes = pl.ds(pl.multiple_of(i * 256, 256), 256)
+        dout_o[lanes, :] = product_tn(gl[:, :, lanes].reshape(512, 256), whole(df)).astype(BF)
+        din_o[lanes, :] = product_tn(hb[:, :, lanes].reshape(512, 256), whole(du)).astype(BF)
+        return carry
+
+    lax.fori_loop(0, 3, ffn_grads, 0)
+    for k in (1, 2, 3):
+        back[k].wait_recv()
+    up = dz[...] + own[...] + rs1_r[0].astype(F32) + rs1_r[1].astype(F32) + rs1_r[2].astype(F32)
+    grad, dgain, dshift = norm_rows_back(z1[...], vec[2:3, :], up)
+    dvec_o[2:3, :] = dgain
+    dvec_o[3:4, :] = dshift
+    dz1[...] = grad
+    low = grad.astype(BF)
+    da[f] = low
+    dvec_o[1:2, :] = jnp.sum(low.astype(F32), axis=0, keepdims=True)
+    came = [None] + [launch(da.at[f], da.at[f], place.plane(k)) for k in (1, 2, 3)]
+    dkt[...] = jnp.zeros_like(dkt)
+    for k in range(4):
+        g = place.f_at(-k)
+        rows = pl.ds(pl.multiple_of(g * ROWS, ROWS), ROWS)
+        if k:
+            came[k].wait_recv()
+        dctx[rows, :] = product_nt(da[g], wo[...]).astype(BF)
+
+    def attend(i, carry):
+        h, b = i // 4, lax.rem(i, 4)
+        lanes = pl.ds(pl.multiple_of(h * 128, 128), 128)
+        rows = pl.ds(pl.multiple_of(b * ROWS, ROWS), ROWS)
+        keys = all_keys(kv, kp, z, b, lanes)
+        q, g = qp[rows, lanes], dctx[rows, lanes]
+        low = p[h, b]
+        pf = low.astype(F32)
+        dp = product_nt(g, keys)
+        t = pf * dp
+        ds = (t - pf * jnp.sum(t, axis=1, keepdims=True)).astype(BF)
+        dqf[h, rows, :] = product(ds, keys) * (HEAD_DIM ** (-0.5))
+        dkv = product_tn(jnp.concatenate([ds, low], axis=0), jnp.concatenate([q, g], axis=0))
+        dkt[:, lanes] += dkv[:1024]
+        dself[b, :, lanes] = dkv[1024:1280]
+        dpar[b, :, lanes] = dkv[1280:]
+        return carry
+
+    lax.fori_loop(0, 12, attend, 0)
+    for cc in range(2):
+        tgt[cc, 0] = dkt[cc * 512 : (cc + 1) * 512, :].astype(BF)
+
+    def scatter(i, carry):
+        zt, ft = 1 + i // 4, lax.rem(i, 4)
+        rows = pl.ds(pl.multiple_of(ft * ROWS, ROWS), ROWS)
+        here = jnp.where(zt == z, 1.0, 0.0)
+        for cc in range(2):
+            half = slice(cc * ROWS, (cc + 1) * ROWS)
+            total = dself[ft, half, :] * here
+            for b in range(4):
+                total = total + dpar[b, half, :] * route[b, 4 * zt + ft]
+            tgt[cc, zt, rows, :] = total.astype(BF)
+        return carry
+
+    lax.fori_loop(0, 12, scatter, 0)
+    near = launch(tgt.at[1 - c], tgt_r, place.sibling())
+    lane = lax.broadcasted_iota(jnp.int32, (ROWS, 128), 1)
+    for g in range(4):
+        rows = slice(g * ROWS, (g + 1) * ROWS)
+        first = jnp.where(lane < 64, dqf[0, rows, :], pltpu.roll(dqf[1, rows, :], 64, 1))
+        dqkv[g, :, 0:128] = first.astype(BF)
+        dqkv[g, :, 128:256] = jnp.where(lane < 64, dqf[2, rows, :], 0.0).astype(BF)
+    near.wait_recv()
+    for zt in range(4):
+        summed[zt] = (tgt[c, zt].astype(F32) + tgt_r[zt].astype(F32)).astype(BF)
+    far = [launch(summed.at[place.z_at(k)], summed_r.at[k - 1], place.column(k)) for k in (1, 2, 3)]
+    do_o[...] = product_tn(ctx[...], whole(da)).astype(BF)
+    for a in far:
+        a.wait_recv()
+    total = summed[z].astype(F32) + summed_r[0].astype(F32) + summed_r[1].astype(F32) + summed_r[2].astype(F32)
+    for g in range(4):
+        dqkv[g, :, 256:] = total[g * ROWS : (g + 1) * ROWS, :].astype(BF)
+    back = [None]
+    for k in (1, 2, 3, 0):
+        g = place.f_at(-k)
+        part = product_nt(dqkv[g], wqkv[...])
+        if k:
+            rs2_s[k - 1] = part.astype(BF)
+            back.append(launch(rs2_s.at[k - 1], rs2_r.at[k - 1], place.plane(-k)))
+        else:
+            own[...] = part
+
+    def qkv_grads(i, carry):
+        lanes = pl.ds(pl.multiple_of(i * 256, 256), 256)
+        dqkv_o[lanes, :] = product_tn(xb[:, :, lanes].reshape(512, 256), whole(dqkv)).astype(BF)
+        return carry
+
+    lax.fori_loop(0, 3, qkv_grads, 0)
+    sums = jnp.sum(whole(dqkv).astype(F32), axis=0, keepdims=True)
+    dvec_o[0:1, :] = jnp.concatenate([sums, jnp.zeros((1, WIDE - PACKED), F32)], axis=1)
+    for k in (1, 2, 3):
+        back[k].wait_recv()
+    dx_ref[...] = dz1[...] + own[...] + rs2_r[0].astype(F32) + rs2_r[1].astype(F32) + rs2_r[2].astype(F32)
+    for a in flying:
+        a.wait_send()
+
+
+def reduce_kernel(
+    gcol, gout, go, gsm, col_o, out_o, o_o, sm_o,
+    col_a, out_a, o_a, sm_a, col_u, out_u, o_u, sm_u, col_b, out_b, o_b, sm_b, col_v, o_v, sm_v,
+    send_sems, recv_sems,
+):
+    place = Place()
+    z, f, c = place.z, place.f, place.c
+    sends, recvs = Pool(send_sems), Pool(recv_sems)
+    flying = []
+
+    def launch(src, dst, device):
+        a = remote(src, dst, (sends.take(), recvs.take()), device)
+        a.start()
+        flying.append(a)
+        return a
+
+    greet(place)
+    sib = place.sibling()
+    near = [
+        launch(gcol.at[1 - c], col_a, sib),
+        launch(gout.at[1 - c], out_a, sib),
+        launch(go.at[1 - c], o_a, sib),
+        launch(gsm, sm_a, sib),
+    ]
+    for a in near:
+        a.wait_recv()
+    sm_u[...] = gsm[...] + sm_a[...]
+    o_u[...] = (go[c].astype(F32) + o_a[...].astype(F32)).astype(BF)
+
+    def chip_sum(i, carry):
+        col_u[i] = (gcol[c, i].astype(F32) + col_a[i].astype(F32)).astype(BF)
+        out_u[i] = (gout[c, i].astype(F32) + out_a[i].astype(F32)).astype(BF)
+        return carry
+
+    lax.fori_loop(0, 4, chip_sum, 0)
+    far = []
+    for k in (1, 2, 3):
+        there = place.z_at(k)
+        far.append(launch(col_u.at[there], col_b.at[k - 1], place.column(k)))
+        far.append(launch(out_u.at[there], out_b.at[k - 1], place.column(k)))
+        far.append(launch(sm_u, sm_b.at[k - 1], place.column(k)))
+    o_send, o_recv = sends.take(), recvs.block(4)
+    shift = lax.rem(f - z + 4, 4)
+    o_far = remote(o_u, o_b.at[shift], (o_send, o_recv(shift)), place.at(f, f, c))
+
+    @pl.when(f != z)
+    def _():
+        o_far.start()
+
+    @pl.when(f == z)
+    def _():
+        for k in (1, 2, 3):
+            remote(o_u, o_b.at[k], (o_send, o_recv(k)), place.at(f, f, c)).wait_recv()
+        for g in range(4):
+            rows = slice(g * 48, (g + 1) * 48)
+            o_v[g] = (
+                o_u[rows, :].astype(F32)
+                + o_b[1, rows, :].astype(F32)
+                + o_b[2, rows, :].astype(F32)
+                + o_b[3, rows, :].astype(F32)
+            ).astype(BF)
+
+    for a in far:
+        a.wait_recv()
+    sm_v[...] = sm_u[...] + sm_b[0] + sm_b[1] + sm_b[2]
+    out_o[...] = out_u[z].astype(F32) + out_b[0].astype(F32) + out_b[1].astype(F32) + out_b[2].astype(F32)
+    for g in range(4):
+        rows = slice(g * 48, (g + 1) * 48)
+        col_v[g] = (
+            col_u[z, rows, :].astype(F32)
+            + col_b[0, rows, :].astype(F32)
+            + col_b[1, rows, :].astype(F32)
+            + col_b[2, rows, :].astype(F32)
+        ).astype(BF)
+    last = []
+    for k in (1, 2, 3):
+        last.append(launch(col_v.at[place.f_at(k)], col_o.at[f], place.plane(k)))
+        last.append(launch(sm_v, sm_o.at[f], place.plane(k)))
+    col_o[f] = col_v[f]
+    sm_o[f] = sm_v[...]
+    o_sends, o_last = sends.block(4), recvs.take()
+    moves = [
+        remote(o_v.at[place.f_at(k)], o_o, (o_sends(k), o_last), place.plane(k)) for k in (1, 2, 3)
+    ]
+
+    @pl.when(f == z)
+    def _():
+        for m in moves:
+            m.start()
+        o_o[...] = o_v[f]
+
+    @pl.when(f != z)
+    def _():
+        moves[0].wait_recv()
+
+    for a in last:
+        a.wait_recv()
+    for a in flying:
+        a.wait_send()
+
+    @pl.when(f != z)
+    def _():
+        o_far.wait_send()
+
+    @pl.when(f == z)
+    def _():
+        for m in moves:
+            m.wait_send()
+
+
+ANY = pl.BlockSpec(memory_space=pl.ANY)
+VM = pl.BlockSpec(memory_space=pltpu.VMEM)
+SM = pl.BlockSpec(memory_space=pltpu.SMEM)
+LIMIT = 60 * 1024 * 1024
+
+
+def shape(*dims, dtype=BF):
+    return jax.ShapeDtypeStruct(dims, dtype)
+
+
+def call(kernel, number, outs, out_specs, in_specs, scratch, sems, args, flops):
+    return pl.pallas_call(
+        kernel,
+        out_shape=outs,
+        in_specs=in_specs,
+        out_specs=out_specs,
+        scratch_shapes=[pltpu.VMEM(s.shape, s.dtype) for s in scratch]
+        + [pltpu.SemaphoreType.DMA((n,)) for n in sems],
+        compiler_params=pltpu.CompilerParams(
+            collective_id=number, has_side_effects=True, vmem_limit_bytes=LIMIT
+        ),
+        cost_estimate=pl.CostEstimate(flops=flops, bytes_accessed=20000000, transcendentals=0),
+    )(*args)
+
+
+def column_parts(query, key, value, inner):
+    n = query.shape[0] * query.shape[1]
+    q = query.reshape(n, 4, 3, 64)
+    q = jnp.pad(q, ((0, 0), (0, 0), (0, 1), (0, 0))).reshape(n, 4, 256)
+    kv = jnp.stack([key.reshape(n, 4, 3, 64), value.reshape(n, 4, 3, 64)], axis=3).reshape(n, 4, 384)
+    up = inner.reshape(n, 4, 4, 192).transpose(0, 2, 1, 3).reshape(n, 4, WIDE)
+    return jnp.concatenate([q, kv, up], axis=2).transpose(1, 0, 2)
+
+
+def gather_weights(col, rows_out, rows_o, small):
+    return call(
+        weights_kernel, 0,
+        (shape(4, 2, 4, 48, 1408), shape(4, 2, 192, WIDE), shape(2, 4, 48, WIDE), shape(4, 2, 4, 16, 128)),
+        (ANY,) * 4, [ANY] * 4, [], (64, 64, 8), (col, rows_out, rows_o, small), 1000,
+    )
+
+
+def forward_layer(state, weights, vec, route, pen):
+    wqkv, wo, win, wout = weights
+    saved = (
+        shape(4, ROWS, WIDE), shape(512, SLICE), shape(4, 2, 512, SLICE), shape(4, 2, ROWS, SLICE), shape(3, 4, ROWS, NKEYS),
+        shape(512, SLICE), shape(ROWS, WIDE, dtype=F32), shape(4, ROWS, WIDE), shape(4, ROWS, WIDE, dtype=F32),
+        shape(4, ROWS, WIDE), shape(ROWS, WIDE, dtype=F32),
+    )
+    xb, qp, kv, kp, p, ctx, z1, hb, gp, gl, z2 = saved
+    piece = shape(3, ROWS, WIDE)
+    outs = call(
+        forward_kernel, 1, (shape(ROWS, WIDE, dtype=F32),) + saved, (VM,) + (ANY,) * 11,
+        [VM] * 6 + [SM] * 2,
+        [xb, qp, kv, kp, p, ctx, hb, gp, gl, z1, z2, shape(ROWS, WIDE, dtype=F32)] + [piece] * 4,
+        (48, 48, 16), (state, wqkv, wo, win, wout, vec, route, pen), 3 * 10**9,
+    )
+    return outs[0], outs[1:]
+
+
+def backward_layer(upstream, weights, vec, route, saved):
+    wqkv, wo, win, wout = weights
+    local = shape(ROWS, WIDE, dtype=F32)
+    full = shape(4, ROWS, WIDE)
+    piece = shape(3, ROWS, WIDE)
+    keys = shape(4, 256, SLICE, dtype=F32)
+    return call(
+        backward_kernel, 2,
+        (local, shape(WIDE, PACKED), shape(WIDE, WIDE), shape(WIDE, WIDE), shape(SLICE, WIDE), shape(8, WIDE, dtype=F32)),
+        (VM,) * 6, [VM] * 6 + [SM] + [VM] * 11,
+        [full, full, full, shape(512, SLICE), shape(3, 512, 128, dtype=F32), shape(4, ROWS, PACKED), local, local,
+         shape(1024, SLICE, dtype=F32), keys, keys, shape(2, 4, 512, SLICE), shape(4, 512, SLICE),
+         shape(4, 512, SLICE), shape(3, 512, SLICE), local, piece, piece, piece, piece],
+        (48, 48), (upstream, wqkv, wo, win, wout, vec, route) + tuple(saved), 6 * 10**9,
+    )
+
+
+def reduce_grads(gcol, gout, go, gsm):
+    half = [shape(4, 192, 1408), shape(4, 192, WIDE), shape(192, WIDE), shape(16, WIDE, dtype=F32)]
+    far = [shape(3, 192, 1408), shape(3, 192, WIDE), shape(4, 192, WIDE), shape(3, 16, WIDE, dtype=F32)]
+    return call(
+        reduce_kernel, 3,
+        (shape(4, 48, 1408), shape(192, WIDE, dtype=F32), shape(48, WIDE), shape(4, 16, WIDE, dtype=F32)),
+        (VM,) * 4, [VM] * 4,
+        half + half + far + [shape(4, 48, 1408), shape(4, 48, WIDE), shape(16, WIDE, dtype=F32)],
+        (64, 64), (gcol, gout, go, gsm), 1000,
+    )
+
+
+def slice_body(
+    activations, query_weight, query_bias, key_weight, value_weight, value_bias, output_weight, output_bias,
+    first_gain, first_shift, inner_weight, inner_bias, outer_weight, outer_bias, second_gain, second_shift,
+    cotangent, parents, segments,
+):
+    place = Place()
+    z, f, c = place.z, place.f, place.c
+    col = column_parts(query_weight, key_weight, value_weight, inner_weight)
+    vectors = (query_bias, value_bias, output_bias, first_gain, first_shift, outer_bias, second_gain, second_shift)
+    small = jnp.concatenate([v.reshape(-1) for v in vectors] + [inner_bias.reshape(-1), segments[:1].astype(BF)])
+    small = jnp.pad(small, (0, 2048 - small.shape[0])).reshape(16, 128)
+    colg, outg, og, smallg = gather_weights(
+        col, outer_weight.reshape(192, WIDE), output_weight.reshape(48, WIDE), small
+    )
+    wide = colg.reshape(4, 2, 4, 2, 24, 1408).transpose(3, 0, 2, 1, 4, 5).reshape(2, WIDE, 1408)
+    outer = outg.reshape(4, 2, 2, 96, WIDE).transpose(2, 0, 1, 3, 4).reshape(2, WIDE, WIDE)
+    o_rows = og.reshape(2, 4, 2, 24, WIDE).transpose(2, 1, 0, 3, 4).reshape(2, 3, 64, WIDE)
+    o_rows = jnp.pad(o_rows, ((0, 0), (0, 0), (64, 0), (0, 0))).reshape(2, SLICE, WIDE)
+    flat = smallg.transpose(0, 2, 1, 3, 4).reshape(32, 2048).astype(F32)
+    parts = [flat[:, i * 48 : (i + 1) * 48].reshape(32, 2, 24).transpose(1, 0, 2).reshape(2, WIDE) for i in range(8)]
+    q_all, v_all, o_all, g1, s1, out_all, g2, s2 = parts
+    in_all = flat[:, 384:576].reshape(4, 4, 2, 2, 96)
+    in_mine = lax.dynamic_index_in_dim(in_all, f, 1, keepdims=False).transpose(2, 0, 1, 3).reshape(2, WIDE)
+    q_mine = lax.dynamic_slice_in_dim(q_all, 192 * f, 192, 1)
+    v_mine = lax.dynamic_slice_in_dim(v_all, 192 * f, 192, 1).reshape(2, 3, 64)
+    kv_mine = jnp.pad(v_mine, ((0, 0), (0, 0), (64, 0))).reshape(2, SLICE)
+    qkv_mine = jnp.pad(jnp.concatenate([q_mine, jnp.zeros((2, 64), F32), kv_mine], axis=1), ((0, 0), (0, WIDE - PACKED)))
+    vecs = jnp.stack([qkv_mine, o_all, g1, s1, in_mine, out_all, g2, s2], axis=1)
+
+    labels = flat[:, 576].reshape(16, 2)[:, 0].astype(jnp.int32)
+    mine = lax.dynamic_slice_in_dim(labels, 4 * z, 4, 0)
+    parent = lookup_rows(mine, parents)
+    match = (parent[:, None] == labels[None, :]).astype(jnp.int32)
+    branch = parent != labels[0]
+    pen = jnp.concatenate(
+        [jnp.where(branch, 0.0, MASKED), jnp.where(z > 0, jnp.zeros((4,), F32), MASKED)]
+    ).astype(F32)
+    route = jnp.where(branch[:, None], match, 0).astype(F32)
+
+    state = activations.astype(F32)
+    saved = []
+    weights = []
+    for i in range(LAYERS):
+        weights.append((wide[i, :, :PACKED], o_rows[i], wide[i, :, PACKED:], outer[i]))
+        state, kept = forward_layer(state, weights[i], vecs[i], route, pen)
+        saved.append(kept)
+    outcome = state.astype(BF)
+    upstream = cotangent.astype(F32)
+    grads = [None] * LAYERS
+    for i in reversed(range(LAYERS)):
+        upstream, *grads[i] = backward_layer(upstream, weights[i], vecs[i], route, saved[i])
+
+    dqkv, din, dout, do, dvec = (jnp.stack([grads[0][j], grads[1][j]]) for j in range(5))
+    gcol = jnp.concatenate([dqkv, din], axis=2).reshape(2, 4, 4, 2, 24, 1408)
+    gcol = gcol.transpose(3, 1, 2, 0, 4, 5).reshape(2, 4, 192, 1408)
+    gout = dout.reshape(2, 4, 2, 96, WIDE).transpose(2, 1, 0, 3, 4).reshape(2, 4, 192, WIDE)
+    go = do.reshape(2, 3, 2, 64, WIDE)[:, :, 1].reshape(2, 4, 2, 24, WIDE)
+    go = go.transpose(2, 1, 0, 3, 4).reshape(2, 192, WIDE)
+    rcol, rout, ro, rsm = reduce_grads(gcol, gout, go, dvec.reshape(16, WIDE))
+    rcol = rcol.astype(F32).reshape(4, 2, 24, 1408).transpose(1, 2, 0, 3)
+    dq = rcol[..., :192].reshape(2, 24, WIDE)
+    dkv = rcol[..., 256:640].reshape(2, 24, 4, 3, 2, 64)
+    dk = dkv[..., 0, :].reshape(2, 24, WIDE)
+    dv = dkv[..., 1, :].reshape(2, 24, WIDE)
+    dinner = rcol[..., 640:].reshape(2, 24, 4, 4, 192).transpose(0, 1, 3, 2, 4).reshape(2, 24, 3072)
+    rsm = rsm.reshape(4, 2, 8, WIDE)
+    sums = jnp.sum(rsm, axis=0)
+    at = 24 * (8 * z + 2 * f + c)
+
+    def own_part(v):
+        return lax.dynamic_slice_in_dim(v, at, 24, 1)
+
+    dqb = rsm[:, :, 0, :192].transpose(1, 0, 2).reshape(2, WIDE)
+    dvb = rsm[:, :, 0, 256:640].reshape(4, 2, 3, 2, 64)[:, :, :, 1].transpose(1, 0, 2, 3).reshape(2, WIDE)
+    dib = lax.dynamic_index_in_dim(rsm[:, :, 4], f, 0, keepdims=False)
+    dib = lax.dynamic_slice_in_dim(dib, 96 * (2 * z + c), 96, 1)
+    return (
+        outcome, upstream.astype(BF), dq, own_part(dqb), dk, dv, own_part(dvb),
+        ro.astype(F32).reshape(2, 24, WIDE), own_part(sums[:, 1]), own_part(sums[:, 2]), own_part(sums[:, 3]),
+        dinner, dib, rout.reshape(2, 96, WIDE), own_part(sums[:, 5]), own_part(sums[:, 6]), own_part(sums[:, 7]),
+    )
+
+
 def solution(mesh):
     placed = (
         P("fsdp", None),
@@ -396,7 +1169,7 @@
         P("fsdp"),
     )
     return jax.shard_map(
-        body,
+        slice_body if mesh.shape["fsdp"] == 32 else body,
         mesh=mesh,
         in_specs=placed,
         out_specs=(

time: 3500 us -> 687 us (0.20)
  waiting for transfers between devices: 2520 us -> 0 us
  Pallas kernels: 0 us -> 611 us
  matrix products: 447 us -> 0 us
  other arithmetic: 188 us -> 15.6 us
  loops' own time: 79.4 us -> 0 us
  local copies, waits for them, and re-layouts: 130 us -> 51.9 us
  starting transfers between devices: 64.8 us -> 0 us
  blocking collectives: 40.6 us -> 0 us
    ppermute x45 -> x0, waiting for transfers between devices: 1270 us -> none  [partner_2(): lax.ppermute(shard, axis, [(i, i ^ 1 << stride) for i in range(lax.axis_s...]
    reduce_scatter x6 -> x0, waiting for transfers between devices: 636 us -> none  [the longest x2 280 us: body(): lax.psum_scatter(terms[11], 'fsdp', scatter_dimension=0, tiled=True)]
    pallas_call x0 -> x6, Pallas kernels: none -> 611 us  [call(): pl.pallas_call(kernel, out_shape=outs, in_specs=in_specs, out_specs=out_s...]
    dot_general x201 -> x0, matrix products: 441 us -> none  [the longest x84 180 us: product_nt(): lax.dot_general(a, b, (((1,), (1,)), ((), ())), preferred_element_type=jn...]
    unnamed x32 -> x0, waiting for transfers between devices: 343 us -> none
    all_gather x12 -> x0, waiting for transfers between devices: 269 us -> none  [the longest x2 108 us: body(): lax.all_gather(outer_weight[i], 'fsdp', axis=0, tiled=True)]
    another operation x4 -> x0, loops' own time: 79.4 us -> none  [the longest x2 63 us: attend_backward(): grad_q, grad_k, grad_v = lax.map(one_head, jnp.arange(HEADS))]
    select_n x29 -> x1, other arithmetic: 76.8 us -> 0.65 us  [slice_body(): jnp.where(branch, 0.0, MASKED)]
  transfers between devices with their start and end apart: 70 -> 0, of which waited for: 48 -> 0; matrix products, arithmetic and copies ran while one was open for 16% -> 0% of each run, Pallas kernels for 0% -> 0%
where the time goes in v1:
time: 687 us; the launch traced here: 680 us
  Pallas kernels  611 us (89%)
  local copies, waits for them, and re-layouts  51.9 us (8%)
  other arithmetic  15.6 us (2%)
    pallas_call x6, Pallas kernels, call(): pl.pallas_call(kernel, out_shape=outs, in_specs=in_specs, out_specs=out_s...  611 us

profile of v1, /device:TPU:9, one launch (start us, length us, event | category | flops | bytes accessed | tf_op | source)
XLA Modules:
  0.0 679.7 jit_solution(359565537191309042)
XLA Ops:
  0.8 0.8 reshape.243
  1.5 0.7 reshape.244
  2.3 0.7 reshape.245
  3.0 0.7 reshape.246
  3.8 0.7 reshape.247
  4.5 0.7 reshape.251
  5.2 0.7 reshape.248
  6.0 0.7 reshape.249
  6.7 0.7 reshape.250
  7.4 0.7 convert.8
  8.9 1.1 reshape.236
  10.3 1.1 stack_reshape.27
  11.4 1.1 stack_reshape.28
  13.5 0.8 convert_element_type.50.x_ref
  15.3 0.8 maximum_bitcast_fusion.col
  16.2 0.8 convert_element_type.59.dy_ref
  17.0 88.8 %shard_map.314 = (bf16[4,2,4,48,1408]{4,3,2,1,0:T(8,128)(2,1)}, bf16[4,2,192,768]{3,2,1,0:T(8,128)(2,1)}, bf16[2,4,48,768]{3,2,1,0:T(8,128)(2,1)}, bf16[4,2,4,16,128]{4,3,2,1,0:T(8,128)(2,1)}) custom-call(bf16[4,48,1408]{2,1,0:T(8,128)(2,1)} %maximum_bitcast_fusion.col, bf16[192,768]{1,0:T(8,128)(2,1)} %bitcast.190, bf16[48,768]{1,0:T(8,128)(2,1)} %bitcast.200, ...), custom_call_target="tpu_custom_call" | custom-call | flops 1000 | bytes 20000000 | tf_op jit(solution)/shard_map/pallas_call | solution.py:988
  105.8 4.6 copy.182
  111.9 0.7 broadcast_select_fusion
  113.1 0.6 select_convert_fusion.route
  117.1 1.1 pad_slice_fusion
  118.2 3.6 slice_bitcast_fusion.2
  121.7 1.6 slice_bitcast_fusion
  123.3 1.0 copy-done.1
  124.4 1.7 fusion.2
  126.1 101.5 %shard_map.315 = (f32[128,768]{1,0:T(8,128)}, bf16[4,128,768]{2,1,0:T(8,128)(2,1)}, bf16[512,384]{1,0:T(8,128)(2,1)}, bf16[4,2,512,384]{3,2,1,0:T(8,128)(2,1)}, ...) custom-call(f32[128,768]{1,0:T(8,128)} %convert_element_type.50.x_re, ...), custom_call_target="tpu_custom_call" | custom-call | flops 3000000000 | bytes 20000000 | tf_op jit(solution)/shard_map/pallas_call | solution.py:988
  227.6 94.2 %shard_map.316 = (f32[128,768]{1,0:T(8,128)}, bf16[4,128,768]{2,1,0:T(8,128)(2,1)}, bf16[512,384]{1,0:T(8,128)(2,1)}, bf16[4,2,512,384]{3,2,1,0:T(8,128)(2,1)}, ...) custom-call(f32[128,768]{1,0:T(8,128)} %get-tuple-element.65.x_ref, ...), custom_call_target="tpu_custom_call" | custom-call | flops 3000000000 | bytes 20000000 | tf_op jit(solution)/shard_map/pallas_call | solution.py:988
  321.8 1.7 convert_element_type.58
  323.5 104.1 %shard_map.317 = (f32[128,768]{1,0:T(8,128)}, bf16[768,640]{1,0:T(8,128)(2,1)}, bf16[768,768]{1,0:T(8,128)(2,1)}, bf16[768,768]{1,0:T(8,128)(2,1)}, bf16[384,768]{1,0:T(8,128)(2,1)}, /*index=5*/f32[8,768]{1,0:T(8,128)}) custom-call(f32[128,768]{1,0:T(8,128)} %convert_element_type.59.dy_ref, bf16[768,640]{1,0:T(8,128)(2,1)} %get-tuple-element.109.wqkv, ...), custom_call_target="tpu_custom_call" | custom-call | flops 6000000000 | bytes 20000000 | tf_op jit(solution)/shard_map/pallas_call | solution.py:988
  427.7 103.6 %shard_map.318 = (f32[128,768]{1,0:T(8,128)}, bf16[768,640]{1,0:T(8,128)(2,1)}, bf16[768,768]{1,0:T(8,128)(2,1)}, bf16[768,768]{1,0:T(8,128)(2,1)}, bf16[384,768]{1,0:T(8,128)(2,1)}, /*index=5*/f32[8,768]{1,0:T(8,128)}) custom-call(f32[128,768]{1,0:T(8,128)} %get-tuple-element.78.dy_ref, bf16[768,640]{1,0:T(8,128)(2,1)} %get-tuple-element.110.wqkv, ...), custom_call_target="tpu_custom_call" | custom-call | flops 6000000000 | bytes 20000000 | tf_op jit(solution)/shard_map/pallas_call | solution.py:988
  531.3 1.2 pad_maximum_fusion.1
  532.5 0.9 copy.214
  533.4 1.7 convert_element_type.60
  535.1 1.4 maximum_maximum_fusion
  536.6 2.3 copy.209
  539.7 1.6 copy.225
  541.3 118.4 %shard_map.319 = (bf16[4,48,1408]{2,1,0:T(8,128)(2,1)}, f32[192,768]{1,0:T(8,128)}, bf16[48,768]{1,0:T(8,128)(2,1)}, f32[4,16,768]{2,1,0:T(8,128)}) custom-call(bf16[2,4,192,1408]{3,2,1,0:T(8,128)(2,1)} %bitcast.151, bf16[2,4,192,768]{3,2,1,0:T(8,128)(2,1)} %bitcast.155, bf16[2,192,768]{2,1,0:T(8,128)(2,1)} %bitcast.159, f32[16,768]{1,0:T(8,128)} %maximum_bitcast_fusion.1.gsm), custom_call_target="tpu_custom_call" | custom-call | flops 1000 | bytes 20000000 | tf_op jit(solution)/shard_map/pallas_call | solution.py:988
  659.7 0.8 slice.185
  661.3 0.9 slice.189
  663.1 0.9 slice.195
  664.7 0.9 reduce_sum.21
  669.5 1.6 convert.10
  671.0 1.1 copy_bitcast_fusion.1
  672.3 0.8 reshape.277
  674.2 1.6 reshape.285
  676.7 0.9 reshape_squeeze.18
  677.7 0.9 reshape_squeeze.17
  678.7 0.8 copy.249
  (128 shorter events, 17.6 us)
Async XLA Ops:
  0.7 13.7 %copy-start.10 = (bf16[2,24,3072]{2,1,0:T(8,128)(2,1)S(1)}, bf16[2,24,3072]{2,1,0:T(8,128)(2,1)}, u32[]{:S(2)}) copy-start(bf16[2,24,3072]{2,1,0:T(8,128)(2,1)} %param.29) | copy-start | bytes 884740
  0.7 12.8 %copy-start.11 = (bf16[128,768]{1,0:T(8,128)(2,1)S(1)}, bf16[128,768]{1,0:T(8,128)(2,1)}, u32[]{:S(2)}) copy-start(bf16[128,768]{1,0:T(8,128)(2,1)} %param.19) | copy-start | bytes 589828
  12.8 3.4 copy-start.12
  105.8 4.6 copy-start.9
  105.8 4.7 copy-start.13
  110.5 1.2 copy-start.16
  117.1 4.7 copy-start
  121.7 2.5 copy-start.1
  427.7 103.6 %copy-start.7 = (bf16[384,768]{1,0:T(8,128)(2,1)S(1)}, bf16[384,768]{1,0:T(8,128)(2,1)}, u32[]{:S(2)}) copy-start(bf16[384,768]{1,0:T(8,128)(2,1)} %get-tuple-element.98) | copy-start | bytes 1769476
  531.3 3.8 copy-start.3
  531.3 3.8 copy-start.5
  531.3 3.8 copy-start.6
  536.5 2.4 copy-start.14
  536.5 2.4 copy-start.15
  536.5 3.0 copy-start.2
  536.5 3.0 copy-start.4
  675.8 2.9 copy-start.8

commit v2 on v1

--- a/solution.py
+++ b/solution.py
@@ -421,24 +421,248 @@
     def plane(self, k):
         return self.at(self.z, self.f_at(k), self.c)
 
+    def across(self, k):
+        return self.at(self.z, self.f_at(k), 1 - self.c)
+
     def column(self, k):
         return self.at(self.z_at(k), self.f, self.c)
 
     def sibling(self):
         return self.at(self.z, self.f, 1 - self.c)
-
-
-def greet(place):
-    barrier = pltpu.get_barrier_semaphore()
-    for dev in [place.plane(k) for k in (1, 2, 3)] + [place.column(k) for k in (1, 2, 3)] + [place.sibling()]:
-        pl.semaphore_signal(barrier, inc=1, device_id=(dev,), device_id_type=MESH)
-    pl.semaphore_wait(barrier, 7)
 
 
 def remote(src, dst, sems, device):
     return pltpu.make_async_remote_copy(
         src_ref=src, dst_ref=dst, send_sem=sems[0], recv_sem=sems[1], device_id=(device,), device_id_type=MESH
     )
+
+
+class Run:
+    def __init__(self, send_sems, recv_sems, local_sems):
+        self.place = Place()
+        self.sends, self.recvs, self.locals = Pool(send_sems), Pool(recv_sems), Pool(local_sems)
+        self.flying, self.saving = [], []
+
+    def greet(self, wide):
+        place = self.place
+        there = [place.plane(k) for k in (1, 2, 3)] + [place.column(k) for k in (1, 2, 3)] + [place.sibling()]
+        if wide:
+            there += [place.across(k) for k in (1, 2, 3)]
+        barrier = pltpu.get_barrier_semaphore()
+        for dev in there:
+            pl.semaphore_signal(barrier, inc=1, device_id=(dev,), device_id_type=MESH)
+        pl.semaphore_wait(barrier, len(there))
+
+    def launch(self, src, dst, device):
+        a = remote(src, dst, (self.sends.take(), self.recvs.take()), device)
+        a.start()
+        self.flying.append((None, a))
+        return a
+
+    def launch_if(self, cond, src, dst, sems, device):
+        a = remote(src, dst, sems, device)
+
+        @pl.when(cond)
+        def _():
+            a.start()
+
+        self.flying.append((cond, a))
+        return a
+
+    def local(self, src, dst):
+        a = pltpu.make_async_copy(src, dst, self.locals.take())
+        a.start()
+        return a
+
+    def save(self, src, dst):
+        self.saving.append(self.local(src, dst))
+
+    def close(self):
+        for a in self.saving:
+            a.wait()
+        for cond, a in self.flying:
+            if cond is None:
+                a.wait_send()
+            else:
+
+                @pl.when(cond)
+                def _(a=a):
+                    a.wait_send()
+
+
+class Spread:
+    def __init__(self, run, chunk, full):
+        self.run, self.chunk, self.full = run, chunk, full
+
+    def start(self):
+        run, place = self.run, self.run.place
+        mine = self.full.at[place.z, place.c]
+        self.own = run.local(self.chunk, mine)
+        self.far = [run.launch(self.chunk, mine, place.column(k)) for k in (1, 2, 3)]
+        self.near = [run.launch(self.chunk, mine, place.sibling())]
+
+    def relay(self):
+        run, place = self.run, self.run.place
+        for k in (1, 2, 3):
+            self.far[k - 1].wait_recv()
+            there = self.full.at[place.z_at(-k), place.c]
+            self.near.append(run.launch(there, there, place.sibling()))
+
+    def finish(self):
+        self.own.wait()
+        for a in self.near:
+            a.wait_recv()
+
+
+class SpreadOutput:
+    def __init__(self, run, chunk, full):
+        self.run, self.chunk = run, chunk
+        self.part = full.at[pl.ds(pl.multiple_of(run.place.c * 96, 96), 96)]
+
+    def start(self):
+        run, place = self.run, self.run.place
+        self.copy = pltpu.make_async_copy(self.chunk, self.part, run.locals.take())
+
+        @pl.when(place.f == place.z)
+        def _():
+            self.copy.start()
+
+        arrive = run.recvs.take()
+        for k in (1, 2, 3):
+            self.far = run.launch_if(
+                place.f == place.z, self.chunk, self.part, (run.sends.take(), arrive), place.column(k)
+            )
+
+    def relay(self):
+        run, place = self.run, self.run.place
+
+        @pl.when(place.f == place.z)
+        def _():
+            self.copy.wait()
+
+        @pl.when(place.f != place.z)
+        def _():
+            self.far.wait_recv()
+
+        self.near = run.launch(self.part, self.part, place.sibling())
+
+    def finish(self):
+        self.near.wait_recv()
+
+
+class Collect:
+    def __init__(self, run, part, near, far, total, out):
+        self.run, self.part, self.near, self.far, self.total, self.out = run, part, near, far, total, out
+
+    def start(self):
+        place = self.run.place
+        self.a = self.run.launch(self.part.at[1 - place.c], self.near, place.sibling())
+
+    def middle(self):
+        run, place = self.run, self.run.place
+        self.a.wait_recv()
+
+        def add(i, carry):
+            self.near[i] = (self.part[place.c, i].astype(F32) + self.near[i].astype(F32)).astype(BF)
+            return carry
+
+        lax.fori_loop(0, 4, add, 0)
+        self.moves = [
+            run.launch(self.near.at[place.z_at(k)], self.far.at[k - 1], place.column(k)) for k in (1, 2, 3)
+        ]
+
+    def end(self):
+        run, place = self.run, self.run.place
+        for a in self.moves:
+            a.wait_recv()
+        result = self.near[place.z].astype(F32)
+        for k in range(3):
+            result = result + self.far[k].astype(F32)
+        if self.total is None:
+            self.out[...] = result
+            return
+        self.total[...] = result
+        scatter_rows(self, self.total, self.out.at[place.f], None)
+
+    def last(self):
+        if self.total is None:
+            return
+        place = self.run.place
+        for k in (1, 2, 3):
+            g = place.f_at(k)
+            remote(
+                self.out.at[g], self.out.at[g], (self.send, self.arrive(g)), place.plane(k)
+            ).wait_recv()
+
+        @pl.when(place.c != place.f // 2)
+        def _():
+            remote(
+                self.out.at[place.f], self.out.at[place.f], (self.send, self.arrive(place.f)), place.sibling()
+            ).wait_recv()
+
+
+def scatter_rows(task, total, landing, cond):
+    run, place = task.run, task.run.place
+    arrive = run.recvs.block(4)
+    for j in range(4):
+        there = place.at(place.z, 2 * place.c + j // 2, j % 2)
+        here = jnp.logical_and(place.f == 2 * place.c + j // 2, place.c == j % 2)
+        away = jnp.logical_not(here)
+        if cond is not None:
+            here, away = jnp.logical_and(here, cond), jnp.logical_and(away, cond)
+        task.send = run.sends.take()
+        slot = arrive(place.f) if cond is None else arrive(0)
+        run.launch_if(away, total.at[pl.ds(24 * j, 24)], landing, (task.send, slot), there)
+
+        @pl.when(here)
+        def _(j=j):
+            landing[...] = total[24 * j : 24 * (j + 1), :]
+
+    task.arrive = arrive
+
+
+class CollectOutput:
+    def __init__(self, run, part, near, far, total, out):
+        self.run, self.part, self.near, self.far, self.total, self.out = run, part, near, far, total, out
+
+    def start(self):
+        place = self.run.place
+        self.a = self.run.launch(self.part.at[1 - place.c], self.near, place.sibling())
+
+    def middle(self):
+        run, place = self.run, self.run.place
+        self.a.wait_recv()
+        self.near[...] = (self.part[place.c].astype(F32) + self.near[...].astype(F32)).astype(BF)
+        self.slot = run.recvs.block(4)
+        self.one = run.sends.take()
+        shift = lax.rem(place.f - place.z + 4, 4)
+        run.launch_if(
+            place.f != place.z, self.near, self.far.at[shift], (self.one, self.slot(shift)),
+            place.at(place.f, place.f, place.c),
+        )
+
+    def end(self):
+        place = self.run.place
+
+        @pl.when(place.f == place.z)
+        def _():
+            result = self.near[...].astype(F32)
+            for k in (1, 2, 3):
+                remote(
+                    self.near, self.far.at[k], (self.one, self.slot(k)), place.column(k)
+                ).wait_recv()
+                result = result + self.far[k].astype(F32)
+            self.total[...] = result
+
+        scatter_rows(self, self.total, self.out, place.f == place.z)
+
+    def last(self):
+        place = self.run.place
+        mine = jnp.logical_and(place.f == place.z, place.c == place.f // 2)
+
+        @pl.when(jnp.logical_not(mine))
+        def _():
+            remote(self.out, self.out, (self.send, self.arrive(0)), place.sibling()).wait_recv()
 
 
 def norm_rows(z, gain, shift):
@@ -460,113 +684,75 @@
     return inner, jnp.sum(upstream * scaled, axis=0, keepdims=True), jnp.sum(upstream, axis=0, keepdims=True)
 
 
-def weights_kernel(
-    col, rows_out, rows_o, small, colg, outg, og, smallg, send_sems, recv_sems, local_sems
-):
-    place = Place()
+def exchange_kernel(col, rows_o, small, colp, op, smallg, send_sems, recv_sems, local_sems):
+    run = Run(send_sems, recv_sems, local_sems)
+    place = run.place
     z, f, c = place.z, place.f, place.c
-    sends, recvs, locs = Pool(send_sems), Pool(recv_sems), Pool(local_sems)
-
-    def pair():
-        return sends.take(), recvs.take()
-
-    mine = [
-        pltpu.make_async_copy(col.at[f], colg.at[z, c, f], locs.take()),
-        pltpu.make_async_copy(small, smallg.at[z, c, f], locs.take()),
-        pltpu.make_async_copy(rows_out, outg.at[z, c], locs.take()),
-    ]
-    o_copy = pltpu.make_async_copy(rows_o, og.at[c, f], locs.take())
-    for m in mine:
-        m.start()
-
-    @pl.when(f == z)
+    mine = c == f // 2
+    slot = 2 * lax.rem(f, 2) + c
+    own = pltpu.make_async_copy(col.at[f], colp.at[slot], run.locals.take())
+    own_o = pltpu.make_async_copy(rows_o, op.at[slot], run.locals.take())
+    keep = jnp.logical_and(mine, f == z)
+
+    @pl.when(mine)
     def _():
-        o_copy.start()
-
-    greet(place)
-    flying = []
-    first = []
+        own.start()
+
+    @pl.when(keep)
+    def _():
+        own_o.start()
+
+    own_small = run.local(small, smallg.at[z, c, f])
+    run.greet(True)
+    first = [run.launch(small, smallg.at[z, c, f], place.plane(k)) for k in (1, 2, 3)]
+    arrive, arrive_o = run.recvs.block(4), run.recvs.block(4)
     for k in (1, 2, 3):
-        a = remote(col.at[place.f_at(k)], colg.at[z, c, f], pair(), place.plane(k))
-        b = remote(small, smallg.at[z, c, f], pair(), place.plane(k))
-        a.start()
-        b.start()
-        first += [a, b]
-        flying += [a, b]
-    o_send, o_recv = sends.take(), recvs.block(4)
-    o_index = lax.rem(z - f + 4, 4)
-    o_first = remote(rows_o, og.at[c, f], (o_send, o_recv(o_index)), place.at(z, z, c))
-
-    @pl.when(f != z)
-    def _():
-        o_first.start()
-
-    out_moves = []
-    for k in (1, 2, 3):
-        a = remote(rows_out, outg.at[z, c], pair(), place.column(k))
-        a.start()
-        out_moves.append(a)
-    flying += out_moves
-    for m in mine:
-        m.wait()
+        run.launch_if(
+            f >= 0, col.at[place.f_at(k)], colp.at[slot], (run.sends.take(), arrive(slot)),
+            place.at(z, place.f_at(k), f // 2),
+        )
+    one = run.sends.take()
+    run.launch_if(
+        jnp.logical_not(mine), col.at[f], colp.at[slot], (one, arrive(slot)), place.sibling()
+    )
+    run.launch_if(
+        jnp.logical_not(keep), rows_o, op.at[slot], (run.sends.take(), arrive_o(slot)), place.at(z, z, f // 2)
+    )
+    own_small.wait()
     for a in first:
         a.wait_recv()
-    moves = []
+    block = smallg.at[z, c]
+    far = [run.launch(block, block, place.column(k)) for k in (1, 2, 3)]
+    near = [run.launch(block, block, place.sibling())]
     for k in (1, 2, 3):
-        a = remote(colg.at[z, c], colg.at[z, c], pair(), place.column(k))
-        b = remote(smallg.at[z, c], smallg.at[z, c], pair(), place.column(k))
-        a.start()
-        b.start()
-        moves.append((a, b))
-        flying += [a, b]
-    o_sends, o_arrive = sends.block(4), recvs.take()
-    o_moves = [
-        remote(og.at[c], og.at[c], (o_sends(k), o_arrive), place.column(k)) for k in (1, 2, 3)
-    ]
-
-    @pl.when(f == z)
+        far[k - 1].wait_recv()
+        there = smallg.at[place.z_at(-k), c]
+        near.append(run.launch(there, there, place.sibling()))
+
+    for j in range(4):
+        me = jnp.logical_and(f == 2 * c + j // 2, c == j % 2)
+        other = jnp.logical_not(me)
+
+        @pl.when(other)
+        def _(j=j):
+            remote(col.at[0], colp.at[j], (one, arrive(j)), place.sibling()).wait_recv()
+
+        @pl.when(jnp.logical_and(other, f == z))
+        def _(j=j):
+            remote(rows_o, op.at[j], (one, arrive_o(j)), place.sibling()).wait_recv()
+
+    for a in near:
+        a.wait_recv()
+
+    @pl.when(mine)
     def _():
-        o_copy.wait()
-        for k in (1, 2, 3):
-            remote(rows_o, og.at[c, f], (o_send, o_recv(k)), place.at(z, z, c)).wait_recv()
-        for m in o_moves:
-            m.start()
-
-    side = []
-
-    def hand_over(zz):
-        for ref in (colg, outg, smallg):
-            a = remote(ref.at[zz, c], ref.at[zz, c], pair(), place.sibling())
-            a.start()
-            side.append(a)
-
-    hand_over(z)
-    for k in (1, 2, 3):
-        moves[k - 1][0].wait_recv()
-        moves[k - 1][1].wait_recv()
-        out_moves[k - 1].wait_recv()
-        hand_over(place.z_at(-k))
-
-    @pl.when(f != z)
+        own.wait()
+
+    @pl.when(keep)
     def _():
-        o_moves[0].wait_recv()
-
-    a = remote(og.at[c], og.at[c], pair(), place.sibling())
-    a.start()
-    side.append(a)
-    for a in side:
-        a.wait_recv()
-    for a in flying + side:
-        a.wait_send()
-
-    @pl.when(f != z)
-    def _():
-        o_first.wait_send()
-
-    @pl.when(f == z)
-    def _():
-        for m in o_moves:
-            m.wait_send()
+        own_o.wait()
+
+    run.close()
 
 
 def pick_parents(kp, kv, route, zz, cc):
@@ -591,37 +777,51 @@
     )
 
 
-def forward_kernel(
-    x_ref, wqkv, wo, win, wout, vec, route, pen,
-    xn_ref, xb_o, qp_o, kv_o, kp_o, p_o, ctx_o, z1_o, hb_o, gp_o, gl_o, z2_o,
-    xb, qp, kv, kp, p, ctx, hb, gp, gl, z1, z2, own, rs1_s, rs1_r, rs2_s, rs2_r,
-    send_sems, recv_sems, local_sems,
-):
-    place = Place()
+def flat(ref):
+    return ref[...].reshape(-1, ref.shape[-1])
+
+
+def forward_kernel(first, *refs):
+    refs = list(refs)
+
+    def take(n):
+        out = refs[:n]
+        del refs[:n]
+        return out
+
+    x_ref, qkv_in, o_in, in_c, out_c, vec, route, pen = take(8)
+    if first:
+        qkv_next, o_next = take(2)
+    xn_ref, xb_o, qp_o, kv_o, kp_o, p_o, ctx_o, z1_o, hb_o, gp_o, gl_o, z2_o, win_o, wout_o = take(14)
+    if first:
+        wqkv_o, wo_o, wqkv_n, wo_n = take(4)
+    xb, qp, kv, kp, p, ctx, z1, hb, gp, gl, z2, win, wout, wqkv, wo, heads, own, rs1_s, rs1_r, rs2_s, rs2_r = take(21)
+    run = Run(*refs)
+    place = run.place
     z, f, c = place.z, place.f, place.c
-    sends, recvs, locs = Pool(send_sems), Pool(recv_sems), Pool(local_sems)
-    flying, saving = [], []
-
-    def launch(src, dst, device):
-        a = remote(src, dst, (sends.take(), recvs.take()), device)
-        a.start()
-        flying.append(a)
-        return a
-
-    def save(src, dst):
-        a = pltpu.make_async_copy(src, dst, locs.take())
-        a.start()
-        saving.append(a)
+    launch = run.launch
 
     xb[f] = x_ref[...].astype(BF)
-    greet(place)
+    wo[192:256, :] = jnp.zeros((64, WIDE), BF)
+    if not first:
+        loads = [run.local(qkv_in, wqkv), run.local(o_in, wo.at[pl.ds(0, 192)])]
+    run.greet(False)
     came = [None] + [launch(xb.at[f], xb.at[f], place.plane(k)) for k in (1, 2, 3)]
+    if first:
+        a_tasks = [Spread(run, qkv_in, wqkv), SpreadOutput(run, o_in, wo)]
+        for t in a_tasks:
+            t.start()
+        a_tasks[0].relay()
+        a_tasks[0].finish()
+    else:
+        for a in loads:
+            a.wait()
     lane = lax.broadcasted_iota(jnp.int32, (ROWS, 128), 1)
     for k in range(4):
         g = place.f_at(-k)
         if k:
             came[k].wait_recv()
-        qkv = product(xb[g], wqkv[...]) + vec[0:1, :PACKED]
+        qkv = product(xb[g], flat(wqkv)) + vec[0:1, :PACKED]
         rows = pl.ds(pl.multiple_of(g * ROWS, ROWS), ROWS)
         kv[z, c, rows, :] = qkv[:, 256:].astype(BF)
         scaled = qkv[:, :256] * (HEAD_DIM ** (-0.5))
@@ -631,8 +831,11 @@
         qp[rows, 256:384] = scaled[:, 128:].astype(BF)
     move = [launch(kv.at[z, c], kv.at[z, c], place.column(k)) for k in (1, 2, 3)]
     side = [launch(kv.at[z, c], kv.at[z, c], place.sibling())]
-    save(xb, xb_o)
-    save(qp, qp_o)
+    m_tasks = [Spread(run, in_c, win), Spread(run, out_c, wout)]
+    for t in m_tasks:
+        t.start()
+    run.save(xb, xb_o)
+    run.save(qp, qp_o)
     kp[...] = jnp.zeros_like(kp)
     pick_parents(kp, kv, route, z, c)
     for k in (1, 2, 3):
@@ -643,8 +846,13 @@
     for k in range(4):
         side[k].wait_recv()
         pick_parents(kp, kv, route, place.z_at(-k), 1 - c)
-    save(kp, kp_o)
-    save(kv, kv_o)
+    run.save(kp, kp_o)
+    run.save(kv, kv_o)
+    if first:
+        a_tasks[1].relay()
+        n_tasks = [Spread(run, qkv_next, wqkv_n), SpreadOutput(run, o_next, wo_n)]
+        for t in n_tasks:
+            t.start()
 
     def attend(i, carry):
         h, b = i // 4, lax.rem(i, 4)
@@ -658,82 +866,109 @@
         e = jnp.exp(s - jnp.max(s, axis=1, keepdims=True))
         pb = (e / jnp.sum(e, axis=1, keepdims=True)).astype(BF)
         p[h, b] = pb
-        ctx[rows, lanes] = product(pb, keys).astype(BF)
+        heads[h, b] = product(pb, keys)
         return carry
 
     lax.fori_loop(0, 12, attend, 0)
-    save(p, p_o)
-    save(ctx, ctx_o)
+    run.save(p, p_o)
+    if first:
+        a_tasks[1].finish()
     back = [None]
     for k in (1, 2, 3, 0):
         g = place.f_at(-k)
-        rows = pl.ds(pl.multiple_of(g * ROWS, ROWS), ROWS)
-        part = product(ctx[rows, :], wo[...])
+        ctx[g, :, 0:128] = jnp.where(lane < 64, pltpu.roll(heads[0, g], 64, 1), heads[1, g]).astype(BF)
+        ctx[g, :, 128:256] = jnp.where(lane < 64, pltpu.roll(heads[2, g], 64, 1), 0.0).astype(BF)
+        part = product(ctx[g], wo[...])
         if k:
             rs1_s[k - 1] = part.astype(BF)
             back.append(launch(rs1_s.at[k - 1], rs1_r.at[k - 1], place.plane(-k)))
         else:
             own[...] = part
+    run.save(ctx, ctx_o)
+    for t in m_tasks:
+        t.relay()
     for k in (1, 2, 3):
         back[k].wait_recv()
     total = own[...] + rs1_r[0].astype(F32) + rs1_r[1].astype(F32) + rs1_r[2].astype(F32)
     zz = x_ref[...] + total + vec[1:2, :]
     z1[...] = zz
-    save(z1, z1_o)
+    run.save(z1, z1_o)
     hidden = norm_rows(zz, vec[2:3, :], vec[3:4, :])
     hb[f] = hidden.astype(BF)
     came = [None] + [launch(hb.at[f], hb.at[f], place.plane(k)) for k in (1, 2, 3)]
     back = [None]
+    for t in m_tasks:
+        t.finish()
     for k in range(4):
         g = place.f_at(-k)
         if k:
             came[k].wait_recv()
-        u = product(hb[g], win[...]) + vec[4:5, :]
+        u = product(hb[g], flat(win)) + vec[4:5, :]
         cdf = 0.5 * (1.0 + lax.erf(u * (0.5 ** 0.5)))
         gp[g] = cdf + u * jnp.exp(-0.5 * u * u) * 0.3989422804014327
         low = (u * cdf).astype(BF)
         gl[g] = low
-        part = product(low, wout[...])
+        part = product(low, flat(wout))
         if k:
             rs2_s[k - 1] = part.astype(BF)
             back.append(launch(rs2_s.at[k - 1], rs2_r.at[k - 1], place.plane(-k)))
         else:
             own[...] = part
-    save(hb, hb_o)
-    save(gp, gp_o)
-    save(gl, gl_o)
+    run.save(hb, hb_o)
+    run.save(gp, gp_o)
+    run.save(gl, gl_o)
+    run.save(win, win_o)
+    run.save(wout, wout_o)
+    if first:
+        run.save(wqkv, wqkv_o)
+        run.save(wo.at[pl.ds(0, 192)], wo_o)
+        for t in n_tasks:
+            t.relay()
     for k in (1, 2, 3):
         back[k].wait_recv()
     total = own[...] + rs2_r[0].astype(F32) + rs2_r[1].astype(F32) + rs2_r[2].astype(F32)
     zz = norm_rows(z1[...], vec[2:3, :], vec[3:4, :]) + total + vec[5:6, :]
     z2[...] = zz
-    save(z2, z2_o)
+    run.save(z2, z2_o)
     xn_ref[...] = norm_rows(zz, vec[6:7, :], vec[7:8, :])
-    for a in saving:
-        a.wait()
-    for a in flying:
-        a.wait_send()
-
-
-def backward_kernel(
-    dy_ref, wqkv, wo, win, wout, vec, route, xb, qp, kv, kp, p, ctx, z1, hb, gp, gl, z2,
-    dx_ref, dqkv_o, din_o, dout_o, do_o, dvec_o,
-    df, du, da, dctx, dqf, dqkv, dz, dz1, dkt, dself, dpar, tgt, tgt_r, summed, summed_r,
-    own, rs1_s, rs1_r, rs2_s, rs2_r, send_sems, recv_sems,
-):
-    place = Place()
+    if first:
+        for t in n_tasks:
+            t.finish()
+    run.close()
+
+
+def backward_kernel(extra, *refs):
+    refs = list(refs)
+
+    def take(n):
+        out = refs[:n]
+        del refs[:n]
+        return out
+
+    dy_ref, win, wout, vec, route, z1, hb, gp, gl, z2 = take(10)
+    late_in = take(8)
+    if extra:
+        pq_in, po_in = take(2)
+    dx_ref, pq, po, din_o, dout_o, dvec_o = take(6)
+    if extra:
+        dqkv_o, do_o = take(2)
+    late = take(8)
+    wqkv, wo, xb, qp, kv, kp, p, ctx = late
+    (
+        df, du, da, dctx, dqf, dqkv, dz, dz1, dkt, dself, dpar, tgt, tgt_r, summed, summed_r,
+        own, rs1_s, rs1_r, rs2_s, rs2_r,
+    ) = take(20)
+    pin, nin, fin, tin, pout, nout, fout = take(7)
+    if extra:
+        nq, fq, tq, no, fo, to = take(6)
+    run = Run(*refs)
+    place = run.place
     z, f, c = place.z, place.f, place.c
-    sends, recvs = Pool(send_sems), Pool(recv_sems)
-    flying = []
-
-    def launch(src, dst, device):
-        a = remote(src, dst, (sends.take(), recvs.take()), device)
-        a.start()
-        flying.append(a)
-        return a
-
-    def whole(ref):
-        return ref[...].reshape(4 * ROWS, ref.shape[-1])
+    launch = run.launch
+    loads = []
+    for n, (src, dst) in enumerate(zip(late_in, late)):
+        loads.append(run.local(src, dst.at[pl.ds(0, 192)] if n == 1 else dst))
+    wo[192:256, :] = jnp.zeros((64, WIDE), BF)
 
     grad, dgain, dshift = norm_rows_back(z2[...], vec[6:7, :], dy_ref[...])
     dvec_o[6:7, :] = dgain
@@ -742,32 +977,49 @@
     low = grad.astype(BF)
     df[f] = low
     dvec_o[5:6, :] = jnp.sum(low.astype(F32), axis=0, keepdims=True)
-    greet(place)
+    run.greet(True)
     came = [None] + [launch(df.at[f], df.at[f], place.plane(k)) for k in (1, 2, 3)]
+    a_tasks = []
+    if extra:
+        a_tasks = [Collect(run, pq_in, nq, fq, tq, dqkv_o), CollectOutput(run, po_in, no, fo, to, do_o)]
+    for t in a_tasks:
+        t.start()
     back = [None]
     bias = jnp.zeros((1, WIDE), F32)
     for k in range(4):
         g = place.f_at(-k)
         if k:
             came[k].wait_recv()
-        low = (product_nt(df[g], wout[...]) * gp[g]).astype(BF)
+        low = (product_nt(df[g], flat(wout)) * gp[g]).astype(BF)
         du[g] = low
         bias = bias + jnp.sum(low.astype(F32), axis=0, keepdims=True)
-        part = product_nt(low, win[...])
+        part = product_nt(low, flat(win))
         if k:
             rs1_s[k - 1] = part.astype(BF)
             back.append(launch(rs1_s.at[k - 1], rs1_r.at[k - 1], place.plane(-k)))
         else:
             own[...] = part
+            for t in a_tasks:
+                t.middle()
     dvec_o[4:5, :] = bias
+    m_tasks = [Collect(run, pin, nin, fin, tin, din_o), Collect(run, pout, nout, fout, None, dout_o)]
+
+    def split_rows(dst, left, right, i):
+        lanes = pl.ds(pl.multiple_of(i * 384, 128), 384)
+        value = product_tn(left[:, :, lanes].reshape(512, 384), flat(right)).astype(BF)
+        for zz in range(2):
+            for cc in range(2):
+                at = (2 * zz + cc) * 96
+                dst[cc, 2 * i + zz] = value[at : at + 96, :]
 
     def ffn_grads(i, carry):
-        lanes = pl.ds(pl.multiple_of(i * 256, 256), 256)
-        dout_o[lanes, :] = product_tn(gl[:, :, lanes].reshape(512, 256), whole(df)).astype(BF)
-        din_o[lanes, :] = product_tn(hb[:, :, lanes].reshape(512, 256), whole(du)).astype(BF)
+        split_rows(pout, gl, df, i)
+        split_rows(pin, hb, du, i)
         return carry
 
-    lax.fori_loop(0, 3, ffn_grads, 0)
+    lax.fori_loop(0, 2, ffn_grads, 0)
+    for t in m_tasks:
+        t.start()
     for k in (1, 2, 3):
         back[k].wait_recv()
     up = dz[...] + own[...] + rs1_r[0].astype(F32) + rs1_r[1].astype(F32) + rs1_r[2].astype(F32)
@@ -779,13 +1031,24 @@
     da[f] = low
     dvec_o[1:2, :] = jnp.sum(low.astype(F32), axis=0, keepdims=True)
     came = [None] + [launch(da.at[f], da.at[f], place.plane(k)) for k in (1, 2, 3)]
+    for t in a_tasks:
+        t.end()
+    for t in m_tasks:
+        t.middle()
     dkt[...] = jnp.zeros_like(dkt)
+    lane = lax.broadcasted_iota(jnp.int32, (ROWS, 128), 1)
+    for a in loads:
+        a.wait()
     for k in range(4):
         g = place.f_at(-k)
         rows = pl.ds(pl.multiple_of(g * ROWS, ROWS), ROWS)
         if k:
             came[k].wait_recv()
-        dctx[rows, :] = product_nt(da[g], wo[...]).astype(BF)
+        packed = product_nt(da[g], wo[...])
+        ahead, after = packed[:, :128], packed[:, 128:]
+        dctx[rows, 0:128] = jnp.where(lane < 64, 0.0, pltpu.roll(ahead, 64, 1)).astype(BF)
+        dctx[rows, 128:256] = jnp.where(lane < 64, 0.0, ahead).astype(BF)
+        dctx[rows, 256:384] = jnp.where(lane < 64, 0.0, pltpu.roll(after, 64, 1)).astype(BF)
 
     def attend(i, carry):
         h, b = i // 4, lax.rem(i, 4)
@@ -823,17 +1086,18 @@
 
     lax.fori_loop(0, 12, scatter, 0)
     near = launch(tgt.at[1 - c], tgt_r, place.sibling())
-    lane = lax.broadcasted_iota(jnp.int32, (ROWS, 128), 1)
     for g in range(4):
         rows = slice(g * ROWS, (g + 1) * ROWS)
-        first = jnp.where(lane < 64, dqf[0, rows, :], pltpu.roll(dqf[1, rows, :], 64, 1))
-        dqkv[g, :, 0:128] = first.astype(BF)
+        ahead = jnp.where(lane < 64, dqf[0, rows, :], pltpu.roll(dqf[1, rows, :], 64, 1))
+        dqkv[g, :, 0:128] = ahead.astype(BF)
         dqkv[g, :, 128:256] = jnp.where(lane < 64, dqf[2, rows, :], 0.0).astype(BF)
     near.wait_recv()
     for zt in range(4):
         summed[zt] = (tgt[c, zt].astype(F32) + tgt_r[zt].astype(F32)).astype(BF)
     far = [launch(summed.at[place.z_at(k)], summed_r.at[k - 1], place.column(k)) for k in (1, 2, 3)]
-    do_o[...] = product_tn(ctx[...], whole(da)).astype(BF)
+    value = product_tn(flat(ctx), flat(da)).astype(BF)
+    for cc in range(2):
+        po[cc] = value[96 * cc : 96 * (cc + 1), :]
     for a in far:
         a.wait_recv()
     total = summed[z].astype(F32) + summed_r[0].astype(F32) + summed_r[1].astype(F32) + summed_r[2].astype(F32)
@@ -842,7 +1106,7 @@
     back = [None]
     for k in (1, 2, 3, 0):
         g = place.f_at(-k)
-        part = product_nt(dqkv[g], wqkv[...])
+        part = product_nt(dqkv[g], flat(wqkv))
         if k:
             rs2_s[k - 1] = part.astype(BF)
             back.append(launch(rs2_s.at[k - 1], rs2_r.at[k - 1], place.plane(-k)))
@@ -850,148 +1114,74 @@
             own[...] = part
 
     def qkv_grads(i, carry):
-        lanes = pl.ds(pl.multiple_of(i * 256, 256), 256)
-        dqkv_o[lanes, :] = product_tn(xb[:, :, lanes].reshape(512, 256), whole(dqkv)).astype(BF)
+        split_rows(pq, xb, dqkv, i)
         return carry
 
-    lax.fori_loop(0, 3, qkv_grads, 0)
-    sums = jnp.sum(whole(dqkv).astype(F32), axis=0, keepdims=True)
+    lax.fori_loop(0, 2, qkv_grads, 0)
+    sums = jnp.sum(flat(dqkv).astype(F32), axis=0, keepdims=True)
     dvec_o[0:1, :] = jnp.concatenate([sums, jnp.zeros((1, WIDE - PACKED), F32)], axis=1)
+    for t in m_tasks:
+        t.end()
+    for t in a_tasks:
+        t.last()
     for k in (1, 2, 3):
         back[k].wait_recv()
     dx_ref[...] = dz1[...] + own[...] + rs2_r[0].astype(F32) + rs2_r[1].astype(F32) + rs2_r[2].astype(F32)
-    for a in flying:
-        a.wait_send()
+    for t in m_tasks:
+        t.last()
+    run.close()
 
 
 def reduce_kernel(
-    gcol, gout, go, gsm, col_o, out_o, o_o, sm_o,
-    col_a, out_a, o_a, sm_a, col_u, out_u, o_u, sm_u, col_b, out_b, o_b, sm_b, col_v, o_v, sm_v,
-    send_sems, recv_sems,
+    pq, po, gsm, dqkv_o, do_o, sm_o, nq, fq, tq, no, fo, to, sm_a, sm_u, sm_b, sm_v, send_sems, recv_sems, local_sems
 ):
-    place = Place()
-    z, f, c = place.z, place.f, place.c
-    sends, recvs = Pool(send_sems), Pool(recv_sems)
-    flying = []
-
-    def launch(src, dst, device):
-        a = remote(src, dst, (sends.take(), recvs.take()), device)
-        a.start()
-        flying.append(a)
-        return a
-
-    greet(place)
-    sib = place.sibling()
-    near = [
-        launch(gcol.at[1 - c], col_a, sib),
-        launch(gout.at[1 - c], out_a, sib),
-        launch(go.at[1 - c], o_a, sib),
-        launch(gsm, sm_a, sib),
-    ]
-    for a in near:
-        a.wait_recv()
+    run = Run(send_sems, recv_sems, local_sems)
+    place = run.place
+    f = place.f
+    launch = run.launch
+    run.greet(True)
+    tasks = [Collect(run, pq, nq, fq, tq, dqkv_o), CollectOutput(run, po, no, fo, to, do_o)]
+    for t in tasks:
+        t.start()
+    a = launch(gsm, sm_a, place.sibling())
+    for t in tasks:
+        t.middle()
+    a.wait_recv()
     sm_u[...] = gsm[...] + sm_a[...]
-    o_u[...] = (go[c].astype(F32) + o_a[...].astype(F32)).astype(BF)
-
-    def chip_sum(i, carry):
-        col_u[i] = (gcol[c, i].astype(F32) + col_a[i].astype(F32)).astype(BF)
-        out_u[i] = (gout[c, i].astype(F32) + out_a[i].astype(F32)).astype(BF)
-        return carry
-
-    lax.fori_loop(0, 4, chip_sum, 0)
-    far = []
-    for k in (1, 2, 3):
-        there = place.z_at(k)
-        far.append(launch(col_u.at[there], col_b.at[k - 1], place.column(k)))
-        far.append(launch(out_u.at[there], out_b.at[k - 1], place.column(k)))
-        far.append(launch(sm_u, sm_b.at[k - 1], place.column(k)))
-    o_send, o_recv = sends.take(), recvs.block(4)
-    shift = lax.rem(f - z + 4, 4)
-    o_far = remote(o_u, o_b.at[shift], (o_send, o_recv(shift)), place.at(f, f, c))
-
-    @pl.when(f != z)
-    def _():
-        o_far.start()
-
-    @pl.when(f == z)
-    def _():
-        for k in (1, 2, 3):
-            remote(o_u, o_b.at[k], (o_send, o_recv(k)), place.at(f, f, c)).wait_recv()
-        for g in range(4):
-            rows = slice(g * 48, (g + 1) * 48)
-            o_v[g] = (
-                o_u[rows, :].astype(F32)
-                + o_b[1, rows, :].astype(F32)
-                + o_b[2, rows, :].astype(F32)
-                + o_b[3, rows, :].astype(F32)
-            ).astype(BF)
-
+    far = [launch(sm_u, sm_b.at[k - 1], place.column(k)) for k in (1, 2, 3)]
     for a in far:
         a.wait_recv()
     sm_v[...] = sm_u[...] + sm_b[0] + sm_b[1] + sm_b[2]
-    out_o[...] = out_u[z].astype(F32) + out_b[0].astype(F32) + out_b[1].astype(F32) + out_b[2].astype(F32)
-    for g in range(4):
-        rows = slice(g * 48, (g + 1) * 48)
-        col_v[g] = (
-            col_u[z, rows, :].astype(F32)
-            + col_b[0, rows, :].astype(F32)
-            + col_b[1, rows, :].astype(F32)
-            + col_b[2, rows, :].astype(F32)
-        ).astype(BF)
-    last = []
-    for k in (1, 2, 3):
-        last.append(launch(col_v.at[place.f_at(k)], col_o.at[f], place.plane(k)))
-        last.append(launch(sm_v, sm_o.at[f], place.plane(k)))
-    col_o[f] = col_v[f]
+    last = [launch(sm_v, sm_o.at[f], place.plane(k)) for k in (1, 2, 3)]
     sm_o[f] = sm_v[...]
-    o_sends, o_last = sends.block(4), recvs.take()
-    moves = [
-        remote(o_v.at[place.f_at(k)], o_o, (o_sends(k), o_last), place.plane(k)) for k in (1, 2, 3)
-    ]
-
-    @pl.when(f == z)
-    def _():
-        for m in moves:
-            m.start()
-        o_o[...] = o_v[f]
-
-    @pl.when(f != z)
-    def _():
-        moves[0].wait_recv()
-
+    for t in tasks:
+        t.end()
     for a in last:
         a.wait_recv()
-    for a in flying:
-        a.wait_send()
-
-    @pl.when(f != z)
-    def _():
-        o_far.wait_send()
-
-    @pl.when(f == z)
-    def _():
-        for m in moves:
-            m.wait_send()
+    for t in tasks:
+        t.last()
+    run.close()
 
 
 ANY = pl.BlockSpec(memory_space=pl.ANY)
 VM = pl.BlockSpec(memory_space=pltpu.VMEM)
 SM = pl.BlockSpec(memory_space=pltpu.SMEM)
 LIMIT = 60 * 1024 * 1024
+SEMS = (128, 128, 32)
 
 
 def shape(*dims, dtype=BF):
     return jax.ShapeDtypeStruct(dims, dtype)
 
 
-def call(kernel, number, outs, out_specs, in_specs, scratch, sems, args, flops):
+def call(kernel, number, outs, out_specs, in_specs, scratch, args, flops):
     return pl.pallas_call(
         kernel,
-        out_shape=outs,
+        out_shape=tuple(outs),
         in_specs=in_specs,
-        out_specs=out_specs,
+        out_specs=tuple(out_specs),
         scratch_shapes=[pltpu.VMEM(s.shape, s.dtype) for s in scratch]
-        + [pltpu.SemaphoreType.DMA((n,)) for n in sems],
+        + [pltpu.SemaphoreType.DMA((n,)) for n in SEMS],
         compiler_params=pltpu.CompilerParams(
             collective_id=number, has_side_effects=True, vmem_limit_bytes=LIMIT
         ),
@@ -1008,58 +1198,71 @@
     return jnp.concatenate([q, kv, up], axis=2).transpose(1, 0, 2)
 
 
-def gather_weights(col, rows_out, rows_o, small):
+LOCAL = shape(ROWS, WIDE, dtype=F32)
+FULL = shape(4, ROWS, WIDE)
+PIECE = shape(3, ROWS, WIDE)
+QKV = shape(4, 2, 96, PACKED)
+BIG = shape(4, 2, 96, WIDE)
+OUTPUT = shape(192, WIDE)
+SAVED = (
+    FULL, shape(512, SLICE), shape(4, 2, 512, SLICE), shape(4, 2, ROWS, SLICE), shape(3, 4, ROWS, NKEYS),
+    shape(4, ROWS, 256), LOCAL, FULL, shape(4, ROWS, WIDE, dtype=F32), FULL, LOCAL,
+)
+
+
+def forward_layer(first, state, qkv, o, in_c, out_c, vec, route, pen, following):
+    outs = (LOCAL,) + SAVED + (BIG, BIG) + ((QKV, OUTPUT, QKV, OUTPUT) if first else ())
+    got = call(
+        lambda *refs: forward_kernel(first, *refs), 1 if first else 2, outs, (VM,) + (ANY,) * (len(outs) - 1),
+        [VM] + [ANY] * 4 + [VM] + [SM] * 2 + [ANY] * len(following),
+        list(SAVED)
+        + [BIG, BIG, QKV, shape(256, WIDE), shape(3, 4, ROWS, 128, dtype=F32), LOCAL]
+        + [PIECE] * 4,
+        (state, qkv, o, in_c, out_c, vec, route, pen) + tuple(following), 3 * 10**9,
+    )
+    return got[0], got[1:12], got[12:]
+
+
+def collect_scratch(columns, rows):
+    return [shape(4, 96, columns), shape(3, 96, columns)] + ([shape(96, columns, dtype=F32)] if rows else [])
+
+
+OUT_SCRATCH = [shape(96, WIDE), shape(4, 96, WIDE), shape(96, WIDE, dtype=F32)]
+PARTS = (shape(2, 4, 96, PACKED), shape(2, 96, WIDE))
+SHARES = (shape(4, 24, PACKED, dtype=F32), shape(24, WIDE, dtype=F32))
+
+
+def backward_layer(upstream, weights, vec, route, saved, before):
+    wqkv, wo, win, wout = weights
+    xb, qp, kv, kp, p, ctx, z1, hb, gp, gl, z2 = saved
+    keys = shape(4, 256, SLICE, dtype=F32)
+    extra = len(before) > 0
+    outs = (LOCAL,) + PARTS + (
+        shape(4, 24, WIDE, dtype=F32), shape(96, WIDE, dtype=F32), shape(8, WIDE, dtype=F32)
+    ) + (SHARES if extra else ())
+    late = [QKV, shape(256, WIDE)] + [SAVED[i] for i in range(6)]
+    scratch = late + [
+        FULL, FULL, FULL, shape(512, SLICE), shape(3, 512, 128, dtype=F32), shape(4, ROWS, PACKED), LOCAL, LOCAL,
+        shape(1024, SLICE, dtype=F32), keys, keys, shape(2, 4, 512, SLICE), shape(4, 512, SLICE),
+        shape(4, 512, SLICE), shape(3, 512, SLICE), LOCAL, PIECE, PIECE, PIECE, PIECE,
+    ]
+    scratch += [shape(2, 4, 96, WIDE)] + collect_scratch(WIDE, True) + [shape(2, 4, 96, WIDE)] + collect_scratch(WIDE, False)
+    if extra:
+        scratch += collect_scratch(PACKED, True) + OUT_SCRATCH
     return call(
-        weights_kernel, 0,
-        (shape(4, 2, 4, 48, 1408), shape(4, 2, 192, WIDE), shape(2, 4, 48, WIDE), shape(4, 2, 4, 16, 128)),
-        (ANY,) * 4, [ANY] * 4, [], (64, 64, 8), (col, rows_out, rows_o, small), 1000,
-    )
-
-
-def forward_layer(state, weights, vec, route, pen):
-    wqkv, wo, win, wout = weights
-    saved = (
-        shape(4, ROWS, WIDE), shape(512, SLICE), shape(4, 2, 512, SLICE), shape(4, 2, ROWS, SLICE), shape(3, 4, ROWS, NKEYS),
-        shape(512, SLICE), shape(ROWS, WIDE, dtype=F32), shape(4, ROWS, WIDE), shape(4, ROWS, WIDE, dtype=F32),
-        shape(4, ROWS, WIDE), shape(ROWS, WIDE, dtype=F32),
-    )
-    xb, qp, kv, kp, p, ctx, z1, hb, gp, gl, z2 = saved
-    piece = shape(3, ROWS, WIDE)
-    outs = call(
-        forward_kernel, 1, (shape(ROWS, WIDE, dtype=F32),) + saved, (VM,) + (ANY,) * 11,
-        [VM] * 6 + [SM] * 2,
-        [xb, qp, kv, kp, p, ctx, hb, gp, gl, z1, z2, shape(ROWS, WIDE, dtype=F32)] + [piece] * 4,
-        (48, 48, 16), (state, wqkv, wo, win, wout, vec, route, pen), 3 * 10**9,
-    )
-    return outs[0], outs[1:]
-
-
-def backward_layer(upstream, weights, vec, route, saved):
-    wqkv, wo, win, wout = weights
-    local = shape(ROWS, WIDE, dtype=F32)
-    full = shape(4, ROWS, WIDE)
-    piece = shape(3, ROWS, WIDE)
-    keys = shape(4, 256, SLICE, dtype=F32)
+        lambda *refs: backward_kernel(extra, *refs), 4 if extra else 3, outs, (VM,) * len(outs),
+        [VM] * 4 + [SM] + [VM] * 5 + [ANY] * 8 + [VM] * len(before), scratch,
+        (upstream, win, wout, vec, route, z1, hb, gp, gl, z2, wqkv, wo, xb, qp, kv, kp, p, ctx) + tuple(before),
+        6 * 10**9,
+    )
+
+
+def reduce_rest(pq, po, gsm):
+    sm = shape(16, WIDE, dtype=F32)
     return call(
-        backward_kernel, 2,
-        (local, shape(WIDE, PACKED), shape(WIDE, WIDE), shape(WIDE, WIDE), shape(SLICE, WIDE), shape(8, WIDE, dtype=F32)),
-        (VM,) * 6, [VM] * 6 + [SM] + [VM] * 11,
-        [full, full, full, shape(512, SLICE), shape(3, 512, 128, dtype=F32), shape(4, ROWS, PACKED), local, local,
-         shape(1024, SLICE, dtype=F32), keys, keys, shape(2, 4, 512, SLICE), shape(4, 512, SLICE),
-         shape(4, 512, SLICE), shape(3, 512, SLICE), local, piece, piece, piece, piece],
-        (48, 48), (upstream, wqkv, wo, win, wout, vec, route) + tuple(saved), 6 * 10**9,
-    )
-
-
-def reduce_grads(gcol, gout, go, gsm):
-    half = [shape(4, 192, 1408), shape(4, 192, WIDE), shape(192, WIDE), shape(16, WIDE, dtype=F32)]
-    far = [shape(3, 192, 1408), shape(3, 192, WIDE), shape(4, 192, WIDE), shape(3, 16, WIDE, dtype=F32)]
-    return call(
-        reduce_kernel, 3,
-        (shape(4, 48, 1408), shape(192, WIDE, dtype=F32), shape(48, WIDE), shape(4, 16, WIDE, dtype=F32)),
-        (VM,) * 4, [VM] * 4,
-        half + half + far + [shape(4, 48, 1408), shape(4, 48, WIDE), shape(16, WIDE, dtype=F32)],
-        (64, 64), (gcol, gout, go, gsm), 1000,
+        reduce_kernel, 5, SHARES + (shape(4, 16, WIDE, dtype=F32),), (VM,) * 3, [VM] * 3,
+        collect_scratch(PACKED, True) + OUT_SCRATCH + [sm, sm, shape(3, 16, WIDE, dtype=F32), sm],
+        (pq, po, gsm), 1000,
     )
 
 
@@ -1074,17 +1277,16 @@
     vectors = (query_bias, value_bias, output_bias, first_gain, first_shift, outer_bias, second_gain, second_shift)
     small = jnp.concatenate([v.reshape(-1) for v in vectors] + [inner_bias.reshape(-1), segments[:1].astype(BF)])
     small = jnp.pad(small, (0, 2048 - small.shape[0])).reshape(16, 128)
-    colg, outg, og, smallg = gather_weights(
-        col, outer_weight.reshape(192, WIDE), output_weight.reshape(48, WIDE), small
-    )
-    wide = colg.reshape(4, 2, 4, 2, 24, 1408).transpose(3, 0, 2, 1, 4, 5).reshape(2, WIDE, 1408)
-    outer = outg.reshape(4, 2, 2, 96, WIDE).transpose(2, 0, 1, 3, 4).reshape(2, WIDE, WIDE)
-    o_rows = og.reshape(2, 4, 2, 24, WIDE).transpose(2, 1, 0, 3, 4).reshape(2, 3, 64, WIDE)
-    o_rows = jnp.pad(o_rows, ((0, 0), (0, 0), (64, 0), (0, 0))).reshape(2, SLICE, WIDE)
-    flat = smallg.transpose(0, 2, 1, 3, 4).reshape(32, 2048).astype(F32)
-    parts = [flat[:, i * 48 : (i + 1) * 48].reshape(32, 2, 24).transpose(1, 0, 2).reshape(2, WIDE) for i in range(8)]
+    colp, op, smallg = call(
+        exchange_kernel, 0, (shape(4, 48, 1408), shape(4, 48, WIDE), shape(4, 2, 4, 16, 128)), (ANY,) * 3, [ANY] * 3,
+        [], (col, output_weight.reshape(48, WIDE), small), 1000,
+    )
+    colp = colp.reshape(4, 2, 24, 1408).transpose(1, 0, 2, 3).reshape(2, 96, 1408)
+    op = op.reshape(4, 2, 24, WIDE).transpose(1, 0, 2, 3).reshape(2, 96, WIDE)
+    small = smallg.transpose(0, 2, 1, 3, 4).reshape(32, 2048).astype(F32)
+    parts = [small[:, i * 48 : (i + 1) * 48].reshape(32, 2, 24).transpose(1, 0, 2).reshape(2, WIDE) for i in range(8)]
     q_all, v_all, o_all, g1, s1, out_all, g2, s2 = parts
-    in_all = flat[:, 384:576].reshape(4, 4, 2, 2, 96)
+    in_all = small[:, 384:576].reshape(4, 4, 2, 2, 96)
     in_mine = lax.dynamic_index_in_dim(in_all, f, 1, keepdims=False).transpose(2, 0, 1, 3).reshape(2, WIDE)
     q_mine = lax.dynamic_slice_in_dim(q_all, 192 * f, 192, 1)
     v_mine = lax.dynamic_slice_in_dim(v_all, 192 * f, 192, 1).reshape(2, 3, 64)
@@ -1092,7 +1294,7 @@
     qkv_mine = jnp.pad(jnp.concatenate([q_mine, jnp.zeros((2, 64), F32), kv_mine], axis=1), ((0, 0), (0, WIDE - PACKED)))
     vecs = jnp.stack([qkv_mine, o_all, g1, s1, in_mine, out_all, g2, s2], axis=1)
 
-    labels = flat[:, 576].reshape(16, 2)[:, 0].astype(jnp.int32)
+    labels = small[:, 576].reshape(16, 2)[:, 0].astype(jnp.int32)
     mine = lax.dynamic_slice_in_dim(labels, 4 * z, 4, 0)
     parent = lookup_rows(mine, parents)
     match = (parent[:, None] == labels[None, :]).astype(jnp.int32)
@@ -1102,32 +1304,28 @@
     ).astype(F32)
     route = jnp.where(branch[:, None], match, 0).astype(F32)
 
-    state = activations.astype(F32)
-    saved = []
-    weights = []
-    for i in range(LAYERS):
-        weights.append((wide[i, :, :PACKED], o_rows[i], wide[i, :, PACKED:], outer[i]))
-        state, kept = forward_layer(state, weights[i], vecs[i], route, pen)
-        saved.append(kept)
+    qkv_c = [colp[i, :, :PACKED] for i in range(2)]
+    in_c = [colp[i, :, PACKED:] for i in range(2)]
+    state, kept0, (win0, wout0, wqkv0, wo0, wqkv1, wo1) = forward_layer(
+        True, activations.astype(F32), qkv_c[0], op[0], in_c[0], outer_weight[0], vecs[0], route, pen, (qkv_c[1], op[1])
+    )
+    state, kept1, (win1, wout1) = forward_layer(
+        False, state, wqkv1, wo1, in_c[1], outer_weight[1], vecs[1], route, pen, ()
+    )
     outcome = state.astype(BF)
-    upstream = cotangent.astype(F32)
-    grads = [None] * LAYERS
-    for i in reversed(range(LAYERS)):
-        upstream, *grads[i] = backward_layer(upstream, weights[i], vecs[i], route, saved[i])
-
-    dqkv, din, dout, do, dvec = (jnp.stack([grads[0][j], grads[1][j]]) for j in range(5))
-    gcol = jnp.concatenate([dqkv, din], axis=2).reshape(2, 4, 4, 2, 24, 1408)
-    gcol = gcol.transpose(3, 1, 2, 0, 4, 5).reshape(2, 4, 192, 1408)
-    gout = dout.reshape(2, 4, 2, 96, WIDE).transpose(2, 1, 0, 3, 4).reshape(2, 4, 192, WIDE)
-    go = do.reshape(2, 3, 2, 64, WIDE)[:, :, 1].reshape(2, 4, 2, 24, WIDE)
-    go = go.transpose(2, 1, 0, 3, 4).reshape(2, 192, WIDE)
-    rcol, rout, ro, rsm = reduce_grads(gcol, gout, go, dvec.reshape(16, WIDE))
-    rcol = rcol.astype(F32).reshape(4, 2, 24, 1408).transpose(1, 2, 0, 3)
-    dq = rcol[..., :192].reshape(2, 24, WIDE)
-    dkv = rcol[..., 256:640].reshape(2, 24, 4, 3, 2, 64)
+    upstream, pq, po, din1, dout1, dvec1 = backward_layer(
+        cotangent.astype(F32), (wqkv1, wo1, win1, wout1), vecs[1], route, kept1, ()
+    )
+    upstream, pq, po, din0, dout0, dvec0, dqkv1, do1 = backward_layer(
+        upstream, (wqkv0, wo0, win0, wout0), vecs[0], route, kept0, (pq, po)
+    )
+    dqkv0, do0, rsm = reduce_rest(pq, po, jnp.concatenate([dvec0, dvec1]))
+    dqkv = jnp.stack([dqkv0, dqkv1]).transpose(0, 2, 1, 3)
+    dq = dqkv[..., :192].reshape(2, 24, WIDE)
+    dkv = dqkv[..., 256:].reshape(2, 24, 4, 3, 2, 64)
     dk = dkv[..., 0, :].reshape(2, 24, WIDE)
     dv = dkv[..., 1, :].reshape(2, 24, WIDE)
-    dinner = rcol[..., 640:].reshape(2, 24, 4, 4, 192).transpose(0, 1, 3, 2, 4).reshape(2, 24, 3072)
+    dinner = jnp.stack([din0, din1]).reshape(2, 4, 24, 4, 192).transpose(0, 2, 3, 1, 4).reshape(2, 24, 3072)
     rsm = rsm.reshape(4, 2, 8, WIDE)
     sums = jnp.sum(rsm, axis=0)
     at = 24 * (8 * z + 2 * f + c)
@@ -1141,8 +1339,8 @@
     dib = lax.dynamic_slice_in_dim(dib, 96 * (2 * z + c), 96, 1)
     return (
         outcome, upstream.astype(BF), dq, own_part(dqb), dk, dv, own_part(dvb),
-        ro.astype(F32).reshape(2, 24, WIDE), own_part(sums[:, 1]), own_part(sums[:, 2]), own_part(sums[:, 3]),
-        dinner, dib, rout.reshape(2, 96, WIDE), own_part(sums[:, 5]), own_part(sums[:, 6]), own_part(sums[:, 7]),
+        jnp.stack([do0, do1]), own_part(sums[:, 1]), own_part(sums[:, 2]), own_part(sums[:, 3]),
+        dinner, dib, jnp.stack([dout0, dout1]), own_part(sums[:, 5]), own_part(sums[:, 6]), own_part(sums[:, 7]),
     )
 
 

time: 687 us -> 555 us (0.81)
  Pallas kernels: 611 us -> 502 us
  local copies, waits for them, and re-layouts: 51.9 us -> 31.6 us
    pallas_call x6, Pallas kernels: 611 us -> 502 us  [call(): pl.pallas_call(kernel, out_shape=tuple(outs), in_specs=in_specs, out_spec...]
    reshape x11 -> x8, local copies, waits for them, and re-layouts: 11.2 us -> 4.2 us  [the longest x1 1.55 us: slice_body(): jnp.stack([din0, din1]).reshape(2, 4, 24, 4, 192).transpose(0, 2, 3, 1, 4)]
where the time goes in v2:
time: 555 us; the launch traced here: 548 us
  Pallas kernels  502 us (90%)
  local copies, waits for them, and re-layouts  31.6 us (6%)
  other arithmetic  13.4 us (2%)
    pallas_call x6, Pallas kernels, call(): pl.pallas_call(kernel, out_shape=tuple(outs), in_specs=in_specs, out_spec...  502 us

profile of v2, /device:TPU:9, one launch (start us, length us, event | category | flops | bytes accessed | tf_op | source)
XLA Modules:
  0.0 548.5 jit_solution(11880979204430437279)
XLA Ops:
  0.8 0.7 reshape.192
  1.5 0.7 reshape.193
  2.2 0.7 reshape.194
  3.0 0.7 reshape.195
  3.7 0.7 reshape.196
  4.4 0.7 reshape.200
  5.2 0.7 reshape.197
  5.9 0.7 reshape.198
  6.7 0.7 reshape.199
  7.4 0.7 convert.5
  8.2 0.6 pad_bitcast_fusion.1.small
  8.9 1.1 reshape.186
  11.7 0.8 convert_element_type.46.refs_0_
  13.5 0.8 maximum_bitcast_fusion.1.col
  14.3 0.8 convert_element_type.55.refs_0_
  15.1 16.3 %shard_map.314 = (bf16[4,48,1408]{2,1,0:T(8,128)(2,1)}, bf16[4,48,768]{2,1,0:T(8,128)(2,1)}, bf16[4,2,4,16,128]{4,3,2,1,0:T(8,128)(2,1)}) custom-call(bf16[4,48,1408]{2,1,0:T(8,128)(2,1)} %maximum_bitcast_fusion.1.col, bf16[48,768]{1,0:T(8,128)(2,1)} %bitcast.147, bf16[16,128]{1,0:T(8,128)(2,1)} %pad_bitcast_fusion.1.small), custom_call_target="tpu_custom_call" | custom-call | flops 1000 | bytes 20000000 | tf_op jit(solution)/shard_map/pallas_call | solution.py:1178
  31.5 1.1 copy.156
  32.7 0.7 fusion.3
  33.4 0.7 slice_bitcast_fusion.4
  34.1 0.8 slice_bitcast_fusion
  36.3 0.7 broadcast_select_fusion
  37.0 0.5 concatenate.19.refs_7_
  37.5 0.6 select_convert_fusion.refs_6_.refs_4_
  40.8 0.6 slice_bitcast_fusion.6
  41.5 115.4 %shard_map.315 = (f32[128,768]{1,0:T(8,128)}, bf16[4,128,768]{2,1,0:T(8,128)(2,1)}, bf16[512,384]{1,0:T(8,128)(2,1)}, bf16[4,2,512,384]{3,2,1,0:T(8,128)(2,1)}, ...) custom-call(f32[128,768]{1,0:T(8,128)} %convert_element_type.46.refs, ...), custom_call_target="tpu_custom_call" | custom-call | flops 3000000000 | bytes 20000000 | tf_op jit(solution)/shard_map/pallas_call | solution.py:1178
  156.8 116.9 %shard_map.316 = (f32[128,768]{1,0:T(8,128)}, bf16[4,128,768]{2,1,0:T(8,128)(2,1)}, bf16[512,384]{1,0:T(8,128)(2,1)}, bf16[4,2,512,384]{3,2,1,0:T(8,128)(2,1)}, ...) custom-call(f32[128,768]{1,0:T(8,128)} %get-tuple-element.72.refs_0_, ...), custom_call_target="tpu_custom_call" | custom-call | flops 3000000000 | bytes 20000000 | tf_op jit(solution)/shard_map/pallas_call | solution.py:1178
  273.7 1.7 convert_element_type.54
  275.4 106.3 %shard_map.317 = (f32[128,768]{1,0:T(8,128)}, bf16[2,4,96,640]{3,2,1,0:T(8,128)(2,1)}, bf16[2,96,768]{2,1,0:T(8,128)(2,1)}, f32[4,24,768]{2,1,0:T(8,128)}, f32[96,768]{1,0:T(8,128)}, /*index=5*/f32[8,768]{1,0:T(8,128)}) custom-call(f32[128,768]{1,0:T(8,128)} %convert_element_type.55.refs_0_, bf16[4,2,96,768]{3,2,1,0:T(8,128)(2,1)} %get-tuple-element.76.refs_1_, ...), custom_call_target="tpu_custom_call" | custom-call | flops 6000000000 | bytes 20000000 | tf_op jit(solution)/shard_map/pallas_call | solution.py:1178
  381.7 107.1 %shard_map.318 = (f32[128,768]{1,0:T(8,128)}, bf16[2,4,96,640]{3,2,1,0:T(8,128)(2,1)}, bf16[2,96,768]{2,1,0:T(8,128)(2,1)}, f32[4,24,768]{2,1,0:T(8,128)}, f32[9...) custom-call(f32[128,768]{1,0:T(8,128)} %get-tuple-element.89.refs_0_, ...), custom_call_target="tpu_custom_call" | custom-call | flops 6000000000 | bytes 20000000 | tf_op jit(solution)/shard_map/pallas_call | solution.py:1178
  488.9 1.7 convert_element_type.56
  490.6 1.4 pad_maximum_fusion.3.gsm
  492.0 39.7 %shard_map.319 = (f32[4,24,640]{2,1,0:T(8,128)}, f32[24,768]{1,0:T(8,128)}, f32[4,16,768]{2,1,0:T(8,128)}) custom-call(bf16[2,4,96,640]{3,2,1,0:T(8,128)(2,1)} %get-tuple-element.108.pq, bf16[2,96,768]{2,1,0:T(8,128)(2,1)} %get-tuple-element.109.po, f32[16,768]{1,0:T(8,128)} %pad_maximum_fusion.3.gsm), custom_call_target="tpu_custom_call" | custom-call | flops 1000 | bytes 20000000 | tf_op jit(solution)/shard_map/pallas_call | solution.py:1178
  531.7 1.0 maximum_bitcast_fusion.2
  532.7 1.6 pad_maximum_fusion.2
  534.4 0.6 constant_dynamic-slice_fusion.8
  535.2 0.6 constant_dynamic-slice_fusion.7
  535.9 0.6 constant_dynamic-slice_fusion.3
  536.6 0.6 constant_dynamic-slice_fusion
  537.3 0.6 constant_dynamic-slice_fusion.1
  537.9 0.6 constant_dynamic-slice_fusion.2
  538.5 0.6 constant_dynamic-slice_fusion.4
  539.2 0.6 constant_dynamic-slice_fusion.5
  539.8 0.6 constant_dynamic-slice_fusion.6
  540.6 0.8 reshape.218
  542.3 0.9 reshape_squeeze.14
  543.3 0.9 pad_maximum_fusion
  544.2 0.9 reshape_squeeze.13
  546.4 1.6 reshape.223
  (121 shorter events, 9.7 us)
Async XLA Ops:
  0.7 9.8 %copy-start.13 = (bf16[2,24,768]{2,1,0:T(8,128)(2,1)S(1)}, bf16[2,24,768]{2,1,0:T(8,128)(2,1)}, u32[]{:S(2)}) copy-start(bf16[2,24,768]{2,1,0:T(8,128)(2,1)} %param.23) | copy-start | bytes 221188
  0.7 9.6 %copy-start.12 = (bf16[2,24,768]{2,1,0:T(8,128)(2,1)S(1)}, bf16[2,24,768]{2,1,0:T(8,128)(2,1)}, u32[]{:S(2)}) copy-start(bf16[2,24,768]{2,1,0:T(8,128)(2,1)} %param.22) | copy-start | bytes 221188
  10.3 1.4 copy-start.9
  10.7 1.8 copy-start.2
  13.0 1.4 copy-start.10
  31.5 1.2 copy-start.1
  31.5 2.6 copy-start.3
  32.7 2.3 copy-start.11
  34.1 2.0 copy-start.16
  381.7 108.9 %copy-start.15 = (f32[8,768]{1,0:T(8,128)S(1)}, f32[8,768]{1,0:T(8,128)}, u32[]{:S(2)}) copy-start(f32[8,768]{1,0:T(8,128)} %get-tuple-element.111) | copy-start | bytes 73732
  488.9 42.8 %copy-start.8 = (f32[4,24,640]{2,1,0:T(8,128)S(1)}, f32[4,24,640]{2,1,0:T(8,128)}, u32[]{:S(2)}) copy-start(f32[4,24,640]{2,1,0:T(8,128)} %get-tuple-element.113) | copy-start | bytes 737284
  492.0 40.7 %copy-start.14 = (f32[24,768]{1,0:T(8,128)S(1)}, f32[24,768]{1,0:T(8,128)}, u32[]{:S(2)}) copy-start(f32[24,768]{1,0:T(8,128)} %get-tuple-element.116) | copy-start | bytes 221188
  531.6 2.6 copy-start
  541.8 1.5 copy-start.5
  541.8 1.5 copy-start.7
  543.3 1.9 copy-start.6
  544.1 1.3 copy-start.4

commit v3 on v2

--- a/solution.py
+++ b/solution.py
@@ -755,24 +755,210 @@
     run.close()
 
 
-def pick_parents(kp, kv, route, zz, cc):
+class KeyChain:
+    def __init__(self, run, trunk, mine, slots, up, down, cs, up_out, down_out, place_in):
+        self.run, self.trunk, self.mine, self.slots = run, trunk, mine, slots
+        self.up, self.down, self.cs, self.up_out, self.down_out, self.place_in = up, down, cs, up_out, down_out, place_in
+
+    def start(self):
+        run, place = self.run, self.run.place
+        z, c = place.z, place.c
+        self.pairs = [[(run.sends.take(), run.recvs.take()) for _ in range(4)] for _ in range(3)]
+        for j in range(4):
+            run.launch_if(z == 0, self.mine.at[c, j], self.trunk.at[c, j], self.pairs[0][j], place.column(1))
+        self.near = [run.launch(self.mine.at[c], self.mine.at[c], place.sibling())]
+
+        @pl.when(z == 0)
+        def _():
+            self.trunk[c] = self.mine[c]
+
+        for j in range(4):
+            total = self.mine[c, 0] * self.place_in[j, 0].astype(BF)
+            for ft in range(1, 4):
+                total = total + self.mine[c, ft] * self.place_in[j, ft].astype(BF)
+            self.cs[j] = total
+            run.launch_if(z == 1, self.cs.at[j], self.up.at[j], self.pairs[1][j], place.column(1))
+            run.launch_if(z == 3, self.cs.at[j], self.down.at[j], self.pairs[2][j], place.column(-1))
+
+    def wait(self, which, j):
+        dst = (self.trunk.at[self.run.place.c, j], self.up.at[j], self.down.at[j])[which]
+        remote(dst, dst, self.pairs[which][j], self.run.place.column(1)).wait_recv()
+
+    def finish(self):
+        run, place = self.run, self.run.place
+        z, c = place.z, place.c
+        trunk = [self.trunk.at[c, j] for j in range(4)]
+        for j in range(4):
+
+            @pl.when(z == 1)
+            def _(j=j):
+                self.wait(0, j)
+
+            run.launch_if(z == 1, trunk[j], trunk[j], self.pairs[0][j], place.column(1))
+        for j in range(4):
+
+            @pl.when(z == 2)
+            def _(j=j):
+                self.wait(1, j)
+                self.up_out[j] = self.cs[j] + self.up[j]
+
+            run.launch_if(z == 2, self.up_out.at[j], self.up.at[j], self.pairs[1][j], place.column(1))
+
+            @pl.when(z == 2)
+            def _(j=j):
+                self.wait(2, j)
+                self.down_out[j] = self.cs[j] + self.down[j]
+
+            run.launch_if(z == 2, self.down_out.at[j], self.down.at[j], self.pairs[2][j], place.column(-1))
+
+            @pl.when(z == 2)
+            def _(j=j):
+                self.slots[c, j] = self.up_out[j] + self.down[j]
+
+        for j in range(4):
+
+            @pl.when(z == 2)
+            def _(j=j):
+                self.wait(0, j)
+
+            run.launch_if(z == 2, trunk[j], trunk[j], self.pairs[0][j], place.column(1))
+        for j in range(4):
+
+            @pl.when(z == 0)
+            def _(j=j):
+                self.slots[c, j] = self.cs[j]
+
+            @pl.when(z == 1)
+            def _(j=j):
+                self.wait(2, j)
+                self.slots[c, j] = self.cs[j] + self.down[j]
+
+            @pl.when(z == 3)
+            def _(j=j):
+                self.wait(1, j)
+                self.slots[c, j] = self.cs[j] + self.up[j]
+
+        self.near.append(run.launch(self.slots.at[c], self.slots.at[c], place.sibling()))
+
+        @pl.when(z == 3)
+        def _():
+            for j in range(4):
+                self.wait(0, j)
+
+        self.near.append(run.launch(self.trunk.at[c], self.trunk.at[c], place.sibling()))
+        for a in self.near:
+            a.wait_recv()
+
+
+class GradChain:
+    def __init__(self, run, mine, near, trunk_in, up, down, up_out, down_out, total):
+        self.run, self.mine, self.near, self.trunk_in = run, mine, near, trunk_in
+        self.up, self.down, self.up_out, self.down_out, self.total = up, down, up_out, down_out, total
+
+    def start(self):
+        run, place = self.run, self.run.place
+        self.pairs = [[(run.sends.take(), run.recvs.take()) for _ in range(4)] for _ in range(3)]
+        self.a = run.launch(self.mine.at[1 - place.c], self.near, place.sibling())
+
+    def wait(self, which, j):
+        dst = (self.trunk_in, self.up, self.down)[which].at[j]
+        remote(dst, dst, self.pairs[which][j], self.run.place.column(1)).wait_recv()
+
+    def middle(self):
+        run, place = self.run, self.run.place
+        z, c = place.z, place.c
+        self.a.wait_recv()
+        near = self.near
+        for kind in range(3):
+            for j in range(4):
+                near[kind, j] = (self.mine[c, kind, j].astype(F32) + near[kind, j].astype(F32)).astype(BF)
+                if kind == 0:
+                    run.launch_if(z == 3, near.at[0, j], self.trunk_in.at[j], self.pairs[0][j], place.column(-1))
+                elif kind == 1:
+                    run.launch_if(z == 1, near.at[1, j], self.up.at[j], self.pairs[1][j], place.column(1))
+                    run.launch_if(z == 3, near.at[1, j], self.down.at[j], self.pairs[2][j], place.column(-1))
+
+    def pass_on(self):
+        run, place = self.run, self.run.place
+        z = place.z
+        near = self.near
+        for j in range(4):
+            cond = jnp.logical_or(z == 1, z == 2)
+
+            @pl.when(cond)
+            def _(j=j):
+                self.wait(0, j)
+                near[0, j] = (near[0, j].astype(F32) + self.trunk_in[j].astype(F32)).astype(BF)
+
+            run.launch_if(cond, near.at[0, j], self.trunk_in.at[j], self.pairs[0][j], place.column(-1))
+
+            @pl.when(z == 2)
+            def _(j=j):
+                self.wait(1, j)
+                self.up_out[j] = (near[1, j].astype(F32) + self.up[j].astype(F32)).astype(BF)
+
+            run.launch_if(z == 2, self.up_out.at[j], self.up.at[j], self.pairs[1][j], place.column(1))
+        for j in range(4):
+
+            @pl.when(z == 2)
+            def _(j=j):
+                self.wait(2, j)
+                self.down_out[j] = (near[1, j].astype(F32) + self.down[j].astype(F32)).astype(BF)
+
+            run.launch_if(z == 2, self.down_out.at[j], self.down.at[j], self.pairs[2][j], place.column(-1))
+
+    def finish(self, place_in, store):
+        place = self.run.place
+        z = place.z
+        near = self.near
+
+        @pl.when(z == 0)
+        def _():
+            for j in range(4):
+                self.wait(0, j)
+                store(j, near[0, j].astype(F32) + self.trunk_in[j].astype(F32))
+
+        @pl.when(z == 1)
+        def _():
+            for j in range(4):
+                self.wait(2, j)
+                self.total[j] = (near[1, j].astype(F32) + self.down[j].astype(F32)).astype(BF)
+
+        @pl.when(z == 2)
+        def _():
+            for j in range(4):
+                self.total[j] = (self.up_out[j].astype(F32) + self.down[j].astype(F32)).astype(BF)
+
+        @pl.when(z == 3)
+        def _():
+            for j in range(4):
+                self.wait(1, j)
+                self.total[j] = (near[1, j].astype(F32) + self.up[j].astype(F32)).astype(BF)
+
+        @pl.when(z > 0)
+        def _():
+            for ft in range(4):
+                total = near[2, ft].astype(F32)
+                for j in range(4):
+                    total = total + self.total[j].astype(F32) * place_in[j, ft]
+                store(ft, total)
+
+
+def pick_parents(kp, slots, choose):
     def one(b, carry):
-        total = kp[b, cc]
-        for ft in range(4):
-            total = total + kv[zz, cc, ft * ROWS : (ft + 1) * ROWS, :] * route[b, 4 * zz + ft].astype(BF)
-        kp[b, cc] = total
+        for cc in range(2):
+            total = slots[cc, 0] * choose[b, 0].astype(BF)
+            for j in range(1, 4):
+                total = total + slots[cc, j] * choose[b, j].astype(BF)
+            kp[b, cc] = total
         return carry
 
     lax.fori_loop(0, 4, one, 0)
 
 
-def all_keys(kv, kp, z, b, lanes):
-    rows = pl.ds(pl.multiple_of(b * ROWS, ROWS), ROWS)
+def all_keys(trunk, mine, kp, b, lanes):
     return jnp.concatenate(
-        [
-            kv[0, 0, :, lanes], kv[0, 1, :, lanes], kv[z, 0, rows, lanes], kv[z, 1, rows, lanes],
-            kp[b, 0, :, lanes], kp[b, 1, :, lanes],
-        ],
+        [trunk[:, :, :, lanes].reshape(1024, 128), mine[0, b, :, lanes], mine[1, b, :, lanes], kp[b, 0, :, lanes], kp[b, 1, :, lanes]],
         axis=0,
     )
 
@@ -789,13 +975,14 @@
         del refs[:n]
         return out
 
-    x_ref, qkv_in, o_in, in_c, out_c, vec, route, pen = take(8)
+    x_ref, qkv_in, o_in, in_c, out_c, vec, place_in, choose, pen = take(9)
     if first:
         qkv_next, o_next = take(2)
-    xn_ref, xb_o, qp_o, kv_o, kp_o, p_o, ctx_o, z1_o, hb_o, gp_o, gl_o, z2_o, win_o, wout_o = take(14)
+    xn_ref, xb_o, qp_o, trunk_o, mine_o, kp_o, p_o, ctx_o, z1_o, hb_o, gp_o, gl_o, z2_o, win_o, wout_o = take(15)
     if first:
         wqkv_o, wo_o, wqkv_n, wo_n = take(4)
-    xb, qp, kv, kp, p, ctx, z1, hb, gp, gl, z2, win, wout, wqkv, wo, heads, own, rs1_s, rs1_r, rs2_s, rs2_r = take(21)
+    xb, qp, trunk, mine, kp, p, ctx, z1, hb, gp, gl, z2, win, wout, wqkv, wo, heads, own, rs1_s, rs1_r, rs2_s, rs2_r = take(22)
+    chain_refs = take(6)
     run = Run(*refs)
     place = run.place
     z, f, c = place.z, place.f, place.c
@@ -823,31 +1010,24 @@
             came[k].wait_recv()
         qkv = product(xb[g], flat(wqkv)) + vec[0:1, :PACKED]
         rows = pl.ds(pl.multiple_of(g * ROWS, ROWS), ROWS)
-        kv[z, c, rows, :] = qkv[:, 256:].astype(BF)
+        mine[c, g] = qkv[:, 256:].astype(BF)
         scaled = qkv[:, :256] * (HEAD_DIM ** (-0.5))
         front = scaled[:, :128]
         qp[rows, 0:128] = jnp.where(lane < 64, front, 0.0).astype(BF)
         qp[rows, 128:256] = jnp.where(lane < 64, pltpu.roll(front, 64, 1), 0.0).astype(BF)
         qp[rows, 256:384] = scaled[:, 128:].astype(BF)
-    move = [launch(kv.at[z, c], kv.at[z, c], place.column(k)) for k in (1, 2, 3)]
-    side = [launch(kv.at[z, c], kv.at[z, c], place.sibling())]
+    chain = KeyChain(run, trunk, mine, *chain_refs, place_in)
+    chain.start()
     m_tasks = [Spread(run, in_c, win), Spread(run, out_c, wout)]
+    run.save(xb, xb_o)
+    run.save(qp, qp_o)
+    chain.finish()
     for t in m_tasks:
         t.start()
-    run.save(xb, xb_o)
-    run.save(qp, qp_o)
-    kp[...] = jnp.zeros_like(kp)
-    pick_parents(kp, kv, route, z, c)
-    for k in (1, 2, 3):
-        move[k - 1].wait_recv()
-        there = place.z_at(-k)
-        side.append(launch(kv.at[there, c], kv.at[there, c], place.sibling()))
-        pick_parents(kp, kv, route, there, c)
-    for k in range(4):
-        side[k].wait_recv()
-        pick_parents(kp, kv, route, place.z_at(-k), 1 - c)
+    pick_parents(kp, chain.slots, choose)
     run.save(kp, kp_o)
-    run.save(kv, kv_o)
+    run.save(trunk, trunk_o)
+    run.save(mine, mine_o)
     if first:
         a_tasks[1].relay()
         n_tasks = [Spread(run, qkv_next, wqkv_n), SpreadOutput(run, o_next, wo_n)]
@@ -858,7 +1038,7 @@
         h, b = i // 4, lax.rem(i, 4)
         lanes = pl.ds(pl.multiple_of(h * 128, 128), 128)
         rows = pl.ds(pl.multiple_of(b * ROWS, ROWS), ROWS)
-        keys = all_keys(kv, kp, z, b, lanes)
+        keys = all_keys(trunk, mine, kp, b, lanes)
         s = product_nt(qp[rows, lanes], keys)
         s = jnp.concatenate(
             [s[:, :1024], s[:, 1024:1280] + pen[4 + b], s[:, 1280:] + pen[b]], axis=1
@@ -945,22 +1125,25 @@
         del refs[:n]
         return out
 
-    dy_ref, win, wout, vec, route, z1, hb, gp, gl, z2 = take(10)
-    late_in = take(8)
+    dy_ref, win, wout, vec, place_in, choose, z1, hb, gp, gl, z2 = take(11)
+    late_in = take(9)
     if extra:
-        pq_in, po_in = take(2)
-    dx_ref, pq, po, din_o, dout_o, dvec_o = take(6)
+        pq_in, pk_in, dvec_in = take(3)
+    dx_ref, din_o, dout_o, do_o = take(4)
     if extra:
-        dqkv_o, do_o = take(2)
-    late = take(8)
-    wqkv, wo, xb, qp, kv, kp, p, ctx = late
+        dq_n, dk_n, dq_o, dk_o, sm_o = take(5)
+    else:
+        pq, pk, dvec_o = take(3)
+    late = take(9)
+    wqkv, wo, xb, qp, trunk, mine, kp, p, ctx = late
     (
-        df, du, da, dctx, dqf, dqkv, dz, dz1, dkt, dself, dpar, tgt, tgt_r, summed, summed_r,
-        own, rs1_s, rs1_r, rs2_s, rs2_r,
-    ) = take(20)
-    pin, nin, fin, tin, pout, nout, fout = take(7)
+        df, du, da, dctx, dqf, dqkv, dz, dz1, dkt, dself, dpar, tgt, own, rs1_s, rs1_r, rs2_s, rs2_r,
+    ) = take(17)
+    chain_refs = take(7)
+    pin, nin, fin, tin, pout, nout, fout, po, no, fo, to = take(11)
     if extra:
-        nq, fq, tq, no, fo, to = take(6)
+        pq, pk, dvec_o = take(3)
+        nq, fq, tq, nk, fk, tk, nq2, fq2, tq2, nk2, fk2, tk2, sm, sm_a, sm_b, sm_v = take(16)
     run = Run(*refs)
     place = run.place
     z, f, c = place.z, place.f, place.c
@@ -981,7 +1164,7 @@
     came = [None] + [launch(df.at[f], df.at[f], place.plane(k)) for k in (1, 2, 3)]
     a_tasks = []
     if extra:
-        a_tasks = [Collect(run, pq_in, nq, fq, tq, dqkv_o), CollectOutput(run, po_in, no, fo, to, do_o)]
+        a_tasks = [Collect(run, pq_in, nq, fq, tq, dq_n), Collect(run, pk_in, nk, fk, tk, dk_n)]
     for t in a_tasks:
         t.start()
     back = [None]
@@ -1003,18 +1186,19 @@
                 t.middle()
     dvec_o[4:5, :] = bias
     m_tasks = [Collect(run, pin, nin, fin, tin, din_o), Collect(run, pout, nout, fout, None, dout_o)]
+    o_task = CollectOutput(run, po, no, fo, to, do_o)
 
     def split_rows(dst, left, right, i):
         lanes = pl.ds(pl.multiple_of(i * 384, 128), 384)
-        value = product_tn(left[:, :, lanes].reshape(512, 384), flat(right)).astype(BF)
+        value = product_tn(left[:, :, lanes].reshape(512, 384), right).astype(BF)
         for zz in range(2):
             for cc in range(2):
                 at = (2 * zz + cc) * 96
                 dst[cc, 2 * i + zz] = value[at : at + 96, :]
 
     def ffn_grads(i, carry):
-        split_rows(pout, gl, df, i)
-        split_rows(pin, hb, du, i)
+        split_rows(pout, gl, flat(df), i)
+        split_rows(pin, hb, flat(du), i)
         return carry
 
     lax.fori_loop(0, 2, ffn_grads, 0)
@@ -1049,12 +1233,16 @@
         dctx[rows, 0:128] = jnp.where(lane < 64, 0.0, pltpu.roll(ahead, 64, 1)).astype(BF)
         dctx[rows, 128:256] = jnp.where(lane < 64, 0.0, ahead).astype(BF)
         dctx[rows, 256:384] = jnp.where(lane < 64, 0.0, pltpu.roll(after, 64, 1)).astype(BF)
+    value = product_tn(flat(ctx), flat(da)).astype(BF)
+    for cc in range(2):
+        po[cc] = value[96 * cc : 96 * (cc + 1), :]
+    o_task.start()
 
     def attend(i, carry):
         h, b = i // 4, lax.rem(i, 4)
         lanes = pl.ds(pl.multiple_of(h * 128, 128), 128)
         rows = pl.ds(pl.multiple_of(b * ROWS, ROWS), ROWS)
-        keys = all_keys(kv, kp, z, b, lanes)
+        keys = all_keys(trunk, mine, kp, b, lanes)
         q, g = qp[rows, lanes], dctx[rows, lanes]
         low = p[h, b]
         pf = low.astype(F32)
@@ -1070,39 +1258,42 @@
 
     lax.fori_loop(0, 12, attend, 0)
     for cc in range(2):
-        tgt[cc, 0] = dkt[cc * 512 : (cc + 1) * 512, :].astype(BF)
-
-    def scatter(i, carry):
-        zt, ft = 1 + i // 4, lax.rem(i, 4)
-        rows = pl.ds(pl.multiple_of(ft * ROWS, ROWS), ROWS)
-        here = jnp.where(zt == z, 1.0, 0.0)
+        for j in range(4):
+            at = cc * 512 + j * ROWS
+            tgt[cc, 0, j] = dkt[at : at + ROWS, :].astype(BF)
+
+    def scatter(j, carry):
         for cc in range(2):
             half = slice(cc * ROWS, (cc + 1) * ROWS)
-            total = dself[ft, half, :] * here
-            for b in range(4):
-                total = total + dpar[b, half, :] * route[b, 4 * zt + ft]
-            tgt[cc, zt, rows, :] = total.astype(BF)
+            total = dpar[0, half, :] * choose[0, j]
+            for b in range(1, 4):
+                total = total + dpar[b, half, :] * choose[b, j]
+            tgt[cc, 1, j] = total.astype(BF)
+            tgt[cc, 2, j] = dself[j, half, :].astype(BF)
         return carry
 
-    lax.fori_loop(0, 12, scatter, 0)
-    near = launch(tgt.at[1 - c], tgt_r, place.sibling())
+    lax.fori_loop(0, 4, scatter, 0)
+    chain = GradChain(run, tgt, *chain_refs)
+    chain.start()
     for g in range(4):
         rows = slice(g * ROWS, (g + 1) * ROWS)
         ahead = jnp.where(lane < 64, dqf[0, rows, :], pltpu.roll(dqf[1, rows, :], 64, 1))
         dqkv[g, :, 0:128] = ahead.astype(BF)
         dqkv[g, :, 128:256] = jnp.where(lane < 64, dqf[2, rows, :], 0.0).astype(BF)
-    near.wait_recv()
-    for zt in range(4):
-        summed[zt] = (tgt[c, zt].astype(F32) + tgt_r[zt].astype(F32)).astype(BF)
-    far = [launch(summed.at[place.z_at(k)], summed_r.at[k - 1], place.column(k)) for k in (1, 2, 3)]
-    value = product_tn(flat(ctx), flat(da)).astype(BF)
-    for cc in range(2):
-        po[cc] = value[96 * cc : 96 * (cc + 1), :]
-    for a in far:
-        a.wait_recv()
-    total = summed[z].astype(F32) + summed_r[0].astype(F32) + summed_r[1].astype(F32) + summed_r[2].astype(F32)
-    for g in range(4):
-        dqkv[g, :, 256:] = total[g * ROWS : (g + 1) * ROWS, :].astype(BF)
+    chain.middle()
+    o_task.middle()
+    chain.pass_on()
+
+    def q_grads(i, carry):
+        split_rows(pq, xb, dqkv[:, :, :256].reshape(512, 256), i)
+        return carry
+
+    lax.fori_loop(0, 2, q_grads, 0)
+
+    def store(ft, value):
+        dqkv[ft, :, 256:] = value.astype(BF)
+
+    chain.finish(place_in, store)
     back = [None]
     for k in (1, 2, 3, 0):
         g = place.f_at(-k)
@@ -1113,52 +1304,44 @@
         else:
             own[...] = part
 
-    def qkv_grads(i, carry):
-        split_rows(pq, xb, dqkv, i)
+    def k_grads(i, carry):
+        split_rows(pk, xb, dqkv[:, :, 256:].reshape(512, SLICE), i)
         return carry
 
-    lax.fori_loop(0, 2, qkv_grads, 0)
+    lax.fori_loop(0, 2, k_grads, 0)
     sums = jnp.sum(flat(dqkv).astype(F32), axis=0, keepdims=True)
     dvec_o[0:1, :] = jnp.concatenate([sums, jnp.zeros((1, WIDE - PACKED), F32)], axis=1)
-    for t in m_tasks:
+    end_tasks = []
+    if extra:
+        end_tasks = [Collect(run, pk, nk2, fk2, tk2, dk_o), Collect(run, pq, nq2, fq2, tq2, dq_o)]
+        for t in end_tasks:
+            t.start()
+        sm[0:8, :] = dvec_o[...]
+        sm[8:16, :] = dvec_in[...]
+        sm_near = launch(sm, sm_a, place.sibling())
+        for t in end_tasks:
+            t.middle()
+        sm_near.wait_recv()
+        sm_a[...] = sm[...] + sm_a[...]
+        sm_far = [launch(sm_a, sm_b.at[k - 1], place.column(k)) for k in (1, 2, 3)]
+    for t in m_tasks + [o_task]:
         t.end()
     for t in a_tasks:
         t.last()
     for k in (1, 2, 3):
         back[k].wait_recv()
     dx_ref[...] = dz1[...] + own[...] + rs2_r[0].astype(F32) + rs2_r[1].astype(F32) + rs2_r[2].astype(F32)
-    for t in m_tasks:
-        t.last()
-    run.close()
-
-
-def reduce_kernel(
-    pq, po, gsm, dqkv_o, do_o, sm_o, nq, fq, tq, no, fo, to, sm_a, sm_u, sm_b, sm_v, send_sems, recv_sems, local_sems
-):
-    run = Run(send_sems, recv_sems, local_sems)
-    place = run.place
-    f = place.f
-    launch = run.launch
-    run.greet(True)
-    tasks = [Collect(run, pq, nq, fq, tq, dqkv_o), CollectOutput(run, po, no, fo, to, do_o)]
-    for t in tasks:
-        t.start()
-    a = launch(gsm, sm_a, place.sibling())
-    for t in tasks:
-        t.middle()
-    a.wait_recv()
-    sm_u[...] = gsm[...] + sm_a[...]
-    far = [launch(sm_u, sm_b.at[k - 1], place.column(k)) for k in (1, 2, 3)]
-    for a in far:
-        a.wait_recv()
-    sm_v[...] = sm_u[...] + sm_b[0] + sm_b[1] + sm_b[2]
-    last = [launch(sm_v, sm_o.at[f], place.plane(k)) for k in (1, 2, 3)]
-    sm_o[f] = sm_v[...]
-    for t in tasks:
-        t.end()
-    for a in last:
-        a.wait_recv()
-    for t in tasks:
+    if extra:
+        for t in end_tasks:
+            t.end()
+        for a in sm_far:
+            a.wait_recv()
+        sm_v[...] = sm_a[...] + sm_b[0] + sm_b[1] + sm_b[2]
+        sm_last = [launch(sm_v, sm_o.at[f], place.plane(k)) for k in (1, 2, 3)]
+        sm_o[f] = sm_v[...]
+        for a in sm_last:
+            a.wait_recv()
+    for t in m_tasks + [o_task] + end_tasks:
         t.last()
     run.close()
 
@@ -1167,7 +1350,7 @@
 VM = pl.BlockSpec(memory_space=pltpu.VMEM)
 SM = pl.BlockSpec(memory_space=pltpu.SMEM)
 LIMIT = 60 * 1024 * 1024
-SEMS = (128, 128, 32)
+SEMS = (160, 160, 32)
 
 
 def shape(*dims, dtype=BF):
@@ -1204,23 +1387,25 @@
 QKV = shape(4, 2, 96, PACKED)
 BIG = shape(4, 2, 96, WIDE)
 OUTPUT = shape(192, WIDE)
+HALVES = shape(2, 4, ROWS, SLICE)
+QUARTERS = shape(4, ROWS, SLICE)
 SAVED = (
-    FULL, shape(512, SLICE), shape(4, 2, 512, SLICE), shape(4, 2, ROWS, SLICE), shape(3, 4, ROWS, NKEYS),
+    FULL, shape(512, SLICE), HALVES, HALVES, shape(4, 2, ROWS, SLICE), shape(3, 4, ROWS, NKEYS),
     shape(4, ROWS, 256), LOCAL, FULL, shape(4, ROWS, WIDE, dtype=F32), FULL, LOCAL,
 )
 
 
-def forward_layer(first, state, qkv, o, in_c, out_c, vec, route, pen, following):
+def forward_layer(first, state, qkv, o, in_c, out_c, vec, place_in, choose, pen, following):
     outs = (LOCAL,) + SAVED + (BIG, BIG) + ((QKV, OUTPUT, QKV, OUTPUT) if first else ())
     got = call(
         lambda *refs: forward_kernel(first, *refs), 1 if first else 2, outs, (VM,) + (ANY,) * (len(outs) - 1),
-        [VM] + [ANY] * 4 + [VM] + [SM] * 2 + [ANY] * len(following),
+        [VM] + [ANY] * 4 + [VM] + [SM] * 3 + [ANY] * len(following),
         list(SAVED)
         + [BIG, BIG, QKV, shape(256, WIDE), shape(3, 4, ROWS, 128, dtype=F32), LOCAL]
-        + [PIECE] * 4,
-        (state, qkv, o, in_c, out_c, vec, route, pen) + tuple(following), 3 * 10**9,
-    )
-    return got[0], got[1:12], got[12:]
+        + [PIECE] * 4 + [HALVES] + [QUARTERS] * 5,
+        (state, qkv, o, in_c, out_c, vec, place_in, choose, pen) + tuple(following), 3 * 10**9,
+    )
+    return got[0], got[1:13], got[13:]
 
 
 def collect_scratch(columns, rows):
@@ -1228,41 +1413,37 @@
 
 
 OUT_SCRATCH = [shape(96, WIDE), shape(4, 96, WIDE), shape(96, WIDE, dtype=F32)]
-PARTS = (shape(2, 4, 96, PACKED), shape(2, 96, WIDE))
-SHARES = (shape(4, 24, PACKED, dtype=F32), shape(24, WIDE, dtype=F32))
-
-
-def backward_layer(upstream, weights, vec, route, saved, before):
+PARTS = (shape(2, 4, 96, 256), shape(2, 4, 96, SLICE))
+SHARES = (shape(4, 24, 256, dtype=F32), shape(4, 24, SLICE, dtype=F32))
+
+
+def backward_layer(upstream, weights, vec, place_in, choose, saved, before):
     wqkv, wo, win, wout = weights
-    xb, qp, kv, kp, p, ctx, z1, hb, gp, gl, z2 = saved
+    xb, qp, trunk, mine, kp, p, ctx, z1, hb, gp, gl, z2 = saved
     keys = shape(4, 256, SLICE, dtype=F32)
     extra = len(before) > 0
-    outs = (LOCAL,) + PARTS + (
-        shape(4, 24, WIDE, dtype=F32), shape(96, WIDE, dtype=F32), shape(8, WIDE, dtype=F32)
-    ) + (SHARES if extra else ())
-    late = [QKV, shape(256, WIDE)] + [SAVED[i] for i in range(6)]
-    scratch = late + [
+    sums, sums2 = shape(8, WIDE, dtype=F32), shape(16, WIDE, dtype=F32)
+    outs = (LOCAL, shape(4, 24, WIDE, dtype=F32), shape(96, WIDE, dtype=F32), shape(24, WIDE, dtype=F32))
+    outs += SHARES + SHARES + (shape(4, 16, WIDE, dtype=F32),) if extra else PARTS + (sums,)
+    scratch = [QKV, shape(256, WIDE)] + list(SAVED[:7]) + [
         FULL, FULL, FULL, shape(512, SLICE), shape(3, 512, 128, dtype=F32), shape(4, ROWS, PACKED), LOCAL, LOCAL,
-        shape(1024, SLICE, dtype=F32), keys, keys, shape(2, 4, 512, SLICE), shape(4, 512, SLICE),
-        shape(4, 512, SLICE), shape(3, 512, SLICE), LOCAL, PIECE, PIECE, PIECE, PIECE,
-    ]
-    scratch += [shape(2, 4, 96, WIDE)] + collect_scratch(WIDE, True) + [shape(2, 4, 96, WIDE)] + collect_scratch(WIDE, False)
+        shape(1024, SLICE, dtype=F32), keys, keys, shape(2, 3, 4, ROWS, SLICE), LOCAL, PIECE, PIECE, PIECE, PIECE,
+        shape(3, 4, ROWS, SLICE),
+    ] + [QUARTERS] * 6
+    part = shape(2, 4, 96, WIDE)
+    scratch += [part] + collect_scratch(WIDE, True) + [part] + collect_scratch(WIDE, False)
+    scratch += [shape(2, 96, WIDE)] + OUT_SCRATCH
     if extra:
-        scratch += collect_scratch(PACKED, True) + OUT_SCRATCH
+        scratch += list(PARTS) + [sums]
+        scratch += (collect_scratch(256, True) + collect_scratch(SLICE, True)) * 1
+        scratch += collect_scratch(256, True) + collect_scratch(SLICE, True)
+        scratch += [sums2, sums2, shape(3, 16, WIDE, dtype=F32), sums2]
     return call(
         lambda *refs: backward_kernel(extra, *refs), 4 if extra else 3, outs, (VM,) * len(outs),
-        [VM] * 4 + [SM] + [VM] * 5 + [ANY] * 8 + [VM] * len(before), scratch,
-        (upstream, win, wout, vec, route, z1, hb, gp, gl, z2, wqkv, wo, xb, qp, kv, kp, p, ctx) + tuple(before),
+        [VM] * 4 + [SM] * 2 + [VM] * 5 + [ANY] * 9 + [VM] * len(before), scratch,
+        (upstream, win, wout, vec, place_in, choose, z1, hb, gp, gl, z2, wqkv, wo, xb, qp, trunk, mine, kp, p, ctx)
+        + tuple(before),
         6 * 10**9,
-    )
-
-
-def reduce_rest(pq, po, gsm):
-    sm = shape(16, WIDE, dtype=F32)
-    return call(
-        reduce_kernel, 5, SHARES + (shape(4, 16, WIDE, dtype=F32),), (VM,) * 3, [VM] * 3,
-        collect_scratch(PACKED, True) + OUT_SCRATCH + [sm, sm, shape(3, 16, WIDE, dtype=F32), sm],
-        (pq, po, gsm), 1000,
     )
 
 
@@ -1275,72 +1456,71 @@
     z, f, c = place.z, place.f, place.c
     col = column_parts(query_weight, key_weight, value_weight, inner_weight)
     vectors = (query_bias, value_bias, output_bias, first_gain, first_shift, outer_bias, second_gain, second_shift)
-    small = jnp.concatenate([v.reshape(-1) for v in vectors] + [inner_bias.reshape(-1), segments[:1].astype(BF)])
-    small = jnp.pad(small, (0, 2048 - small.shape[0])).reshape(16, 128)
+    label = jnp.broadcast_to(segments[:1].astype(BF)[None], (2, 1))
+    small = jnp.concatenate(vectors + (inner_bias, label), axis=1)
+    small = jnp.pad(small, ((0, 14), (0, 384 - small.shape[1])))
     colp, op, smallg = call(
-        exchange_kernel, 0, (shape(4, 48, 1408), shape(4, 48, WIDE), shape(4, 2, 4, 16, 128)), (ANY,) * 3, [ANY] * 3,
+        exchange_kernel, 0, (shape(4, 48, 1408), shape(4, 48, WIDE), shape(4, 2, 4, 16, 384)), (ANY,) * 3, [ANY] * 3,
         [], (col, output_weight.reshape(48, WIDE), small), 1000,
     )
     colp = colp.reshape(4, 2, 24, 1408).transpose(1, 0, 2, 3).reshape(2, 96, 1408)
     op = op.reshape(4, 2, 24, WIDE).transpose(1, 0, 2, 3).reshape(2, 96, WIDE)
-    small = smallg.transpose(0, 2, 1, 3, 4).reshape(32, 2048).astype(F32)
-    parts = [small[:, i * 48 : (i + 1) * 48].reshape(32, 2, 24).transpose(1, 0, 2).reshape(2, WIDE) for i in range(8)]
+    small = smallg[:, :, :, :2].transpose(3, 0, 2, 1, 4).astype(F32)
+    parts = [small[..., i * 24 : (i + 1) * 24].reshape(2, WIDE) for i in range(8)]
     q_all, v_all, o_all, g1, s1, out_all, g2, s2 = parts
-    in_all = small[:, 384:576].reshape(4, 4, 2, 2, 96)
-    in_mine = lax.dynamic_index_in_dim(in_all, f, 1, keepdims=False).transpose(2, 0, 1, 3).reshape(2, WIDE)
+    in_mine = lax.dynamic_index_in_dim(small[..., 192:288], f, 2, keepdims=False).reshape(2, WIDE)
     q_mine = lax.dynamic_slice_in_dim(q_all, 192 * f, 192, 1)
     v_mine = lax.dynamic_slice_in_dim(v_all, 192 * f, 192, 1).reshape(2, 3, 64)
     kv_mine = jnp.pad(v_mine, ((0, 0), (0, 0), (64, 0))).reshape(2, SLICE)
     qkv_mine = jnp.pad(jnp.concatenate([q_mine, jnp.zeros((2, 64), F32), kv_mine], axis=1), ((0, 0), (0, WIDE - PACKED)))
     vecs = jnp.stack([qkv_mine, o_all, g1, s1, in_mine, out_all, g2, s2], axis=1)
 
-    labels = small[:, 576].reshape(16, 2)[:, 0].astype(jnp.int32)
-    mine = lax.dynamic_slice_in_dim(labels, 4 * z, 4, 0)
-    parent = lookup_rows(mine, parents)
-    match = (parent[:, None] == labels[None, :]).astype(jnp.int32)
-    branch = parent != labels[0]
+    labels = small[0, :, :, 0, 288].reshape(16).astype(jnp.int32)
+    above = lookup_rows(labels, parents)
+    order = jnp.arange(16, dtype=jnp.int32)
+    branch = jnp.logical_and(above == labels[0], order >= 4)
+    slot = jnp.where(branch, jnp.sum((branch[:, None] & (order[:, None] < order[None, :])).astype(jnp.int32), axis=0), 4)
+    in_slot = slot[None, :] == jnp.arange(4, dtype=jnp.int32)[:, None]
+    place_in = lax.dynamic_slice_in_dim(in_slot.astype(F32), 4 * z, 4, 1)
+    parent = lax.dynamic_slice_in_dim(above, 4 * z, 4, 0)
+    match = parent[:, None, None] == jnp.where(in_slot, labels[None, :], -1)[None]
+    choose = jnp.any(match, axis=2).astype(F32)
     pen = jnp.concatenate(
-        [jnp.where(branch, 0.0, MASKED), jnp.where(z > 0, jnp.zeros((4,), F32), MASKED)]
+        [jnp.where(jnp.any(match, axis=(1, 2)), 0.0, MASKED), jnp.where(z > 0, jnp.zeros((4,), F32), MASKED)]
     ).astype(F32)
-    route = jnp.where(branch[:, None], match, 0).astype(F32)
 
     qkv_c = [colp[i, :, :PACKED] for i in range(2)]
     in_c = [colp[i, :, PACKED:] for i in range(2)]
     state, kept0, (win0, wout0, wqkv0, wo0, wqkv1, wo1) = forward_layer(
-        True, activations.astype(F32), qkv_c[0], op[0], in_c[0], outer_weight[0], vecs[0], route, pen, (qkv_c[1], op[1])
+        True, activations.astype(F32), qkv_c[0], op[0], in_c[0], outer_weight[0], vecs[0], place_in, choose, pen,
+        (qkv_c[1], op[1]),
     )
     state, kept1, (win1, wout1) = forward_layer(
-        False, state, wqkv1, wo1, in_c[1], outer_weight[1], vecs[1], route, pen, ()
+        False, state, wqkv1, wo1, in_c[1], outer_weight[1], vecs[1], place_in, choose, pen, ()
     )
     outcome = state.astype(BF)
-    upstream, pq, po, din1, dout1, dvec1 = backward_layer(
-        cotangent.astype(F32), (wqkv1, wo1, win1, wout1), vecs[1], route, kept1, ()
-    )
-    upstream, pq, po, din0, dout0, dvec0, dqkv1, do1 = backward_layer(
-        upstream, (wqkv0, wo0, win0, wout0), vecs[0], route, kept0, (pq, po)
-    )
-    dqkv0, do0, rsm = reduce_rest(pq, po, jnp.concatenate([dvec0, dvec1]))
-    dqkv = jnp.stack([dqkv0, dqkv1]).transpose(0, 2, 1, 3)
-    dq = dqkv[..., :192].reshape(2, 24, WIDE)
-    dkv = dqkv[..., 256:].reshape(2, 24, 4, 3, 2, 64)
+    upstream, din1, dout1, do1, pq, pk, dvec1 = backward_layer(
+        cotangent.astype(F32), (wqkv1, wo1, win1, wout1), vecs[1], place_in, choose, kept1, ()
+    )
+    upstream, din0, dout0, do0, dq1, dk1, dq0, dk0, rsm = backward_layer(
+        upstream, (wqkv0, wo0, win0, wout0), vecs[0], place_in, choose, kept0, (pq, pk, dvec1)
+    )
+    dq = jnp.stack([dq0, dq1]).transpose(0, 2, 1, 3)[..., :192].reshape(2, 24, WIDE)
+    dkv = jnp.stack([dk0, dk1]).transpose(0, 2, 1, 3).reshape(2, 24, 4, 3, 2, 64)
     dk = dkv[..., 0, :].reshape(2, 24, WIDE)
     dv = dkv[..., 1, :].reshape(2, 24, WIDE)
     dinner = jnp.stack([din0, din1]).reshape(2, 4, 24, 4, 192).transpose(0, 2, 3, 1, 4).reshape(2, 24, 3072)
     rsm = rsm.reshape(4, 2, 8, WIDE)
     sums = jnp.sum(rsm, axis=0)
-    at = 24 * (8 * z + 2 * f + c)
-
-    def own_part(v):
-        return lax.dynamic_slice_in_dim(v, at, 24, 1)
-
     dqb = rsm[:, :, 0, :192].transpose(1, 0, 2).reshape(2, WIDE)
     dvb = rsm[:, :, 0, 256:640].reshape(4, 2, 3, 2, 64)[:, :, :, 1].transpose(1, 0, 2, 3).reshape(2, WIDE)
+    rows = jnp.stack([dqb, dvb, sums[:, 1], sums[:, 2], sums[:, 3], sums[:, 5], sums[:, 6], sums[:, 7]])
+    rows = lax.dynamic_slice_in_dim(rows, 24 * (8 * z + 2 * f + c), 24, 2)
     dib = lax.dynamic_index_in_dim(rsm[:, :, 4], f, 0, keepdims=False)
     dib = lax.dynamic_slice_in_dim(dib, 96 * (2 * z + c), 96, 1)
     return (
-        outcome, upstream.astype(BF), dq, own_part(dqb), dk, dv, own_part(dvb),
-        jnp.stack([do0, do1]), own_part(sums[:, 1]), own_part(sums[:, 2]), own_part(sums[:, 3]),
-        dinner, dib, jnp.stack([dout0, dout1]), own_part(sums[:, 5]), own_part(sums[:, 6]), own_part(sums[:, 7]),
+        outcome, upstream.astype(BF), dq, rows[0], dk, dv, rows[1], jnp.stack([do0, do1]), rows[2], rows[3], rows[4],
+        dinner, dib, jnp.stack([dout0, dout1]), rows[5], rows[6], rows[7],
     )
 
 

time: 555 us -> 475 us (0.86)
  Pallas kernels: 502 us -> 433 us
  local copies, waits for them, and re-layouts: 31.6 us -> 19.7 us
    pallas_call x6 -> x5, Pallas kernels: 502 us -> 433 us  [call(): pl.pallas_call(kernel, out_shape=tuple(outs), in_specs=in_specs, out_spec...]
    reshape x17 -> x4, local copies, waits for them, and re-layouts: 8.89 us -> 1.39 us  [the longest x1 0.8 us: slice_body(): jnp.stack([dq0, dq1]).transpose(0, 2, 1, 3)[..., :192].reshape(2, 24, WIDE)]
where the time goes in v3:
time: 475 us; the launch traced here: 467 us
  Pallas kernels  433 us (91%)
  local copies, waits for them, and re-layouts  19.7 us (4%)
  other arithmetic  12.4 us (3%)
    pallas_call x5, Pallas kernels, call(): pl.pallas_call(kernel, out_shape=tuple(outs), in_specs=in_specs, out_spec...  433 us

profile of v3, /device:TPU:9, one launch (start us, length us, event | category | flops | bytes accessed | tf_op | source)
XLA Modules:
  0.0 467.4 jit_solution(10595832134758212644)
XLA Ops:
  0.7 1.7 convert_element_type.50.refs_0_
  2.4 1.5 reshape.173
  4.0 0.3 reshape.174
  4.4 0.2 stack_reshape.34
  4.6 0.2 stack_reshape.33
  4.7 0.3 pad_maximum_fusion.1
  5.1 0.5 copy.136
  5.5 0.2 reshape.172
  5.9 0.2 reshape.170
  6.2 0.2 reshape.187
  6.4 0.8 maximum_bitcast_fusion.1.col
  7.5 0.6 pad.18.small
  8.1 18.0 %shard_map.314 = (bf16[4,48,1408]{2,1,0:T(8,128)(2,1)}, bf16[4,48,768]{2,1,0:T(8,128)(2,1)}, bf16[4,2,4,16,384]{4,3,2,1,0:T(8,128)(2,1)}) custom-call(bf16[4,48,1408]{2,1,0:T(8,128)(2,1)} %maximum_bitcast_fusion.1.col, bf16[48,768]{1,0:T(8,128)(2,1)} %bitcast.146, bf16[16,384]{1,0:T(8,128)(2,1)} %pad.18.small), custom_call_target="tpu_custom_call" | custom-call | flops 1000 | bytes 20000000 | tf_op jit(solution)/shard_map/pallas_call | solution.py:1361
  26.2 1.1 copy.138
  27.3 0.7 slice_bitcast_fusion.4
  28.1 0.7 fusion.13
  28.8 0.8 slice_bitcast_fusion
  29.6 1.0 convert_bitcast_fusion
  30.6 0.3 fusion.14
  32.7 0.6 slice_bitcast_fusion.6
  33.3 0.4 fusion
  33.9 0.2 select_reduce_fusion
  34.3 0.6 constant_dynamic-slice_fusion.9.refs_6_.refs_4_
  35.0 0.3 compare_reduce_fusion
  35.3 0.6 convert_element_type.57.refs_7_.refs_5_
  35.8 0.5 concatenate.16.refs_8_
  36.3 113.4 %shard_map.315 = (f32[128,768]{1,0:T(8,128)}, bf16[4,128,768]{2,1,0:T(8,128)(2,1)}, bf16[512,384]{1,0:T(8,128)(2,1)}, bf16[2,4,128,384]{3,2,1,0:T(8,128)(2,1)}, ...) custom-call(f32[128,768]{1,0:T(8,128)} %convert_element_type.50.refs, ...), custom_call_target="tpu_custom_call" | custom-call | flops 3000000000 | bytes 20000000 | tf_op jit(solution)/shard_map/pallas_call | solution.py:1361
  149.8 99.2 %shard_map.316 = (f32[128,768]{1,0:T(8,128)}, bf16[4,128,768]{2,1,0:T(8,128)(2,1)}, bf16[512,384]{1,0:T(8,128)(2,1)}, bf16[2,4,128,384]{3,2,1,0:T(8,128)(2,1)}, ...) custom-call(f32[128,768]{1,0:T(8,128)} %get-tuple-element.73.refs_0_, ...), custom_call_target="tpu_custom_call" | custom-call | flops 3000000000 | bytes 20000000 | tf_op jit(solution)/shard_map/pallas_call | solution.py:1361
  249.0 1.7 convert_element_type.58
  250.7 0.8 convert_element_type.59.refs_0_
  251.5 96.0 %shard_map.317 = (f32[128,768]{1,0:T(8,128)}, f32[4,24,768]{2,1,0:T(8,128)}, f32[96,768]{1,0:T(8,128)}, f32[24,768]{1,0:T(8,128)}, bf16[2,4,96,256]{3,2,1,0:T(8,...) custom-call(f32[128,768]{1,0:T(8,128)} %convert_element_type.59.refs_0_, ...), custom_call_target="tpu_custom_call" | custom-call | flops 6000000000 | bytes 20000000 | tf_op jit(solution)/shard_map/pallas_call | solution.py:1361
  347.5 106.8 %shard_map.318 = (f32[128,768]{1,0:T(8,128)}, f32[4,24,768]{2,1,0:T(8,128)}, f32[96,768]{1,0:T(8,128)}, f32[24,768]{1,0:T(8,128)}, f32[4,24,256]{2,1,0:T(8,128)}...) custom-call(f32[128,768]{1,0:T(8,128)} %get-tuple-element.91.refs_0_, ...), custom_call_target="tpu_custom_call" | custom-call | flops 6000000000 | bytes 20000000 | tf_op jit(solution)/shard_map/pallas_call | solution.py:1361
  454.3 1.7 convert_element_type.60
  456.1 1.0 maximum_bitcast_fusion.3
  457.1 0.8 reshape.183
  458.5 0.7 fusion.4
  459.2 0.4 reshape.185
  459.6 0.5 fusion.12
  460.1 0.9 reshape_squeeze.11
  461.2 0.9 reshape_squeeze.12
  462.1 0.7 pad_maximum_fusion.2
  462.8 0.3 stack.71
  463.1 0.3 stack.70
  463.4 0.2 maximum_bitcast_fusion
  463.6 0.5 copy.162
  464.1 1.6 reshape.186
  465.7 0.6 constant_dynamic-slice_fusion.7
  466.3 0.9 pad_maximum_fusion
  (122 shorter events, 3.2 us)
Async XLA Ops:
  2.4 2.0 copy-start.10
  2.4 2.2 copy-start.11
  4.4 1.4 copy-start.12
  5.8 1.5 copy-start.24
  5.8 1.5 copy-start.15
  5.8 1.5 copy-start.16
  5.8 1.5 copy-start.17
  5.8 1.5 copy-start.18
  5.8 1.5 copy-start.19
  5.8 1.5 copy-start.20
  5.9 1.5 copy-start.21
  5.9 1.5 copy-start.22
  5.9 1.5 copy-start.23
  26.2 1.9 copy-start.1
  26.2 2.6 copy-start.2
  29.6 4.3 copy-start.25
  149.7 100.9 %copy-start.7 = (bf16[128,768]{1,0:T(8,128)(2,1)S(1)}, bf16[128,768]{1,0:T(8,128)(2,1)}, u32[]{:S(2)}) copy-start(bf16[128,768]{1,0:T(8,128)(2,1)} %param.35) | copy-start | bytes 589828
  454.3 3.6 copy-start
  454.3 4.8 %copy-start.8 = (f32[4,24,384]{2,1,0:T(8,128)S(1)}, f32[4,24,384]{2,1,0:T(8,128)}, u32[]{:S(2)}) copy-start(f32[4,24,384]{2,1,0:T(8,128)} %get-tuple-element.116) | copy-start | bytes 442372
  454.3 4.8 %copy-start.9 = (f32[4,24,384]{2,1,0:T(8,128)S(1)}, f32[4,24,384]{2,1,0:T(8,128)}, u32[]{:S(2)}) copy-start(f32[4,24,384]{2,1,0:T(8,128)} %get-tuple-element.115) | copy-start | bytes 442372
  460.0 2.0 copy-start.13
  460.1 2.0 copy-start.14
  460.1 2.6 copy-start.5
  461.1 2.0 copy-start.6
  463.6 2.8 copy-start.3
  463.6 2.8 copy-start.4

commit v4 on v3

--- a/solution.py
+++ b/solution.py
@@ -492,14 +492,23 @@
 
 class Spread:
     def __init__(self, run, chunk, full):
-        self.run, self.chunk, self.full = run, chunk, full
-
-    def start(self):
+        self.run, self.chunk, self.full, self.pairs = run, chunk, full, None
+
+    def start(self, cond=None):
         run, place = self.run, self.run.place
         mine = self.full.at[place.z, place.c]
-        self.own = run.local(self.chunk, mine)
-        self.far = [run.launch(self.chunk, mine, place.column(k)) for k in (1, 2, 3)]
-        self.near = [run.launch(self.chunk, mine, place.sibling())]
+        if self.pairs is None:
+            self.own = pltpu.make_async_copy(self.chunk, mine, run.locals.take())
+            self.pairs = [(run.sends.take(), run.recvs.take()) for _ in range(4)]
+        cond = place.z >= 0 if cond is None else cond
+
+        @pl.when(cond)
+        def _():
+            self.own.start()
+
+        there = [place.column(k) for k in (1, 2, 3)] + [place.sibling()]
+        copies = [run.launch_if(cond, self.chunk, mine, self.pairs[i], there[i]) for i in range(4)]
+        self.far, self.near = copies[:3], copies[3:]
 
     def relay(self):
         run, place = self.run, self.run.place
@@ -994,6 +1003,9 @@
         loads = [run.local(qkv_in, wqkv), run.local(o_in, wo.at[pl.ds(0, 192)])]
     run.greet(False)
     came = [None] + [launch(xb.at[f], xb.at[f], place.plane(k)) for k in (1, 2, 3)]
+    m_tasks = [Spread(run, in_c, win), Spread(run, out_c, wout)]
+    if not first:
+        m_tasks[0].start()
     if first:
         a_tasks = [Spread(run, qkv_in, wqkv), SpreadOutput(run, o_in, wo)]
         for t in a_tasks:
@@ -1018,21 +1030,18 @@
         qp[rows, 256:384] = scaled[:, 128:].astype(BF)
     chain = KeyChain(run, trunk, mine, *chain_refs, place_in)
     chain.start()
-    m_tasks = [Spread(run, in_c, win), Spread(run, out_c, wout)]
     run.save(xb, xb_o)
     run.save(qp, qp_o)
     chain.finish()
-    for t in m_tasks:
-        t.start()
+    late_tasks = m_tasks if first else m_tasks[1:]
+    for t in late_tasks:
+        t.start(z > 0)
     pick_parents(kp, chain.slots, choose)
     run.save(kp, kp_o)
     run.save(trunk, trunk_o)
     run.save(mine, mine_o)
     if first:
         a_tasks[1].relay()
-        n_tasks = [Spread(run, qkv_next, wqkv_n), SpreadOutput(run, o_next, wo_n)]
-        for t in n_tasks:
-            t.start()
 
     def attend(i, carry):
         h, b = i // 4, lax.rem(i, 4)
@@ -1044,7 +1053,7 @@
             [s[:, :1024], s[:, 1024:1280] + pen[4 + b], s[:, 1280:] + pen[b]], axis=1
         )
         e = jnp.exp(s - jnp.max(s, axis=1, keepdims=True))
-        pb = (e / jnp.sum(e, axis=1, keepdims=True)).astype(BF)
+        pb = (e * (1.0 / jnp.sum(e, axis=1, keepdims=True))).astype(BF)
         p[h, b] = pb
         heads[h, b] = product(pb, keys)
         return carry
@@ -1065,10 +1074,10 @@
         else:
             own[...] = part
     run.save(ctx, ctx_o)
-    for t in m_tasks:
-        t.relay()
     for k in (1, 2, 3):
         back[k].wait_recv()
+    for t in late_tasks:
+        t.start(z == 0)
     total = own[...] + rs1_r[0].astype(F32) + rs1_r[1].astype(F32) + rs1_r[2].astype(F32)
     zz = x_ref[...] + total + vec[1:2, :]
     z1[...] = zz
@@ -1077,6 +1086,12 @@
     hb[f] = hidden.astype(BF)
     came = [None] + [launch(hb.at[f], hb.at[f], place.plane(k)) for k in (1, 2, 3)]
     back = [None]
+    for t in m_tasks:
+        t.relay()
+    if first:
+        n_tasks = [Spread(run, qkv_next, wqkv_n), SpreadOutput(run, o_next, wo_n)]
+        for t in n_tasks:
+            t.start()
     for t in m_tasks:
         t.finish()
     for k in range(4):
@@ -1102,8 +1117,6 @@
     if first:
         run.save(wqkv, wqkv_o)
         run.save(wo.at[pl.ds(0, 192)], wo_o)
-        for t in n_tasks:
-            t.relay()
     for k in (1, 2, 3):
         back[k].wait_recv()
     total = own[...] + rs2_r[0].astype(F32) + rs2_r[1].astype(F32) + rs2_r[2].astype(F32)
@@ -1113,6 +1126,8 @@
     xn_ref[...] = norm_rows(zz, vec[6:7, :], vec[7:8, :])
     if first:
         for t in n_tasks:
+            t.relay()
+        for t in n_tasks:
             t.finish()
     run.close()
 
@@ -1125,8 +1140,8 @@
         del refs[:n]
         return out
 
-    dy_ref, win, wout, vec, place_in, choose, z1, hb, gp, gl, z2 = take(11)
-    late_in = take(9)
+    dy_ref, vec, place_in, choose, z2 = take(5)
+    late_in = take(15)
     if extra:
         pq_in, pk_in, dvec_in = take(3)
     dx_ref, din_o, dout_o, do_o = take(4)
@@ -1134,8 +1149,8 @@
         dq_n, dk_n, dq_o, dk_o, sm_o = take(5)
     else:
         pq, pk, dvec_o = take(3)
-    late = take(9)
-    wqkv, wo, xb, qp, trunk, mine, kp, p, ctx = late
+    late = take(15)
+    wout, gp, win, gl, hb, z1, wo, ctx, trunk, mine, kp, qp, p, xb, wqkv = late
     (
         df, du, da, dctx, dqf, dqkv, dz, dz1, dkt, dself, dpar, tgt, own, rs1_s, rs1_r, rs2_s, rs2_r,
     ) = take(17)
@@ -1150,7 +1165,7 @@
     launch = run.launch
     loads = []
     for n, (src, dst) in enumerate(zip(late_in, late)):
-        loads.append(run.local(src, dst.at[pl.ds(0, 192)] if n == 1 else dst))
+        loads.append(run.local(src, dst.at[pl.ds(0, 192)] if n == 6 else dst))
     wo[192:256, :] = jnp.zeros((64, WIDE), BF)
 
     grad, dgain, dshift = norm_rows_back(z2[...], vec[6:7, :], dy_ref[...])
@@ -1169,6 +1184,8 @@
         t.start()
     back = [None]
     bias = jnp.zeros((1, WIDE), F32)
+    for n in range(3):
+        loads[n].wait()
     for k in range(4):
         g = place.f_at(-k)
         if k:
@@ -1201,12 +1218,15 @@
         split_rows(pin, hb, flat(du), i)
         return carry
 
+    for n in range(3, 5):
+        loads[n].wait()
     lax.fori_loop(0, 2, ffn_grads, 0)
     for t in m_tasks:
         t.start()
     for k in (1, 2, 3):
         back[k].wait_recv()
     up = dz[...] + own[...] + rs1_r[0].astype(F32) + rs1_r[1].astype(F32) + rs1_r[2].astype(F32)
+    loads[5].wait()
     grad, dgain, dshift = norm_rows_back(z1[...], vec[2:3, :], up)
     dvec_o[2:3, :] = dgain
     dvec_o[3:4, :] = dshift
@@ -1221,7 +1241,7 @@
         t.middle()
     dkt[...] = jnp.zeros_like(dkt)
     lane = lax.broadcasted_iota(jnp.int32, (ROWS, 128), 1)
-    for a in loads:
+    for a in loads[6:]:
         a.wait()
     for k in range(4):
         g = place.f_at(-k)
@@ -1237,6 +1257,7 @@
     for cc in range(2):
         po[cc] = value[96 * cc : 96 * (cc + 1), :]
     o_task.start()
+    o_task.middle()
 
     def attend(i, carry):
         h, b = i // 4, lax.rem(i, 4)
@@ -1281,7 +1302,8 @@
         dqkv[g, :, 0:128] = ahead.astype(BF)
         dqkv[g, :, 128:256] = jnp.where(lane < 64, dqf[2, rows, :], 0.0).astype(BF)
     chain.middle()
-    o_task.middle()
+    for t in m_tasks:
+        t.end()
     chain.pass_on()
 
     def q_grads(i, carry):
@@ -1289,11 +1311,25 @@
         return carry
 
     lax.fori_loop(0, 2, q_grads, 0)
+    end_tasks = []
+    if extra:
+        end_tasks = [Collect(run, pk, nk2, fk2, tk2, dk_o), Collect(run, pq, nq2, fq2, tq2, dq_o)]
+        end_tasks[1].start()
 
     def store(ft, value):
         dqkv[ft, :, 256:] = value.astype(BF)
 
     chain.finish(place_in, store)
+
+    def k_grads(i, carry):
+        split_rows(pk, xb, dqkv[:, :, 256:].reshape(512, SLICE), i)
+        return carry
+
+    lax.fori_loop(0, 2, k_grads, 0)
+    if extra:
+        end_tasks[0].start()
+        end_tasks[1].middle()
+        end_tasks[0].middle()
     back = [None]
     for k in (1, 2, 3, 0):
         g = place.f_at(-k)
@@ -1304,28 +1340,16 @@
         else:
             own[...] = part
 
-    def k_grads(i, carry):
-        split_rows(pk, xb, dqkv[:, :, 256:].reshape(512, SLICE), i)
-        return carry
-
-    lax.fori_loop(0, 2, k_grads, 0)
     sums = jnp.sum(flat(dqkv).astype(F32), axis=0, keepdims=True)
     dvec_o[0:1, :] = jnp.concatenate([sums, jnp.zeros((1, WIDE - PACKED), F32)], axis=1)
-    end_tasks = []
     if extra:
-        end_tasks = [Collect(run, pk, nk2, fk2, tk2, dk_o), Collect(run, pq, nq2, fq2, tq2, dq_o)]
-        for t in end_tasks:
-            t.start()
         sm[0:8, :] = dvec_o[...]
         sm[8:16, :] = dvec_in[...]
         sm_near = launch(sm, sm_a, place.sibling())
-        for t in end_tasks:
-            t.middle()
         sm_near.wait_recv()
         sm_a[...] = sm[...] + sm_a[...]
         sm_far = [launch(sm_a, sm_b.at[k - 1], place.column(k)) for k in (1, 2, 3)]
-    for t in m_tasks + [o_task]:
-        t.end()
+    o_task.end()
     for t in a_tasks:
         t.last()
     for k in (1, 2, 3):
@@ -1425,7 +1449,7 @@
     sums, sums2 = shape(8, WIDE, dtype=F32), shape(16, WIDE, dtype=F32)
     outs = (LOCAL, shape(4, 24, WIDE, dtype=F32), shape(96, WIDE, dtype=F32), shape(24, WIDE, dtype=F32))
     outs += SHARES + SHARES + (shape(4, 16, WIDE, dtype=F32),) if extra else PARTS + (sums,)
-    scratch = [QKV, shape(256, WIDE)] + list(SAVED[:7]) + [
+    scratch = [BIG, SAVED[9], BIG, FULL, FULL, LOCAL, shape(256, WIDE), SAVED[6], HALVES, HALVES, SAVED[4], SAVED[1], SAVED[5], FULL, QKV] + [
         FULL, FULL, FULL, shape(512, SLICE), shape(3, 512, 128, dtype=F32), shape(4, ROWS, PACKED), LOCAL, LOCAL,
         shape(1024, SLICE, dtype=F32), keys, keys, shape(2, 3, 4, ROWS, SLICE), LOCAL, PIECE, PIECE, PIECE, PIECE,
         shape(3, 4, ROWS, SLICE),
@@ -1440,8 +1464,8 @@
         scratch += [sums2, sums2, shape(3, 16, WIDE, dtype=F32), sums2]
     return call(
         lambda *refs: backward_kernel(extra, *refs), 4 if extra else 3, outs, (VM,) * len(outs),
-        [VM] * 4 + [SM] * 2 + [VM] * 5 + [ANY] * 9 + [VM] * len(before), scratch,
-        (upstream, win, wout, vec, place_in, choose, z1, hb, gp, gl, z2, wqkv, wo, xb, qp, trunk, mine, kp, p, ctx)
+        [VM] * 2 + [SM] * 2 + [VM] + [ANY] * 15 + [VM] * len(before), scratch,
+        (upstream, vec, place_in, choose, z2, wout, gp, win, gl, hb, z1, wo, ctx, trunk, mine, kp, qp, p, xb, wqkv)
         + tuple(before),
         6 * 10**9,
     )

time: 475 us -> 446 us (0.939)
  Pallas kernels: 433 us -> 406 us
    pallas_call x5, Pallas kernels: 433 us -> 406 us  [call(): pl.pallas_call(kernel, out_shape=tuple(outs), in_specs=in_specs, out_spec...]
where the time goes in v4:
time: 446 us; the launch traced here: 440 us
  Pallas kernels  406 us (91%)
  local copies, waits for them, and re-layouts  19.7 us (4%)
  other arithmetic  12.4 us (3%)
    pallas_call x5, Pallas kernels, call(): pl.pallas_call(kernel, out_shape=tuple(outs), in_specs=in_specs, out_spec...  406 us

profile of v4, /device:TPU:9, one launch (start us, length us, event | category | flops | bytes accessed | tf_op | source)
XLA Modules:
  0.0 440.0 jit_solution(897989867940441529)
XLA Ops:
  0.7 1.7 convert_element_type.50.refs_0_
  2.4 1.5 reshape.173
  4.0 0.3 reshape.174
  4.4 0.2 stack_reshape.34
  4.6 0.2 stack_reshape.33
  4.7 0.3 pad_maximum_fusion.1
  5.1 0.5 copy.136
  5.5 0.2 reshape.172
  5.9 0.2 reshape.170
  6.2 0.2 reshape.187
  6.4 0.8 maximum_bitcast_fusion.1.col
  7.5 0.6 pad.18.small
  8.1 18.0 %shard_map.314 = (bf16[4,48,1408]{2,1,0:T(8,128)(2,1)}, bf16[4,48,768]{2,1,0:T(8,128)(2,1)}, bf16[4,2,4,16,384]{4,3,2,1,0:T(8,128)(2,1)}) custom-call(bf16[4,48,1408]{2,1,0:T(8,128)(2,1)} %maximum_bitcast_fusion.1.col, bf16[48,768]{1,0:T(8,128)(2,1)} %bitcast.146, bf16[16,384]{1,0:T(8,128)(2,1)} %pad.18.small), custom_call_target="tpu_custom_call" | custom-call | flops 1000 | bytes 20000000 | tf_op jit(solution)/shard_map/pallas_call | solution.py:1385
  26.2 1.1 copy.138
  27.3 0.7 slice_bitcast_fusion.4
  28.1 0.7 fusion.13
  28.8 0.8 slice_bitcast_fusion
  29.6 1.0 convert_bitcast_fusion
  30.6 0.3 fusion.14
  32.7 0.6 slice_bitcast_fusion.6
  33.3 0.4 fusion
  33.9 0.2 select_reduce_fusion
  34.3 0.6 constant_dynamic-slice_fusion.9.refs_6_.refs_2_
  35.0 0.3 compare_reduce_fusion
  35.3 0.6 convert_element_type.57.refs_7_.refs_3_
  35.8 0.5 concatenate.16.refs_8_
  36.3 97.5 %shard_map.315 = (f32[128,768]{1,0:T(8,128)}, bf16[4,128,768]{2,1,0:T(8,128)(2,1)}, bf16[512,384]{1,0:T(8,128)(2,1)}, bf16[2,4,128,384]{3,2,1,0:T(8,128)(2,1)}, ...) custom-call(f32[128,768]{1,0:T(8,128)} %convert_element_type.50.refs, ...), custom_call_target="tpu_custom_call" | custom-call | flops 3000000000 | bytes 20000000 | tf_op jit(solution)/shard_map/pallas_call | solution.py:1385
  133.9 77.2 %shard_map.316 = (f32[128,768]{1,0:T(8,128)}, bf16[4,128,768]{2,1,0:T(8,128)(2,1)}, bf16[512,384]{1,0:T(8,128)(2,1)}, bf16[2,4,128,384]{3,2,1,0:T(8,128)(2,1)}, ...) custom-call(f32[128,768]{1,0:T(8,128)} %get-tuple-element.73.refs_0_, ...), custom_call_target="tpu_custom_call" | custom-call | flops 3000000000 | bytes 20000000 | tf_op jit(solution)/shard_map/pallas_call | solution.py:1385
  211.1 1.7 convert_element_type.58
  212.8 0.8 convert_element_type.59.refs_0_
  213.6 102.2 %shard_map.317 = (f32[128,768]{1,0:T(8,128)}, f32[4,24,768]{2,1,0:T(8,128)}, f32[96,768]{1,0:T(8,128)}, f32[24,768]{1,0:T(8,128)}, bf16[2,4,96,256]{3,2,1,0:T(8,...) custom-call(f32[128,768]{1,0:T(8,128)} %convert_element_type.59.refs_0_, ...), custom_call_target="tpu_custom_call" | custom-call | flops 6000000000 | bytes 20000000 | tf_op jit(solution)/shard_map/pallas_call | solution.py:1385
  315.8 111.1 %shard_map.318 = (f32[128,768]{1,0:T(8,128)}, f32[4,24,768]{2,1,0:T(8,128)}, f32[96,768]{1,0:T(8,128)}, f32[24,768]{1,0:T(8,128)}, f32[4,24,256]{2,1,0:T(8,128)}...) custom-call(f32[128,768]{1,0:T(8,128)} %get-tuple-element.91.refs_0_, ...), custom_call_target="tpu_custom_call" | custom-call | flops 6000000000 | bytes 20000000 | tf_op jit(solution)/shard_map/pallas_call | solution.py:1385
  426.9 1.7 convert_element_type.60
  428.6 1.0 maximum_bitcast_fusion.3
  429.7 0.8 reshape.183
  431.0 0.7 fusion.4
  431.8 0.4 reshape.185
  432.2 0.5 fusion.12
  432.7 0.9 reshape_squeeze.11
  433.7 0.9 reshape_squeeze.12
  434.7 0.7 pad_maximum_fusion.2
  435.3 0.3 stack.71
  435.6 0.3 stack.70
  435.9 0.2 maximum_bitcast_fusion
  436.2 0.5 copy.162
  436.7 1.6 reshape.186
  438.3 0.6 constant_dynamic-slice_fusion.7
  438.9 0.9 pad_maximum_fusion
  (122 shorter events, 3.2 us)
Async XLA Ops:
  2.4 2.0 copy-start.10
  2.4 2.2 copy-start.11
  4.4 1.4 copy-start.12
  5.8 1.5 copy-start.24
  5.8 1.5 copy-start.15
  5.8 1.5 copy-start.16
  5.8 1.5 copy-start.17
  5.8 1.5 copy-start.18
  5.8 1.5 copy-start.19
  5.8 1.5 copy-start.20
  5.9 1.5 copy-start.21
  5.9 1.5 copy-start.22
  5.9 1.5 copy-start.23
  26.2 1.9 copy-start.1
  26.2 2.6 copy-start.2
  29.6 4.3 copy-start.25
  133.9 78.9 %copy-start.7 = (bf16[128,768]{1,0:T(8,128)(2,1)S(1)}, bf16[128,768]{1,0:T(8,128)(2,1)}, u32[]{:S(2)}) copy-start(bf16[128,768]{1,0:T(8,128)(2,1)} %param.35) | copy-start | bytes 589828
  426.9 3.6 copy-start
  426.9 4.8 %copy-start.8 = (f32[4,24,384]{2,1,0:T(8,128)S(1)}, f32[4,24,384]{2,1,0:T(8,128)}, u32[]{:S(2)}) copy-start(f32[4,24,384]{2,1,0:T(8,128)} %get-tuple-element.116) | copy-start | bytes 442372
  426.9 4.8 %copy-start.9 = (f32[4,24,384]{2,1,0:T(8,128)S(1)}, f32[4,24,384]{2,1,0:T(8,128)}, u32[]{:S(2)}) copy-start(f32[4,24,384]{2,1,0:T(8,128)} %get-tuple-element.115) | copy-start | bytes 442372
  432.6 2.0 copy-start.13
  432.6 2.0 copy-start.14
  432.7 2.6 copy-start.5
  433.7 2.0 copy-start.6
  436.1 2.8 copy-start.3
  436.1 2.8 copy-start.4

commit v5 on v4

--- a/solution.py
+++ b/solution.py
@@ -764,61 +764,82 @@
     run.close()
 
 
+class TrunkRows:
+    def __init__(self, run, xb, tx):
+        self.run, self.xb, self.tx = run, xb, tx
+
+    def start(self):
+        run, place = self.run, self.run.place
+        self.parts = [pl.ds(0, 64), pl.ds(64, 64)]
+        self.pairs = [(run.sends.take(), run.recvs.take()) for _ in range(2)]
+        for q in range(2):
+            run.launch_if(
+                place.z == 0, self.xb.at[place.f, self.parts[q]], self.tx.at[place.f, self.parts[q]],
+                self.pairs[q], place.column(1),
+            )
+
+    def pass_on(self):
+        run, place = self.run, self.run.place
+        self.round = []
+        for q in range(2):
+            block = self.tx.at[place.f, self.parts[q]]
+
+            @pl.when(place.z > 0)
+            def _():
+                remote(block, block, self.pairs[q], place.column(1)).wait_recv()
+
+            between = jnp.logical_and(place.z > 0, place.z < 3)
+            run.launch_if(between, block, block, self.pairs[q], place.column(1))
+            for k in (1, 2, 3):
+                pair = (run.sends.take(), run.recvs.take())
+                self.round.append((k, run.launch_if(place.z > 0, block, block, pair, place.plane(k))))
+
+    def wait(self, k):
+        for kk, a in self.round:
+            if kk == k:
+                a.wait_recv()
+
+
 class KeyChain:
-    def __init__(self, run, trunk, mine, slots, up, down, cs, up_out, down_out, place_in):
-        self.run, self.trunk, self.mine, self.slots = run, trunk, mine, slots
+    def __init__(self, run, mine, slots, up, down, cs, up_out, down_out, place_in):
+        self.run, self.mine, self.slots = run, mine, slots
         self.up, self.down, self.cs, self.up_out, self.down_out, self.place_in = up, down, cs, up_out, down_out, place_in
 
     def start(self):
         run, place = self.run, self.run.place
         z, c = place.z, place.c
-        self.pairs = [[(run.sends.take(), run.recvs.take()) for _ in range(4)] for _ in range(3)]
-        for j in range(4):
-            run.launch_if(z == 0, self.mine.at[c, j], self.trunk.at[c, j], self.pairs[0][j], place.column(1))
-        self.near = [run.launch(self.mine.at[c], self.mine.at[c], place.sibling())]
-
-        @pl.when(z == 0)
-        def _():
-            self.trunk[c] = self.mine[c]
-
+        self.pairs = [[(run.sends.take(), run.recvs.take()) for _ in range(4)] for _ in range(2)]
         for j in range(4):
             total = self.mine[c, 0] * self.place_in[j, 0].astype(BF)
             for ft in range(1, 4):
                 total = total + self.mine[c, ft] * self.place_in[j, ft].astype(BF)
             self.cs[j] = total
-            run.launch_if(z == 1, self.cs.at[j], self.up.at[j], self.pairs[1][j], place.column(1))
-            run.launch_if(z == 3, self.cs.at[j], self.down.at[j], self.pairs[2][j], place.column(-1))
+            run.launch_if(z == 1, self.cs.at[j], self.up.at[j], self.pairs[0][j], place.column(1))
+            run.launch_if(z == 3, self.cs.at[j], self.down.at[j], self.pairs[1][j], place.column(-1))
+        self.near = [run.launch(self.mine.at[c], self.mine.at[c], place.sibling())]
 
     def wait(self, which, j):
-        dst = (self.trunk.at[self.run.place.c, j], self.up.at[j], self.down.at[j])[which]
+        dst = (self.up.at[j], self.down.at[j])[which]
         remote(dst, dst, self.pairs[which][j], self.run.place.column(1)).wait_recv()
 
     def finish(self):
         run, place = self.run, self.run.place
         z, c = place.z, place.c
-        trunk = [self.trunk.at[c, j] for j in range(4)]
         for j in range(4):
 
-            @pl.when(z == 1)
+            @pl.when(z == 2)
             def _(j=j):
                 self.wait(0, j)
-
-            run.launch_if(z == 1, trunk[j], trunk[j], self.pairs[0][j], place.column(1))
-        for j in range(4):
+                self.up_out[j] = self.cs[j] + self.up[j]
+
+            run.launch_if(z == 2, self.up_out.at[j], self.up.at[j], self.pairs[0][j], place.column(1))
 
             @pl.when(z == 2)
             def _(j=j):
                 self.wait(1, j)
-                self.up_out[j] = self.cs[j] + self.up[j]
-
-            run.launch_if(z == 2, self.up_out.at[j], self.up.at[j], self.pairs[1][j], place.column(1))
-
-            @pl.when(z == 2)
-            def _(j=j):
-                self.wait(2, j)
                 self.down_out[j] = self.cs[j] + self.down[j]
 
-            run.launch_if(z == 2, self.down_out.at[j], self.down.at[j], self.pairs[2][j], place.column(-1))
+            run.launch_if(z == 2, self.down_out.at[j], self.down.at[j], self.pairs[1][j], place.column(-1))
 
             @pl.when(z == 2)
             def _(j=j):
@@ -826,35 +847,21 @@
 
         for j in range(4):
 
-            @pl.when(z == 2)
-            def _(j=j):
-                self.wait(0, j)
-
-            run.launch_if(z == 2, trunk[j], trunk[j], self.pairs[0][j], place.column(1))
-        for j in range(4):
-
             @pl.when(z == 0)
             def _(j=j):
                 self.slots[c, j] = self.cs[j]
 
             @pl.when(z == 1)
             def _(j=j):
-                self.wait(2, j)
+                self.wait(1, j)
                 self.slots[c, j] = self.cs[j] + self.down[j]
 
             @pl.when(z == 3)
             def _(j=j):
-                self.wait(1, j)
+                self.wait(0, j)
                 self.slots[c, j] = self.cs[j] + self.up[j]
 
         self.near.append(run.launch(self.slots.at[c], self.slots.at[c], place.sibling()))
-
-        @pl.when(z == 3)
-        def _():
-            for j in range(4):
-                self.wait(0, j)
-
-        self.near.append(run.launch(self.trunk.at[c], self.trunk.at[c], place.sibling()))
         for a in self.near:
             a.wait_recv()
 
@@ -984,14 +991,20 @@
         del refs[:n]
         return out
 
-    x_ref, qkv_in, o_in, in_c, out_c, vec, place_in, choose, pen = take(9)
+    x_ref, chunks, rows_o, rows_out, vecs, place_in, choose, pen = take(8)
+    if not first:
+        qkv_in, o_in = take(2)
+    layer = 0 if first else 1
+    vec = vecs.at[layer]
+    in_c, out_c = chunks.at[layer, :, pl.ds(PACKED, WIDE)], rows_out.at[layer]
     if first:
-        qkv_next, o_next = take(2)
+        qkv_in, o_in = chunks.at[0, :, pl.ds(0, PACKED)], rows_o.at[0]
+        qkv_next, o_next = chunks.at[1, :, pl.ds(0, PACKED)], rows_o.at[1]
     xn_ref, xb_o, qp_o, trunk_o, mine_o, kp_o, p_o, ctx_o, z1_o, hb_o, gp_o, gl_o, z2_o, win_o, wout_o = take(15)
     if first:
         wqkv_o, wo_o, wqkv_n, wo_n = take(4)
     xb, qp, trunk, mine, kp, p, ctx, z1, hb, gp, gl, z2, win, wout, wqkv, wo, heads, own, rs1_s, rs1_r, rs2_s, rs2_r = take(22)
-    chain_refs = take(6)
+    tx, *chain_refs = take(7)
     run = Run(*refs)
     place = run.place
     z, f, c = place.z, place.f, place.c
@@ -1003,16 +1016,18 @@
         loads = [run.local(qkv_in, wqkv), run.local(o_in, wo.at[pl.ds(0, 192)])]
     run.greet(False)
     came = [None] + [launch(xb.at[f], xb.at[f], place.plane(k)) for k in (1, 2, 3)]
+    trunk_rows = TrunkRows(run, xb, tx)
+    trunk_rows.start()
     m_tasks = [Spread(run, in_c, win), Spread(run, out_c, wout)]
-    if not first:
-        m_tasks[0].start()
     if first:
         a_tasks = [Spread(run, qkv_in, wqkv), SpreadOutput(run, o_in, wo)]
         for t in a_tasks:
             t.start()
+        trunk_rows.pass_on()
         a_tasks[0].relay()
         a_tasks[0].finish()
     else:
+        trunk_rows.pass_on()
         for a in loads:
             a.wait()
     lane = lax.broadcasted_iota(jnp.int32, (ROWS, 128), 1)
@@ -1028,12 +1043,28 @@
         qp[rows, 0:128] = jnp.where(lane < 64, front, 0.0).astype(BF)
         qp[rows, 128:256] = jnp.where(lane < 64, pltpu.roll(front, 64, 1), 0.0).astype(BF)
         qp[rows, 256:384] = scaled[:, 128:].astype(BF)
-    chain = KeyChain(run, trunk, mine, *chain_refs, place_in)
+    chain = KeyChain(run, mine, *chain_refs, place_in)
     chain.start()
+
+    @pl.when(z == 0)
+    def _():
+        trunk[c] = mine[c]
+
+    @pl.when(z > 0)
+    def _():
+        for k in range(4):
+            g = place.f_at(-k)
+            if k:
+                trunk_rows.wait(k)
+            keys = product(tx[g], flat(wqkv)[:, 256:]) + vec[0:1, 256:PACKED]
+            trunk[c, g] = keys.astype(BF)
+
+    trunk_near = launch(trunk.at[c], trunk.at[c], place.sibling())
     run.save(xb, xb_o)
     run.save(qp, qp_o)
     chain.finish()
-    late_tasks = m_tasks if first else m_tasks[1:]
+    trunk_near.wait_recv()
+    late_tasks = m_tasks
     for t in late_tasks:
         t.start(z > 0)
     pick_parents(kp, chain.slots, choose)
@@ -1079,7 +1110,7 @@
     for t in late_tasks:
         t.start(z == 0)
     total = own[...] + rs1_r[0].astype(F32) + rs1_r[1].astype(F32) + rs1_r[2].astype(F32)
-    zz = x_ref[...] + total + vec[1:2, :]
+    zz = x_ref[...].astype(F32) + total + vec[1:2, :]
     z1[...] = zz
     run.save(z1, z1_o)
     hidden = norm_rows(zz, vec[2:3, :], vec[3:4, :])
@@ -1123,7 +1154,7 @@
     zz = norm_rows(z1[...], vec[2:3, :], vec[3:4, :]) + total + vec[5:6, :]
     z2[...] = zz
     run.save(z2, z2_o)
-    xn_ref[...] = norm_rows(zz, vec[6:7, :], vec[7:8, :])
+    xn_ref[...] = norm_rows(zz, vec[6:7, :], vec[7:8, :]).astype(xn_ref.dtype)
     if first:
         for t in n_tasks:
             t.relay()
@@ -1140,7 +1171,8 @@
         del refs[:n]
         return out
 
-    dy_ref, vec, place_in, choose, z2 = take(5)
+    dy_ref, vecs, place_in, choose, z2 = take(5)
+    vec = vecs.at[0 if extra else 1]
     late_in = take(15)
     if extra:
         pq_in, pk_in, dvec_in = take(3)
@@ -1168,7 +1200,7 @@
         loads.append(run.local(src, dst.at[pl.ds(0, 192)] if n == 6 else dst))
     wo[192:256, :] = jnp.zeros((64, WIDE), BF)
 
-    grad, dgain, dshift = norm_rows_back(z2[...], vec[6:7, :], dy_ref[...])
+    grad, dgain, dshift = norm_rows_back(z2[...], vec[6:7, :], dy_ref[...].astype(F32))
     dvec_o[6:7, :] = dgain
     dvec_o[7:8, :] = dshift
     dz[...] = grad
@@ -1354,7 +1386,8 @@
         t.last()
     for k in (1, 2, 3):
         back[k].wait_recv()
-    dx_ref[...] = dz1[...] + own[...] + rs2_r[0].astype(F32) + rs2_r[1].astype(F32) + rs2_r[2].astype(F32)
+    total = dz1[...] + own[...] + rs2_r[0].astype(F32) + rs2_r[1].astype(F32) + rs2_r[2].astype(F32)
+    dx_ref[...] = total.astype(dx_ref.dtype)
     if extra:
         for t in end_tasks:
             t.end()
@@ -1419,15 +1452,15 @@
 )
 
 
-def forward_layer(first, state, qkv, o, in_c, out_c, vec, place_in, choose, pen, following):
-    outs = (LOCAL,) + SAVED + (BIG, BIG) + ((QKV, OUTPUT, QKV, OUTPUT) if first else ())
+def forward_layer(first, state, chunks, rows_o, rows_out, vecs, place_in, choose, pen, here):
+    outs = (LOCAL if first else shape(ROWS, WIDE),) + SAVED + (BIG, BIG) + ((QKV, OUTPUT, QKV, OUTPUT) if first else ())
     got = call(
         lambda *refs: forward_kernel(first, *refs), 1 if first else 2, outs, (VM,) + (ANY,) * (len(outs) - 1),
-        [VM] + [ANY] * 4 + [VM] + [SM] * 3 + [ANY] * len(following),
+        [VM] + [ANY] * 3 + [VM] + [SM] * 3 + [ANY] * len(here),
         list(SAVED)
         + [BIG, BIG, QKV, shape(256, WIDE), shape(3, 4, ROWS, 128, dtype=F32), LOCAL]
-        + [PIECE] * 4 + [HALVES] + [QUARTERS] * 5,
-        (state, qkv, o, in_c, out_c, vec, place_in, choose, pen) + tuple(following), 3 * 10**9,
+        + [PIECE] * 4 + [FULL, HALVES] + [QUARTERS] * 5,
+        (state, chunks, rows_o, rows_out, vecs, place_in, choose, pen) + tuple(here), 3 * 10**9,
     )
     return got[0], got[1:13], got[13:]
 
@@ -1447,7 +1480,8 @@
     keys = shape(4, 256, SLICE, dtype=F32)
     extra = len(before) > 0
     sums, sums2 = shape(8, WIDE, dtype=F32), shape(16, WIDE, dtype=F32)
-    outs = (LOCAL, shape(4, 24, WIDE, dtype=F32), shape(96, WIDE, dtype=F32), shape(24, WIDE, dtype=F32))
+    outs = (shape(ROWS, WIDE) if extra else LOCAL,)
+    outs += (shape(4, 24, WIDE, dtype=F32), shape(96, WIDE, dtype=F32), shape(24, WIDE, dtype=F32))
     outs += SHARES + SHARES + (shape(4, 16, WIDE, dtype=F32),) if extra else PARTS + (sums,)
     scratch = [BIG, SAVED[9], BIG, FULL, FULL, LOCAL, shape(256, WIDE), SAVED[6], HALVES, HALVES, SAVED[4], SAVED[1], SAVED[5], FULL, QKV] + [
         FULL, FULL, FULL, shape(512, SLICE), shape(3, 512, 128, dtype=F32), shape(4, ROWS, PACKED), LOCAL, LOCAL,
@@ -1513,21 +1547,14 @@
         [jnp.where(jnp.any(match, axis=(1, 2)), 0.0, MASKED), jnp.where(z > 0, jnp.zeros((4,), F32), MASKED)]
     ).astype(F32)
 
-    qkv_c = [colp[i, :, :PACKED] for i in range(2)]
-    in_c = [colp[i, :, PACKED:] for i in range(2)]
-    state, kept0, (win0, wout0, wqkv0, wo0, wqkv1, wo1) = forward_layer(
-        True, activations.astype(F32), qkv_c[0], op[0], in_c[0], outer_weight[0], vecs[0], place_in, choose, pen,
-        (qkv_c[1], op[1]),
-    )
-    state, kept1, (win1, wout1) = forward_layer(
-        False, state, wqkv1, wo1, in_c[1], outer_weight[1], vecs[1], place_in, choose, pen, ()
-    )
-    outcome = state.astype(BF)
+    shared = (colp, op, outer_weight, vecs, place_in, choose, pen)
+    state, kept0, (win0, wout0, wqkv0, wo0, wqkv1, wo1) = forward_layer(True, activations, *shared, ())
+    outcome, kept1, (win1, wout1) = forward_layer(False, state, *shared, (wqkv1, wo1))
     upstream, din1, dout1, do1, pq, pk, dvec1 = backward_layer(
-        cotangent.astype(F32), (wqkv1, wo1, win1, wout1), vecs[1], place_in, choose, kept1, ()
+        cotangent, (wqkv1, wo1, win1, wout1), vecs, place_in, choose, kept1, ()
     )
     upstream, din0, dout0, do0, dq1, dk1, dq0, dk0, rsm = backward_layer(
-        upstream, (wqkv0, wo0, win0, wout0), vecs[0], place_in, choose, kept0, (pq, pk, dvec1)
+        upstream, (wqkv0, wo0, win0, wout0), vecs, place_in, choose, kept0, (pq, pk, dvec1)
     )
     dq = jnp.stack([dq0, dq1]).transpose(0, 2, 1, 3)[..., :192].reshape(2, 24, WIDE)
     dkv = jnp.stack([dk0, dk1]).transpose(0, 2, 1, 3).reshape(2, 24, 4, 3, 2, 64)
@@ -1543,7 +1570,7 @@
     dib = lax.dynamic_index_in_dim(rsm[:, :, 4], f, 0, keepdims=False)
     dib = lax.dynamic_slice_in_dim(dib, 96 * (2 * z + c), 96, 1)
     return (
-        outcome, upstream.astype(BF), dq, rows[0], dk, dv, rows[1], jnp.stack([do0, do1]), rows[2], rows[3], rows[4],
+        outcome, upstream, dq, rows[0], dk, dv, rows[1], jnp.stack([do0, do1]), rows[2], rows[3], rows[4],
         dinner, dib, jnp.stack([dout0, dout1]), rows[5], rows[6], rows[7],
     )
 

time: 446 us -> 431 us (0.966)
  Pallas kernels: 406 us -> 395 us
  other arithmetic: 12.4 us -> 6.62 us
    pallas_call x5, Pallas kernels: 406 us -> 395 us  [call(): pl.pallas_call(kernel, out_shape=tuple(outs), in_specs=in_specs, out_spec...]
    convert_element_type x4 -> x0, other arithmetic: 5.91 us -> none  [the longest x1 1.75 us: slice_body(): upstream.astype(BF)]
where the time goes in v5:
time: 431 us; the launch traced here: 424 us
  Pallas kernels  395 us (92%)
  local copies, waits for them, and re-layouts  21.2 us (5%)
  other arithmetic  6.62 us (2%)
    pallas_call x5, Pallas kernels, call(): pl.pallas_call(kernel, out_shape=tuple(outs), in_specs=in_specs, out_spec...  395 us

profile of v5, /device:TPU:9, one launch (start us, length us, event | category | flops | bytes accessed | tf_op | source)
XLA Modules:
  0.0 424.3 jit_solution(16725996551231483865)
XLA Ops:
  0.7 1.5 reshape.171
  2.2 0.2 copy.198
  2.3 0.3 reshape.172
  2.7 0.2 stack_reshape.34
  2.9 0.2 stack_reshape.33
  3.1 0.3 pad_maximum_fusion.1
  3.4 0.5 copy.136
  3.9 0.2 reshape.170
  4.2 0.2 reshape.168
  4.4 0.1 pad.17
  4.5 0.2 reshape.186
  4.7 0.8 maximum_bitcast_fusion.1.col
  5.8 0.6 pad.18.small
  6.4 18.0 %shard_map.314 = (bf16[4,48,1408]{2,1,0:T(8,128)(2,1)}, bf16[4,48,768]{2,1,0:T(8,128)(2,1)}, bf16[4,2,4,16,384]{4,3,2,1,0:T(8,128)(2,1)}) custom-call(bf16[4,48,1408]{2,1,0:T(8,128)(2,1)} %maximum_bitcast_fusion.1.col, bf16[48,768]{1,0:T(8,128)(2,1)} %bitcast.127, bf16[16,384]{1,0:T(8,128)(2,1)} %pad.18.small), custom_call_target="tpu_custom_call" | custom-call | flops 1000 | bytes 20000000 | tf_op jit(solution)/shard_map/pallas_call | solution.py:1418
  24.5 1.9 copy.138
  26.4 0.7 copy.139
  27.1 1.0 convert_bitcast_fusion
  28.1 0.3 fusion.13
  29.1 0.1 stack_reshape.35
  30.1 0.7 stack.59.refs_4_.refs_1_
  30.8 0.4 fusion
  31.4 0.2 select_reduce_fusion
  31.8 0.7 constant_dynamic-slice_fusion.9.refs_5_.refs_2_
  32.5 0.3 compare_reduce_fusion
  32.8 0.6 convert_element_type.44.refs_6_.refs_3_
  33.4 0.5 concatenate.16.refs_7_
  33.9 94.7 %shard_map.315 = (f32[128,768]{1,0:T(8,128)}, bf16[4,128,768]{2,1,0:T(8,128)(2,1)}, bf16[512,384]{1,0:T(8,128)(2,1)}, bf16[2,4,128,384]{3,2,1,0:T(8,128)(2,1)}, ...) custom-call(bf16[128,768]{1,0:T(8,128)(2,1)} %refs_0_.2, ...), custom_call_target="tpu_custom_call" | custom-call | flops 3000000000 | bytes 20000000 | tf_op jit(solution)/shard_map/pallas_call | solution.py:1418
  128.6 79.8 %shard_map.316 = (bf16[128,768]{1,0:T(8,128)(2,1)}, bf16[4,128,768]{2,1,0:T(8,128)(2,1)}, bf16[512,384]{1,0:T(8,128)(2,1)}, bf16[2,4,128,384]{3,2,1,0:T(8,128)(2...) custom-call(f32[128,768]{1,0:T(8,128)} %get-tuple-element.73.refs_0_, ...), custom_call_target="tpu_custom_call" | custom-call | flops 3000000000 | bytes 20000000 | tf_op jit(solution)/shard_map/pallas_call | solution.py:1418
  208.4 92.9 %shard_map.317 = (f32[128,768]{1,0:T(8,128)}, f32[4,24,768]{2,1,0:T(8,128)}, f32[96,768]{1,0:T(8,128)}, f32[24,768]{1,0:T(8,128)}, bf16[2,4,96,256]{3,2,1,0:T(8,...) custom-call(bf16[128,768]{1,0:T(8,128)(2,1)} %refs_0_.3, f32[2,8,768]{2,1,0:T(8,128)} %stack.59.refs_4_.refs_1_, ...), custom_call_target="tpu_custom_call" | custom-call | flops 6000000000 | bytes 20000000 | tf_op jit(solution)/shard_map/pallas_call | solution.py:1418
  301.3 109.3 %shard_map.318 = (bf16[128,768]{1,0:T(8,128)(2,1)}, f32[4,24,768]{2,1,0:T(8,128)}, f32[96,768]{1,0:T(8,128)}, f32[24,768]{1,0:T(8,128)}, f32[4,24,256]{2,1,0:T(8...) custom-call(f32[128,768]{1,0:T(8,128)} %get-tuple-element.91.refs_0_, ...), custom_call_target="tpu_custom_call" | custom-call | flops 6000000000 | bytes 20000000 | tf_op jit(solution)/shard_map/pallas_call | solution.py:1418
  410.7 1.0 maximum_bitcast_fusion.3
  411.8 0.8 reshape.182
  412.6 0.8 slice.148
  414.0 0.7 fusion.4
  414.7 0.4 reshape.184
  415.1 0.5 fusion.12
  415.7 0.9 reshape_squeeze.11
  416.7 0.9 reshape_squeeze.12
  417.6 0.7 pad_maximum_fusion.2
  418.3 0.3 stack.71
  418.6 0.3 stack.70
  418.9 0.2 maximum_bitcast_fusion
  419.1 0.5 copy.162
  419.6 1.6 reshape.185
  421.2 0.6 constant_dynamic-slice_fusion.7
  421.9 0.9 pad_maximum_fusion
  422.7 0.7 copy.211
  423.4 0.7 copy.212
  (116 shorter events, 2.8 us)
Async XLA Ops:
  0.7 2.0 copy-start.10
  0.7 2.2 copy-start.11
  2.7 1.4 copy-start.12
  4.1 1.5 copy-start.24
  4.1 1.5 copy-start.15
  4.1 1.5 copy-start.16
  4.1 1.5 copy-start.17
  4.1 1.5 copy-start.18
  4.2 1.5 copy-start.19
  4.2 1.5 copy-start.20
  4.2 1.5 copy-start.21
  4.2 1.5 copy-start.22
  4.2 1.5 copy-start.23
  24.5 1.9 copy-start.1
  26.4 4.9 %copy-start.25 = (s32[13]{0:T(128)S(1)}, s32[13]{0:T(128)}, u32[]{:S(2)}) copy-start(s32[13]{0:T(128)} %param.36) | copy-start | bytes 160
  410.7 2.9 copy-start
  410.7 4.0 copy-start.8
  410.7 4.0 copy-start.9
  415.5 2.0 copy-start.13
  415.6 2.0 copy-start.14
  415.6 2.6 copy-start.4
  416.6 2.0 copy-start.5
  419.1 2.8 copy-start.2
  419.1 2.8 copy-start.3
  419.6 3.1 copy-start.6
  419.6 3.8 copy-start.7

commit v6 on v5

--- a/solution.py
+++ b/solution.py
@@ -983,8 +983,14 @@
     return ref[...].reshape(-1, ref.shape[-1])
 
 
-def forward_kernel(first, *refs):
-    refs = list(refs)
+def forward_kernel(*refs):
+    run = Run(*refs[-3:])
+    run.prepare = lambda: run.greet(False)
+    forward_body(True, run, list(refs[:-3]))
+    run.close()
+
+
+def forward_body(first, run, refs):
 
     def take(n):
         out = refs[:n]
@@ -1000,12 +1006,12 @@
     if first:
         qkv_in, o_in = chunks.at[0, :, pl.ds(0, PACKED)], rows_o.at[0]
         qkv_next, o_next = chunks.at[1, :, pl.ds(0, PACKED)], rows_o.at[1]
-    xn_ref, xb_o, qp_o, trunk_o, mine_o, kp_o, p_o, ctx_o, z1_o, hb_o, gp_o, gl_o, z2_o, win_o, wout_o = take(15)
-    if first:
+    xn_ref = take(1)[0]
+    if first:
+        xb_o, qp_o, trunk_o, mine_o, kp_o, p_o, ctx_o, z1_o, hb_o, gp_o, gl_o, z2_o, win_o, wout_o = take(14)
         wqkv_o, wo_o, wqkv_n, wo_n = take(4)
     xb, qp, trunk, mine, kp, p, ctx, z1, hb, gp, gl, z2, win, wout, wqkv, wo, heads, own, rs1_s, rs1_r, rs2_s, rs2_r = take(22)
     tx, *chain_refs = take(7)
-    run = Run(*refs)
     place = run.place
     z, f, c = place.z, place.f, place.c
     launch = run.launch
@@ -1014,7 +1020,7 @@
     wo[192:256, :] = jnp.zeros((64, WIDE), BF)
     if not first:
         loads = [run.local(qkv_in, wqkv), run.local(o_in, wo.at[pl.ds(0, 192)])]
-    run.greet(False)
+    run.prepare()
     came = [None] + [launch(xb.at[f], xb.at[f], place.plane(k)) for k in (1, 2, 3)]
     trunk_rows = TrunkRows(run, xb, tx)
     trunk_rows.start()
@@ -1060,17 +1066,22 @@
             trunk[c, g] = keys.astype(BF)
 
     trunk_near = launch(trunk.at[c], trunk.at[c], place.sibling())
-    run.save(xb, xb_o)
-    run.save(qp, qp_o)
+    if first:
+        run.save(xb, xb_o)
+    if first:
+        run.save(qp, qp_o)
     chain.finish()
     trunk_near.wait_recv()
     late_tasks = m_tasks
     for t in late_tasks:
         t.start(z > 0)
     pick_parents(kp, chain.slots, choose)
-    run.save(kp, kp_o)
-    run.save(trunk, trunk_o)
-    run.save(mine, mine_o)
+    if first:
+        run.save(kp, kp_o)
+    if first:
+        run.save(trunk, trunk_o)
+    if first:
+        run.save(mine, mine_o)
     if first:
         a_tasks[1].relay()
 
@@ -1090,7 +1101,8 @@
         return carry
 
     lax.fori_loop(0, 12, attend, 0)
-    run.save(p, p_o)
+    if first:
+        run.save(p, p_o)
     if first:
         a_tasks[1].finish()
     back = [None]
@@ -1104,7 +1116,8 @@
             back.append(launch(rs1_s.at[k - 1], rs1_r.at[k - 1], place.plane(-k)))
         else:
             own[...] = part
-    run.save(ctx, ctx_o)
+    if first:
+        run.save(ctx, ctx_o)
     for k in (1, 2, 3):
         back[k].wait_recv()
     for t in late_tasks:
@@ -1112,7 +1125,8 @@
     total = own[...] + rs1_r[0].astype(F32) + rs1_r[1].astype(F32) + rs1_r[2].astype(F32)
     zz = x_ref[...].astype(F32) + total + vec[1:2, :]
     z1[...] = zz
-    run.save(z1, z1_o)
+    if first:
+        run.save(z1, z1_o)
     hidden = norm_rows(zz, vec[2:3, :], vec[3:4, :])
     hb[f] = hidden.astype(BF)
     came = [None] + [launch(hb.at[f], hb.at[f], place.plane(k)) for k in (1, 2, 3)]
@@ -1140,11 +1154,16 @@
             back.append(launch(rs2_s.at[k - 1], rs2_r.at[k - 1], place.plane(-k)))
         else:
             own[...] = part
-    run.save(hb, hb_o)
-    run.save(gp, gp_o)
-    run.save(gl, gl_o)
-    run.save(win, win_o)
-    run.save(wout, wout_o)
+    if first:
+        run.save(hb, hb_o)
+    if first:
+        run.save(gp, gp_o)
+    if first:
+        run.save(gl, gl_o)
+    if first:
+        run.save(win, win_o)
+    if first:
+        run.save(wout, wout_o)
     if first:
         run.save(wqkv, wqkv_o)
         run.save(wo.at[pl.ds(0, 192)], wo_o)
@@ -1153,35 +1172,55 @@
     total = own[...] + rs2_r[0].astype(F32) + rs2_r[1].astype(F32) + rs2_r[2].astype(F32)
     zz = norm_rows(z1[...], vec[2:3, :], vec[3:4, :]) + total + vec[5:6, :]
     z2[...] = zz
-    run.save(z2, z2_o)
+    if first:
+        run.save(z2, z2_o)
     xn_ref[...] = norm_rows(zz, vec[6:7, :], vec[7:8, :]).astype(xn_ref.dtype)
     if first:
         for t in n_tasks:
             t.relay()
         for t in n_tasks:
             t.finish()
+    return z2, (wout, gp, win, gl, hb, z1, wo, ctx, trunk, mine, kp, qp, p, xb, wqkv)
+
+
+def turn_kernel(*refs):
+    run = Run(*refs[-3:])
+    run.prepare = lambda: run.greet(True)
+    refs = list(refs[:-3])
+    ahead, dy_ref, xn_ref, outs, kept, rest = refs[:10], refs[10], refs[11], refs[12:19], refs[19:48], refs[48:]
+    held = forward_body(False, run, ahead + [xn_ref] + kept)
+    backward_body(False, run, [dy_ref] + ahead[4:7] + outs + rest, held)
     run.close()
 
 
-def backward_kernel(extra, *refs):
-    refs = list(refs)
+def backward_kernel(*refs):
+    run = Run(*refs[-3:])
+    backward_body(True, run, list(refs[:-3]), None)
+    run.close()
+
+
+def backward_body(extra, run, refs, held):
 
     def take(n):
         out = refs[:n]
         del refs[:n]
         return out
 
-    dy_ref, vecs, place_in, choose, z2 = take(5)
+    dy_ref, vecs, place_in, choose = take(4)
     vec = vecs.at[0 if extra else 1]
-    late_in = take(15)
     if extra:
+        z2 = take(1)[0]
+        late_in = take(15)
         pq_in, pk_in, dvec_in = take(3)
     dx_ref, din_o, dout_o, do_o = take(4)
     if extra:
         dq_n, dk_n, dq_o, dk_o, sm_o = take(5)
     else:
         pq, pk, dvec_o = take(3)
-    late = take(15)
+    if extra:
+        late = take(15)
+    else:
+        z2, late = held
     wout, gp, win, gl, hb, z1, wo, ctx, trunk, mine, kp, qp, p, xb, wqkv = late
     (
         df, du, da, dctx, dqf, dqkv, dz, dz1, dkt, dself, dpar, tgt, own, rs1_s, rs1_r, rs2_s, rs2_r,
@@ -1191,14 +1230,14 @@
     if extra:
         pq, pk, dvec_o = take(3)
         nq, fq, tq, nk, fk, tk, nq2, fq2, tq2, nk2, fk2, tk2, sm, sm_a, sm_b, sm_v = take(16)
-    run = Run(*refs)
     place = run.place
     z, f, c = place.z, place.f, place.c
     launch = run.launch
     loads = []
-    for n, (src, dst) in enumerate(zip(late_in, late)):
-        loads.append(run.local(src, dst.at[pl.ds(0, 192)] if n == 6 else dst))
-    wo[192:256, :] = jnp.zeros((64, WIDE), BF)
+    if extra:
+        for n, (src, dst) in enumerate(zip(late_in, late)):
+            loads.append(run.local(src, dst.at[pl.ds(0, 192)] if n == 6 else dst))
+        wo[192:256, :] = jnp.zeros((64, WIDE), BF)
 
     grad, dgain, dshift = norm_rows_back(z2[...], vec[6:7, :], dy_ref[...].astype(F32))
     dvec_o[6:7, :] = dgain
@@ -1207,7 +1246,8 @@
     low = grad.astype(BF)
     df[f] = low
     dvec_o[5:6, :] = jnp.sum(low.astype(F32), axis=0, keepdims=True)
-    run.greet(True)
+    if extra:
+        run.greet(True)
     came = [None] + [launch(df.at[f], df.at[f], place.plane(k)) for k in (1, 2, 3)]
     a_tasks = []
     if extra:
@@ -1216,8 +1256,8 @@
         t.start()
     back = [None]
     bias = jnp.zeros((1, WIDE), F32)
-    for n in range(3):
-        loads[n].wait()
+    for a in loads[:3]:
+        a.wait()
     for k in range(4):
         g = place.f_at(-k)
         if k:
@@ -1250,15 +1290,16 @@
         split_rows(pin, hb, flat(du), i)
         return carry
 
-    for n in range(3, 5):
-        loads[n].wait()
+    for a in loads[3:5]:
+        a.wait()
     lax.fori_loop(0, 2, ffn_grads, 0)
     for t in m_tasks:
         t.start()
     for k in (1, 2, 3):
         back[k].wait_recv()
     up = dz[...] + own[...] + rs1_r[0].astype(F32) + rs1_r[1].astype(F32) + rs1_r[2].astype(F32)
-    loads[5].wait()
+    for a in loads[5:6]:
+        a.wait()
     grad, dgain, dshift = norm_rows_back(z1[...], vec[2:3, :], up)
     dvec_o[2:3, :] = dgain
     dvec_o[3:4, :] = dshift
@@ -1400,14 +1441,13 @@
             a.wait_recv()
     for t in m_tasks + [o_task] + end_tasks:
         t.last()
-    run.close()
 
 
 ANY = pl.BlockSpec(memory_space=pl.ANY)
 VM = pl.BlockSpec(memory_space=pltpu.VMEM)
 SM = pl.BlockSpec(memory_space=pltpu.SMEM)
 LIMIT = 60 * 1024 * 1024
-SEMS = (160, 160, 32)
+SEMS = (256, 256, 32)
 
 
 def shape(*dims, dtype=BF):
@@ -1452,15 +1492,18 @@
 )
 
 
-def forward_layer(first, state, chunks, rows_o, rows_out, vecs, place_in, choose, pen, here):
-    outs = (LOCAL if first else shape(ROWS, WIDE),) + SAVED + (BIG, BIG) + ((QKV, OUTPUT, QKV, OUTPUT) if first else ())
+FORWARD_SCRATCH = (
+    list(SAVED)
+    + [BIG, BIG, QKV, shape(256, WIDE), shape(3, 4, ROWS, 128, dtype=F32), LOCAL]
+    + [PIECE] * 4 + [FULL, HALVES] + [QUARTERS] * 5
+)
+
+
+def forward_layer(state, chunks, rows_o, rows_out, vecs, place_in, choose, pen):
+    outs = (LOCAL,) + SAVED + (BIG, BIG, QKV, OUTPUT, QKV, OUTPUT)
     got = call(
-        lambda *refs: forward_kernel(first, *refs), 1 if first else 2, outs, (VM,) + (ANY,) * (len(outs) - 1),
-        [VM] + [ANY] * 3 + [VM] + [SM] * 3 + [ANY] * len(here),
-        list(SAVED)
-        + [BIG, BIG, QKV, shape(256, WIDE), shape(3, 4, ROWS, 128, dtype=F32), LOCAL]
-        + [PIECE] * 4 + [FULL, HALVES] + [QUARTERS] * 5,
-        (state, chunks, rows_o, rows_out, vecs, place_in, choose, pen) + tuple(here), 3 * 10**9,
+        forward_kernel, 1, outs, (VM,) + (ANY,) * (len(outs) - 1), [VM] + [ANY] * 3 + [VM] + [SM] * 3,
+        FORWARD_SCRATCH, (state, chunks, rows_o, rows_out, vecs, place_in, choose, pen), 3 * 10**9,
     )
     return got[0], got[1:13], got[13:]
 
@@ -1474,32 +1517,45 @@
 SHARES = (shape(4, 24, 256, dtype=F32), shape(4, 24, SLICE, dtype=F32))
 
 
-def backward_layer(upstream, weights, vec, place_in, choose, saved, before):
-    wqkv, wo, win, wout = weights
-    xb, qp, trunk, mine, kp, p, ctx, z1, hb, gp, gl, z2 = saved
+def backward_scratch():
     keys = shape(4, 256, SLICE, dtype=F32)
-    extra = len(before) > 0
-    sums, sums2 = shape(8, WIDE, dtype=F32), shape(16, WIDE, dtype=F32)
-    outs = (shape(ROWS, WIDE) if extra else LOCAL,)
-    outs += (shape(4, 24, WIDE, dtype=F32), shape(96, WIDE, dtype=F32), shape(24, WIDE, dtype=F32))
-    outs += SHARES + SHARES + (shape(4, 16, WIDE, dtype=F32),) if extra else PARTS + (sums,)
-    scratch = [BIG, SAVED[9], BIG, FULL, FULL, LOCAL, shape(256, WIDE), SAVED[6], HALVES, HALVES, SAVED[4], SAVED[1], SAVED[5], FULL, QKV] + [
+    part = shape(2, 4, 96, WIDE)
+    scratch = [
         FULL, FULL, FULL, shape(512, SLICE), shape(3, 512, 128, dtype=F32), shape(4, ROWS, PACKED), LOCAL, LOCAL,
         shape(1024, SLICE, dtype=F32), keys, keys, shape(2, 3, 4, ROWS, SLICE), LOCAL, PIECE, PIECE, PIECE, PIECE,
         shape(3, 4, ROWS, SLICE),
     ] + [QUARTERS] * 6
-    part = shape(2, 4, 96, WIDE)
     scratch += [part] + collect_scratch(WIDE, True) + [part] + collect_scratch(WIDE, False)
-    scratch += [shape(2, 96, WIDE)] + OUT_SCRATCH
-    if extra:
-        scratch += list(PARTS) + [sums]
-        scratch += (collect_scratch(256, True) + collect_scratch(SLICE, True)) * 1
-        scratch += collect_scratch(256, True) + collect_scratch(SLICE, True)
-        scratch += [sums2, sums2, shape(3, 16, WIDE, dtype=F32), sums2]
+    return scratch + [shape(2, 96, WIDE)] + OUT_SCRATCH
+
+
+SUMS, SUMS2 = shape(8, WIDE, dtype=F32), shape(16, WIDE, dtype=F32)
+GRADS = (shape(4, 24, WIDE, dtype=F32), shape(96, WIDE, dtype=F32), shape(24, WIDE, dtype=F32))
+
+
+def turn_layer(state, chunks, rows_o, rows_out, vecs, place_in, choose, pen, wqkv, wo, upstream):
+    outs = (shape(ROWS, WIDE), LOCAL) + GRADS + PARTS + (SUMS,)
     return call(
-        lambda *refs: backward_kernel(extra, *refs), 4 if extra else 3, outs, (VM,) * len(outs),
-        [VM] * 2 + [SM] * 2 + [VM] + [ANY] * 15 + [VM] * len(before), scratch,
-        (upstream, vec, place_in, choose, z2, wout, gp, win, gl, hb, z1, wo, ctx, trunk, mine, kp, qp, p, xb, wqkv)
+        turn_kernel, 2, outs, (VM,) * len(outs), [VM] + [ANY] * 3 + [VM] + [SM] * 3 + [ANY] * 2 + [VM],
+        FORWARD_SCRATCH + backward_scratch(),
+        (state, chunks, rows_o, rows_out, vecs, place_in, choose, pen, wqkv, wo, upstream), 9 * 10**9,
+    )
+
+
+def backward_layer(upstream, weights, vecs, place_in, choose, saved, before):
+    wqkv, wo, win, wout = weights
+    xb, qp, trunk, mine, kp, p, ctx, z1, hb, gp, gl, z2 = saved
+    outs = (shape(ROWS, WIDE),) + GRADS + SHARES + SHARES + (shape(4, 16, WIDE, dtype=F32),)
+    scratch = [
+        BIG, SAVED[9], BIG, FULL, FULL, LOCAL, shape(256, WIDE), SAVED[6], HALVES, HALVES, SAVED[4], SAVED[1], SAVED[5],
+        FULL, QKV,
+    ] + backward_scratch()
+    scratch += list(PARTS) + [SUMS]
+    scratch += (collect_scratch(256, True) + collect_scratch(SLICE, True)) * 2
+    scratch += [SUMS2, SUMS2, shape(3, 16, WIDE, dtype=F32), SUMS2]
+    return call(
+        backward_kernel, 4, outs, (VM,) * len(outs), [VM] * 2 + [SM] * 2 + [VM] + [ANY] * 15 + [VM] * 3, scratch,
+        (upstream, vecs, place_in, choose, z2, wout, gp, win, gl, hb, z1, wo, ctx, trunk, mine, kp, qp, p, xb, wqkv)
         + tuple(before),
         6 * 10**9,
     )
@@ -1548,11 +1604,8 @@
     ).astype(F32)
 
     shared = (colp, op, outer_weight, vecs, place_in, choose, pen)
-    state, kept0, (win0, wout0, wqkv0, wo0, wqkv1, wo1) = forward_layer(True, activations, *shared, ())
-    outcome, kept1, (win1, wout1) = forward_layer(False, state, *shared, (wqkv1, wo1))
-    upstream, din1, dout1, do1, pq, pk, dvec1 = backward_layer(
-        cotangent, (wqkv1, wo1, win1, wout1), vecs, place_in, choose, kept1, ()
-    )
+    state, kept0, (win0, wout0, wqkv0, wo0, wqkv1, wo1) = forward_layer(activations, *shared)
+    outcome, upstream, din1, dout1, do1, pq, pk, dvec1 = turn_layer(state, *shared, wqkv1, wo1, cotangent)
     upstream, din0, dout0, do0, dq1, dk1, dq0, dk0, rsm = backward_layer(
         upstream, (wqkv0, wo0, win0, wout0), vecs, place_in, choose, kept0, (pq, pk, dvec1)
     )

time: 431 us -> 425 us (0.986)
  Pallas kernels: 395 us -> 390 us
    pallas_call x5 -> x4, Pallas kernels: 395 us -> 390 us  [call(): pl.pallas_call(kernel, out_shape=tuple(outs), in_specs=in_specs, out_spec...]
where the time goes in v6:
time: 425 us; the launch traced here: 419 us
  Pallas kernels  390 us (92%)
  local copies, waits for them, and re-layouts  20.1 us (5%)
  other arithmetic  6.7 us (2%)
    pallas_call x4, Pallas kernels, call(): pl.pallas_call(kernel, out_shape=tuple(outs), in_specs=in_specs, out_spec...  390 us

profile of v6, /device:TPU:9, one launch (start us, length us, event | category | flops | bytes accessed | tf_op | source)
XLA Modules:
  0.0 418.8 jit_solution(16877472627949945679)
XLA Ops:
  0.7 1.1 stack_reshape.33
  1.8 1.1 stack_reshape.34
  2.9 0.3 pad_maximum_fusion.1
  3.2 0.5 copy.136
  3.7 0.2 reshape.170
  3.9 0.5 reshape.171
  4.4 0.2 copy.198
  4.6 0.3 reshape.172
  5.1 0.2 reshape.168
  5.2 0.1 pad.17
  5.4 0.2 reshape.186
  5.6 0.8 maximum_bitcast_fusion.1.col
  6.7 0.6 pad.18.small
  7.3 19.8 %shard_map.314 = (bf16[4,48,1408]{2,1,0:T(8,128)(2,1)}, bf16[4,48,768]{2,1,0:T(8,128)(2,1)}, bf16[4,2,4,16,384]{4,3,2,1,0:T(8,128)(2,1)}) custom-call(bf16[4,48,1408]{2,1,0:T(8,128)(2,1)} %maximum_bitcast_fusion.1.col, bf16[48,768]{1,0:T(8,128)(2,1)} %bitcast.127, bf16[16,384]{1,0:T(8,128)(2,1)} %pad.18.small), custom_call_target="tpu_custom_call" | custom-call | flops 1000 | bytes 20000000 | tf_op jit(solution)/shard_map/pallas_call | solution.py:1458
  27.1 1.0 convert_bitcast_fusion
  28.1 0.4 fusion
  28.6 0.2 select_reduce_fusion
  29.1 0.3 compare_reduce_fusion
  29.4 0.5 concatenate.16.refs_7_
  29.9 0.6 convert_element_type.44.refs_6_.refs_3_
  30.5 0.7 constant_dynamic-slice_fusion.9.refs_5_.refs_2_
  31.4 0.3 fusion.13
  32.3 0.1 stack_reshape.35
  32.5 0.1 stack_reshape.36
  32.6 0.1 stack_reshape.37
  32.9 0.1 stack_reshape.40
  33.1 0.7 stack.59.refs_4_.refs_1_
  33.8 0.8 copy.138
  34.7 0.7 copy.139
  35.4 96.4 %shard_map.315 = (f32[128,768]{1,0:T(8,128)}, bf16[4,128,768]{2,1,0:T(8,128)(2,1)}, bf16[512,384]{1,0:T(8,128)(2,1)}, bf16[2,4,128,384]{3,2,1,0:T(8,128)(2,1)}, ...) custom-call(bf16[128,768]{1,0:T(8,128)(2,1)} %refs_0_.1, ...), custom_call_target="tpu_custom_call" | custom-call | flops 3000000000 | bytes 20000000 | tf_op jit(solution)/shard_map/pallas_call | solution.py:1458
  131.8 164.2 %shard_map.316 = (bf16[128,768]{1,0:T(8,128)(2,1)}, f32[128,768]{1,0:T(8,128)}, f32[4,24,768]{2,1,0:T(8,128)}, f32[96,768]{1,0:T(8,128)}, f32[24,768]{1,0:T(8,12...) custom-call(f32[128,768]{1,0:T(8,128)} %get-tuple-element.59.refs_0_, ...), custom_call_target="tpu_custom_call" | custom-call | flops 8999999488 | bytes 20000000 | tf_op jit(solution)/shard_map/pallas_call | solution.py:1458
  296.1 109.9 %shard_map.317 = (bf16[128,768]{1,0:T(8,128)(2,1)}, f32[4,24,768]{2,1,0:T(8,128)}, f32[96,768]{1,0:T(8,128)}, f32[24,768]{1,0:T(8,128)}, f32[4,24,256]{2,1,0:T(8...) custom-call(f32[128,768]{1,0:T(8,128)} %get-tuple-element.63.refs_0_, ...), custom_call_target="tpu_custom_call" | custom-call | flops 6000000000 | bytes 20000000 | tf_op jit(solution)/shard_map/pallas_call | solution.py:1458
  406.0 1.9 pad_maximum_fusion
  408.0 0.6 constant_dynamic-slice_fusion.7
  408.6 0.3 stack.70
  408.9 0.3 stack.71
  409.2 0.2 maximum_bitcast_fusion
  409.4 0.5 copy.162
  410.0 1.6 reshape.185
  411.5 0.7 pad_maximum_fusion.2
  412.2 0.4 reshape.184
  412.6 0.5 fusion.12
  413.2 0.9 reshape_squeeze.11
  414.2 0.9 reshape_squeeze.12
  415.7 0.7 fusion.4
  416.4 0.8 reshape.182
  417.3 0.7 copy.211
  417.9 0.7 copy.212
  (117 shorter events, 2.5 us)
Async XLA Ops:
  1.8 2.2 copy-start.3
  3.9 1.0 copy-start.13
  4.9 1.5 copy-start.25
  5.0 1.5 copy-start.16
  5.0 1.5 copy-start.17
  5.0 1.5 copy-start.18
  5.0 1.5 copy-start.19
  5.0 1.5 copy-start.20
  5.0 1.5 copy-start.21
  5.0 1.5 copy-start.22
  5.0 1.5 copy-start.23
  5.1 1.5 copy-start.24
  5.6 23.1 %copy-start.26 = (s32[13]{0:T(128)S(1)}, s32[13]{0:T(128)}, u32[]{:S(2)}) copy-start(s32[13]{0:T(128)} %param.36) | copy-start | bytes 160
  27.1 6.8 %copy-start = (bf16[4,48,1408]{2,1,0:T(8,128)(2,1)S(1)}, bf16[4,48,1408]{2,1,0:T(8,128)(2,1)}, u32[]{:S(2)}) copy-start(bf16[4,48,1408]{2,1,0:T(8,128)(2,1)} %get-tuple-element.56) | copy-start | bytes 1622020
  31.7 3.0 copy-start.2
  296.0 110.0 %copy-start.6 = (f32[96,768]{1,0:T(8,128)S(1)}, f32[96,768]{1,0:T(8,128)}, u32[]{:S(2)}) copy-start(f32[96,768]{1,0:T(8,128)} %get-tuple-element.94) | copy-start | bytes 884740
  406.0 1.9 copy-start.1
  406.0 2.6 copy-start.5
  406.0 2.9 copy-start.4
  409.9 1.6 copy-start.14
  409.9 1.6 copy-start.15
  409.9 2.3 copy-start.9
  410.0 2.2 copy-start.10
  414.1 2.2 copy-start.11
  414.1 2.2 copy-start.12
  415.1 2.2 copy-start.7
  415.2 2.7 copy-start.8

commit v7 on v6

--- a/solution.py
+++ b/solution.py
@@ -874,7 +874,12 @@
     def start(self):
         run, place = self.run, self.run.place
         self.pairs = [[(run.sends.take(), run.recvs.take()) for _ in range(4)] for _ in range(3)]
-        self.a = run.launch(self.mine.at[1 - place.c], self.near, place.sibling())
+        self.arrive = []
+        self.hand_over(0)
+
+    def hand_over(self, kind):
+        run, place = self.run, self.run.place
+        self.arrive.append(run.launch(self.mine.at[1 - place.c, kind], self.near.at[kind], place.sibling()))
 
     def wait(self, which, j):
         dst = (self.trunk_in, self.up, self.down)[which].at[j]
@@ -883,9 +888,9 @@
     def middle(self):
         run, place = self.run, self.run.place
         z, c = place.z, place.c
-        self.a.wait_recv()
         near = self.near
         for kind in range(3):
+            self.arrive[kind].wait_recv()
             for j in range(4):
                 near[kind, j] = (self.mine[c, kind, j].astype(F32) + near[kind, j].astype(F32)).astype(BF)
                 if kind == 0:
@@ -1100,7 +1105,7 @@
         heads[h, b] = product(pb, keys)
         return carry
 
-    lax.fori_loop(0, 12, attend, 0)
+    lax.fori_loop(0, 12, attend, 0, unroll=2)
     if first:
         run.save(p, p_o)
     if first:
@@ -1295,6 +1300,8 @@
     lax.fori_loop(0, 2, ffn_grads, 0)
     for t in m_tasks:
         t.start()
+    for t in m_tasks:
+        t.middle()
     for k in (1, 2, 3):
         back[k].wait_recv()
     up = dz[...] + own[...] + rs1_r[0].astype(F32) + rs1_r[1].astype(F32) + rs1_r[2].astype(F32)
@@ -1310,8 +1317,6 @@
     came = [None] + [launch(da.at[f], da.at[f], place.plane(k)) for k in (1, 2, 3)]
     for t in a_tasks:
         t.end()
-    for t in m_tasks:
-        t.middle()
     dkt[...] = jnp.zeros_like(dkt)
     lane = lax.broadcasted_iota(jnp.int32, (ROWS, 128), 1)
     for a in loads[6:]:
@@ -1356,6 +1361,9 @@
             at = cc * 512 + j * ROWS
             tgt[cc, 0, j] = dkt[at : at + ROWS, :].astype(BF)
 
+    chain = GradChain(run, tgt, *chain_refs)
+    chain.start()
+
     def scatter(j, carry):
         for cc in range(2):
             half = slice(cc * ROWS, (cc + 1) * ROWS)
@@ -1367,8 +1375,8 @@
         return carry
 
     lax.fori_loop(0, 4, scatter, 0)
-    chain = GradChain(run, tgt, *chain_refs)
-    chain.start()
+    chain.hand_over(1)
+    chain.hand_over(2)
     for g in range(4):
         rows = slice(g * ROWS, (g + 1) * ROWS)
         ahead = jnp.where(lane < 64, dqf[0, rows, :], pltpu.roll(dqf[1, rows, :], 64, 1))

time: 425 us -> 419 us (0.986)
  Pallas kernels: 390 us -> 384 us
    pallas_call x4, Pallas kernels: 390 us -> 384 us  [call(): pl.pallas_call(kernel, out_shape=tuple(outs), in_specs=in_specs, out_spec...]
where the time goes in v7:
time: 419 us; the launch traced here: 412 us
  Pallas kernels  384 us (92%)
  local copies, waits for them, and re-layouts  20.1 us (5%)
  other arithmetic  6.7 us (2%)
    pallas_call x4, Pallas kernels, call(): pl.pallas_call(kernel, out_shape=tuple(outs), in_specs=in_specs, out_spec...  384 us

profile of v7, /device:TPU:9, one launch (start us, length us, event | category | flops | bytes accessed | tf_op | source)
XLA Modules:
  0.0 412.4 jit_solution(10033557666022558746)
XLA Ops:
  0.7 1.1 stack_reshape.33
  1.8 1.1 stack_reshape.34
  2.9 0.3 pad_maximum_fusion.1
  3.2 0.5 copy.136
  3.7 0.2 reshape.170
  3.9 0.5 reshape.171
  4.4 0.2 copy.198
  4.6 0.3 reshape.172
  5.1 0.2 reshape.168
  5.2 0.1 pad.17
  5.4 0.2 reshape.186
  5.6 0.8 maximum_bitcast_fusion.1.col
  6.7 0.6 pad.18.small
  7.3 19.8 %shard_map.314 = (bf16[4,48,1408]{2,1,0:T(8,128)(2,1)}, bf16[4,48,768]{2,1,0:T(8,128)(2,1)}, bf16[4,2,4,16,384]{4,3,2,1,0:T(8,128)(2,1)}) custom-call(bf16[4,48,1408]{2,1,0:T(8,128)(2,1)} %maximum_bitcast_fusion.1.col, bf16[48,768]{1,0:T(8,128)(2,1)} %bitcast.127, bf16[16,384]{1,0:T(8,128)(2,1)} %pad.18.small), custom_call_target="tpu_custom_call" | custom-call | flops 1000 | bytes 20000000 | tf_op jit(solution)/shard_map/pallas_call | solution.py:1466
  27.1 1.0 convert_bitcast_fusion
  28.1 0.4 fusion
  28.6 0.2 select_reduce_fusion
  29.1 0.3 compare_reduce_fusion
  29.4 0.5 concatenate.16.refs_7_
  29.9 0.6 convert_element_type.44.refs_6_.refs_3_
  30.5 0.7 constant_dynamic-slice_fusion.9.refs_5_.refs_2_
  31.4 0.3 fusion.13
  32.3 0.1 stack_reshape.35
  32.5 0.1 stack_reshape.36
  32.6 0.1 stack_reshape.37
  32.9 0.1 stack_reshape.40
  33.1 0.7 stack.59.refs_4_.refs_1_
  33.8 0.8 copy.138
  34.7 0.7 copy.139
  35.4 95.5 %shard_map.315 = (f32[128,768]{1,0:T(8,128)}, bf16[4,128,768]{2,1,0:T(8,128)(2,1)}, bf16[512,384]{1,0:T(8,128)(2,1)}, bf16[2,4,128,384]{3,2,1,0:T(8,128)(2,1)}, ...) custom-call(bf16[128,768]{1,0:T(8,128)(2,1)} %refs_0_.1, ...), custom_call_target="tpu_custom_call" | custom-call | flops 3000000000 | bytes 20000000 | tf_op jit(solution)/shard_map/pallas_call | solution.py:1466
  130.9 161.8 %shard_map.316 = (bf16[128,768]{1,0:T(8,128)(2,1)}, f32[128,768]{1,0:T(8,128)}, f32[4,24,768]{2,1,0:T(8,128)}, f32[96,768]{1,0:T(8,128)}, f32[24,768]{1,0:T(8,12...) custom-call(f32[128,768]{1,0:T(8,128)} %get-tuple-element.59.refs_0_, ...), custom_call_target="tpu_custom_call" | custom-call | flops 8999999488 | bytes 20000000 | tf_op jit(solution)/shard_map/pallas_call | solution.py:1466
  292.8 106.8 %shard_map.317 = (bf16[128,768]{1,0:T(8,128)(2,1)}, f32[4,24,768]{2,1,0:T(8,128)}, f32[96,768]{1,0:T(8,128)}, f32[24,768]{1,0:T(8,128)}, f32[4,24,256]{2,1,0:T(8...) custom-call(f32[128,768]{1,0:T(8,128)} %get-tuple-element.63.refs_0_, ...), custom_call_target="tpu_custom_call" | custom-call | flops 6000000000 | bytes 20000000 | tf_op jit(solution)/shard_map/pallas_call | solution.py:1466
  399.6 1.9 pad_maximum_fusion
  401.5 0.6 constant_dynamic-slice_fusion.7
  402.1 0.3 stack.70
  402.4 0.3 stack.71
  402.7 0.2 maximum_bitcast_fusion
  402.9 0.5 copy.162
  403.5 1.6 reshape.185
  405.1 0.7 pad_maximum_fusion.2
  405.8 0.4 reshape.184
  406.1 0.5 fusion.12
  406.7 0.9 reshape_squeeze.11
  407.7 0.9 reshape_squeeze.12
  409.2 0.7 fusion.4
  410.0 0.8 reshape.182
  410.8 0.7 copy.211
  411.5 0.7 copy.212
  (117 shorter events, 2.5 us)
Async XLA Ops:
  1.8 2.2 copy-start.3
  3.9 1.0 copy-start.13
  4.9 1.5 copy-start.25
  5.0 1.5 copy-start.16
  5.0 1.5 copy-start.17
  5.0 1.5 copy-start.18
  5.0 1.5 copy-start.19
  5.0 1.5 copy-start.20
  5.0 1.5 copy-start.21
  5.0 1.5 copy-start.22
  5.0 1.5 copy-start.23
  5.1 1.5 copy-start.24
  5.6 23.1 %copy-start.26 = (s32[13]{0:T(128)S(1)}, s32[13]{0:T(128)}, u32[]{:S(2)}) copy-start(s32[13]{0:T(128)} %param.36) | copy-start | bytes 160
  27.1 6.8 %copy-start = (bf16[4,48,1408]{2,1,0:T(8,128)(2,1)S(1)}, bf16[4,48,1408]{2,1,0:T(8,128)(2,1)}, u32[]{:S(2)}) copy-start(bf16[4,48,1408]{2,1,0:T(8,128)(2,1)} %get-tuple-element.56) | copy-start | bytes 1622020
  31.7 3.0 copy-start.2
  292.8 106.8 %copy-start.6 = (f32[96,768]{1,0:T(8,128)S(1)}, f32[96,768]{1,0:T(8,128)}, u32[]{:S(2)}) copy-start(f32[96,768]{1,0:T(8,128)} %get-tuple-element.94) | copy-start | bytes 884740
  399.5 1.9 copy-start.1
  399.5 2.6 copy-start.5
  399.5 2.9 copy-start.4
  403.5 1.6 copy-start.14
  403.5 1.6 copy-start.15
  403.5 2.3 copy-start.9
  403.5 2.2 copy-start.10
  407.6 2.2 copy-start.11
  407.6 2.2 copy-start.12
  408.6 2.2 copy-start.7
  408.8 2.7 copy-start.8

commit v8 on v7

--- a/solution.py
+++ b/solution.py
@@ -1290,18 +1290,22 @@
                 at = (2 * zz + cc) * 96
                 dst[cc, 2 * i + zz] = value[at : at + 96, :]
 
-    def ffn_grads(i, carry):
+    def outer_grads(i, carry):
         split_rows(pout, gl, flat(df), i)
+        return carry
+
+    def inner_grads(i, carry):
         split_rows(pin, hb, flat(du), i)
         return carry
 
     for a in loads[3:5]:
         a.wait()
-    lax.fori_loop(0, 2, ffn_grads, 0)
-    for t in m_tasks:
-        t.start()
-    for t in m_tasks:
-        t.middle()
+    lax.fori_loop(0, 2, outer_grads, 0)
+    m_tasks[1].start()
+    lax.fori_loop(0, 2, inner_grads, 0)
+    m_tasks[0].start()
+    m_tasks[1].middle()
+    m_tasks[0].middle()
     for k in (1, 2, 3):
         back[k].wait_recv()
     up = dz[...] + own[...] + rs1_r[0].astype(F32) + rs1_r[1].astype(F32) + rs1_r[2].astype(F32)

time: 419 us -> 419 us (level)
  no operation moved by 1% of the time
where the time goes in v8:
time: 419 us; the launch traced here: 413 us
  Pallas kernels  384 us (92%)
  local copies, waits for them, and re-layouts  20.1 us (5%)
  other arithmetic  6.7 us (2%)
    pallas_call x4, Pallas kernels, call(): pl.pallas_call(kernel, out_shape=tuple(outs), in_specs=in_specs, out_spec...  384 us

profile of v8, /device:TPU:9, one launch (start us, length us, event | category | flops | bytes accessed | tf_op | source)
XLA Modules:
  0.0 412.7 jit_solution(4122204966562585401)
XLA Ops:
  0.7 1.1 stack_reshape.33
  1.8 1.1 stack_reshape.34
  2.9 0.3 pad_maximum_fusion.1
  3.2 0.5 copy.136
  3.7 0.2 reshape.170
  3.9 0.5 reshape.171
  4.4 0.2 copy.198
  4.6 0.3 reshape.172
  5.1 0.2 reshape.168
  5.2 0.1 pad.17
  5.4 0.2 reshape.186
  5.6 0.8 maximum_bitcast_fusion.1.col
  6.7 0.6 pad.18.small
  7.3 19.8 %shard_map.314 = (bf16[4,48,1408]{2,1,0:T(8,128)(2,1)}, bf16[4,48,768]{2,1,0:T(8,128)(2,1)}, bf16[4,2,4,16,384]{4,3,2,1,0:T(8,128)(2,1)}) custom-call(bf16[4,48,1408]{2,1,0:T(8,128)(2,1)} %maximum_bitcast_fusion.1.col, bf16[48,768]{1,0:T(8,128)(2,1)} %bitcast.127, bf16[16,384]{1,0:T(8,128)(2,1)} %pad.18.small), custom_call_target="tpu_custom_call" | custom-call | flops 1000 | bytes 20000000 | tf_op jit(solution)/shard_map/pallas_call | solution.py:1470
  27.1 1.0 convert_bitcast_fusion
  28.1 0.4 fusion
  28.6 0.2 select_reduce_fusion
  29.1 0.3 compare_reduce_fusion
  29.4 0.5 concatenate.16.refs_7_
  29.9 0.6 convert_element_type.44.refs_6_.refs_3_
  30.5 0.7 constant_dynamic-slice_fusion.9.refs_5_.refs_2_
  31.4 0.3 fusion.13
  32.3 0.1 stack_reshape.35
  32.5 0.1 stack_reshape.36
  32.6 0.1 stack_reshape.37
  32.7 0.1 stack_reshape.39
  33.1 0.7 stack.59.refs_4_.refs_1_
  33.8 0.8 copy.138
  34.7 0.7 copy.139
  35.4 95.5 %shard_map.315 = (f32[128,768]{1,0:T(8,128)}, bf16[4,128,768]{2,1,0:T(8,128)(2,1)}, bf16[512,384]{1,0:T(8,128)(2,1)}, bf16[2,4,128,384]{3,2,1,0:T(8,128)(2,1)}, ...) custom-call(bf16[128,768]{1,0:T(8,128)(2,1)} %refs_0_.1, ...), custom_call_target="tpu_custom_call" | custom-call | flops 3000000000 | bytes 20000000 | tf_op jit(solution)/shard_map/pallas_call | solution.py:1470
  130.9 161.6 %shard_map.316 = (bf16[128,768]{1,0:T(8,128)(2,1)}, f32[128,768]{1,0:T(8,128)}, f32[4,24,768]{2,1,0:T(8,128)}, f32[96,768]{1,0:T(8,128)}, f32[24,768]{1,0:T(8,12...) custom-call(f32[128,768]{1,0:T(8,128)} %get-tuple-element.59.refs_0_, ...), custom_call_target="tpu_custom_call" | custom-call | flops 8999999488 | bytes 20000000 | tf_op jit(solution)/shard_map/pallas_call | solution.py:1470
  292.6 107.3 %shard_map.317 = (bf16[128,768]{1,0:T(8,128)(2,1)}, f32[4,24,768]{2,1,0:T(8,128)}, f32[96,768]{1,0:T(8,128)}, f32[24,768]{1,0:T(8,128)}, f32[4,24,256]{2,1,0:T(8...) custom-call(f32[128,768]{1,0:T(8,128)} %get-tuple-element.63.refs_0_, ...), custom_call_target="tpu_custom_call" | custom-call | flops 6000000000 | bytes 20000000 | tf_op jit(solution)/shard_map/pallas_call | solution.py:1470
  399.9 1.9 pad_maximum_fusion
  401.8 0.6 constant_dynamic-slice_fusion.7
  402.5 0.3 stack.70
  402.8 0.3 stack.71
  403.1 0.2 maximum_bitcast_fusion
  403.3 0.5 copy.162
  403.8 1.6 reshape.185
  405.4 0.7 pad_maximum_fusion.2
  406.1 0.4 reshape.184
  406.5 0.5 fusion.12
  407.0 0.9 reshape_squeeze.11
  408.0 0.9 reshape_squeeze.12
  409.5 0.7 fusion.4
  410.3 0.8 reshape.182
  411.1 0.7 copy.211
  411.8 0.7 copy.212
  (117 shorter events, 2.5 us)
Async XLA Ops:
  1.8 2.2 copy-start.3
  3.9 1.0 copy-start.13
  4.9 1.5 copy-start.25
  5.0 1.5 copy-start.16
  5.0 1.5 copy-start.17
  5.0 1.5 copy-start.18
  5.0 1.5 copy-start.19
  5.0 1.5 copy-start.20
  5.0 1.5 copy-start.21
  5.0 1.5 copy-start.22
  5.0 1.5 copy-start.23
  5.1 1.5 copy-start.24
  5.6 23.1 %copy-start.26 = (s32[13]{0:T(128)S(1)}, s32[13]{0:T(128)}, u32[]{:S(2)}) copy-start(s32[13]{0:T(128)} %param.36) | copy-start | bytes 160
  27.1 6.8 %copy-start = (bf16[4,48,1408]{2,1,0:T(8,128)(2,1)S(1)}, bf16[4,48,1408]{2,1,0:T(8,128)(2,1)}, u32[]{:S(2)}) copy-start(bf16[4,48,1408]{2,1,0:T(8,128)(2,1)} %get-tuple-element.56) | copy-start | bytes 1622020
  31.7 3.0 copy-start.2
  292.6 107.3 %copy-start.6 = (f32[96,768]{1,0:T(8,128)S(1)}, f32[96,768]{1,0:T(8,128)}, u32[]{:S(2)}) copy-start(f32[96,768]{1,0:T(8,128)} %get-tuple-element.94) | copy-start | bytes 884740
  399.9 1.9 copy-start.1
  399.9 2.6 copy-start.5
  399.9 2.9 copy-start.4
  403.8 1.6 copy-start.14
  403.8 1.6 copy-start.15
  403.8 2.3 copy-start.9
  403.8 2.2 copy-start.10
  407.9 2.2 copy-start.11
  407.9 2.2 copy-start.12
  409.0 2.2 copy-start.7
  409.1 2.7 copy-start.8
